TPU v7x, 32 devices: a whole 2x2x4 slice. The times are simulated.
32 devices in a mesh: dp: 4 (over x, core), fsdp: 8 (over z, y).
Axes of the slice: x: 2, y: 2, z: 4, core: 2. Of those that a mesh axis runs over, the one named last changes fastest.
Arguments:
- latent: bfloat16 [8192, 512], P(('dp', 'fsdp')), may hold values from -6 to 6
- cotangent: bfloat16 [8192, 16384], P(('dp', 'fsdp')), may hold values from -2 to 2
- quant: bfloat16 [512, 16384], P(None, 'fsdp'), may hold values from -6 to 6
- scales: float32 [4, 128], P(None, 'fsdp'), may hold values from 0.015 to 0.09
- adapter_down: bfloat16 [512, 64], replicated, may hold values from -0.25 to 0.25
- adapter_up: bfloat16 [64, 16384], P(None, 'fsdp'), may hold values from -0.75 to 0.75
Outputs:
- latent_gradient: bfloat16 [8192, 512], P(('dp', 'fsdp'))
- grad_a: float32 [512, 64], replicated
- grad_b: float32 [64, 16384], P(None, 'fsdp')
All inputs are finite; a program needn't handle non-finite values.
Results may differ from a plain program's by a relative error of at most 0.0049.
Values may be sent and summed in bfloat16 or wider, within the bound.
No kernel may reach another device: no remote copies, remote signals or barrier semaphores. Data moves between devices by JAX's collectives and lax.ppermute only.
A program may use at most 128 MiB of HBM per device.

v0:
```python
import jax
import jax.numpy as jnp
from jax import lax
from jax.sharding import PartitionSpec as P

BLOCK = 128


def expand(scales):
    return jnp.repeat(jnp.repeat(scales, BLOCK, axis=0), BLOCK, axis=1)


def contract_cols(left, right):
    return lax.dot_general(
        left, right, (((1,), (1,)), ((), ())), preferred_element_type=jnp.float32
    )


def shards(latent, cotangent, quant, scales, adapter_down, adapter_up):
    weight = (quant.astype(jnp.float32) * expand(scales)).astype(jnp.bfloat16)
    lowrank_term = jnp.dot(latent, adapter_down, preferred_element_type=jnp.float32).astype(
        jnp.bfloat16
    )
    full_weight, full_up = (
        lax.all_gather(weight, "fsdp", axis=1, tiled=True),
        lax.all_gather(adapter_up, "fsdp", axis=1, tiled=True),
    )
    frozen_term = contract_cols(cotangent, full_weight)
    through_sum = contract_cols(cotangent, full_up)
    adapter_pass = through_sum.astype(jnp.bfloat16)
    latent_gradient = (
        frozen_term + jnp.dot(adapter_pass, adapter_down.T, preferred_element_type=jnp.float32)
    ).astype(jnp.bfloat16)
    term_a = jnp.dot(latent.T, adapter_pass, preferred_element_type=jnp.float32)
    term_b = jnp.dot(lowrank_term.T, cotangent, preferred_element_type=jnp.float32)
    tokens_all = cotangent.shape[0] * lax.axis_size("dp") * lax.axis_size("fsdp")
    factor = 1.0 / jnp.sqrt(jnp.float32(tokens_all))
    total_a, total_b = lax.psum((term_a, term_b), ("dp", "fsdp"))
    latent_extent = adapter_up.shape[1]
    own_b = lax.dynamic_slice_in_dim(
        total_b, lax.axis_index("fsdp") * latent_extent, latent_extent, 1
    )
    grad_a = total_a * factor
    grad_b = own_b * factor
    return (latent_gradient, grad_a, grad_b)


def solution(mesh):
    placed = (
        P(("dp", "fsdp"), None),
        P(("dp", "fsdp"), None),
        P(None, "fsdp"),
        P(None, "fsdp"),
        P(),
        P(None, "fsdp"),
    )
    return jax.shard_map(
        shards,
        mesh=mesh,
        in_specs=placed,
        out_specs=(P(("dp", "fsdp"), None), P(), P(None, "fsdp")),
        check_vma=False,
    )
```

profile of v0, /device:TPU:0, one launch (start us, length us, event | category | flops | bytes accessed | tf_op | source)
XLA Modules:
  0.0 458.3 jit_solution(2193988365793274913)
XLA Ops:
  7.2 0.0 copy-start
  7.2 0.0 all-gather.5.cloned.1.call-start
  7.2 0.7 all-gather.5.cloned.1.call-update
  7.9 0.0 all-reduce.3.cloned.1.call-start
  8.0 0.2 copy-done
  8.1 7.3 %fusion.2 = f32[64,16384]{1,0:T(8,128)} fusion(bf16[256,16384]{1,0:T(8,128)(2,1)} %param.7, bf16[256,512]{1,0:T(8,128)(2,1)S(1)} %copy-done, bf16[512,64]{0,1:T(8,128)(2,1)} %param.10), kind=kOutput, calls=%fused_computation.7 | convolution fusion | flops 553664512 | bytes 12910592 | tf_op jit(solution)/shard_map/dot_general | solution.py:35
  15.4 46.8 %all-gather.5.cloned.1.call-done = bf16[64,16384]{1,0:T(8,128)(2,1)} async-done(((bf16[64,2048]{1,0:T(8,128)(2,1)}), bf16[64,16384]{1,0:T(8,128)(2,1)}) %all-gather.5.cloned.1.call-update) | async-done | bytes 2097168 | tf_op jit(solution)/shard_map/all_gather | solution.py:26
  62.2 6.6 %convolution_convert_fusion.1 = bf16[256,64]{0,1:T(8,128)(2,1)S(1)} fusion(bf16[256,16384]{1,0:T(8,128)(2,1)} %param.7, bf16[64,16384]{1,0:T(8,128)(2,1)} %all-gather.5.cloned.1.call-done), kind=kOutput, calls=%fused_computation.8 | convolution fusion | flops 536887296 | bytes 10518528 | tf_op jit(solution)/shard_map/dot_general | solution.py:14
  68.8 0.0 copy-start.3
  68.8 0.8 convolution_bitcast_fusion.1
  69.7 0.0 copy-start.1
  69.7 0.0 all-reduce.3.cloned.1.call-update
  69.7 0.0 all-gather.3.cloned.1.call-start
  69.7 0.0 copy-done.3
  69.8 1.1 broadcast_in_dim.7
  70.9 0.3 copy-done.1
  71.3 3.1 fusion
  74.4 0.0 all-gather.3.cloned.1.call-update
  74.4 137.0 %all-reduce.3.cloned.1.call-done = (f32[512,64]{0,1:T(8,128)}, f32[64,16384]{1,0:T(8,128)}) async-done(((f32[512,64]{0,1:T(8,128)}, f32[64,16384]{1,0:T(8,128)}), (f32[512,64]{0,1:T(8,128)}, f32[64,16384]{1,0:T(8,128)})) %all-reduce.3.cloned.1.call-update) | async-done | bytes 4325392 | tf_op jit(solution)/shard_map/psum | solution.py:38
  211.4 1.6 broadcast_multiply_fusion
  213.0 1.9 dynamic-slice_multiply_fusion
  214.9 0.0 copy-start.2
  214.9 225.2 %all-gather.3.cloned.1.call-done = bf16[512,16384]{1,0:T(8,128)(2,1)} async-done(((bf16[512,2048]{1,0:T(8,128)(2,1)}), bf16[512,16384]{1,0:T(8,128)(2,1)}) %all-gather.3.cloned.1.call-update) | async-done | bytes 16777232 | tf_op jit(solution)/shard_map/all_gather | solution.py:25
  440.1 10.5 %convolution_bitcast_fusion = f32[256,512]{0,1:T(8,128)S(1)} fusion(bf16[512,16384]{1,0:T(8,128)(2,1)} %all-gather.3.cloned.1.call-done, bf16[256,16384]{1,0:T(8,128)(2,1)} %param.7), kind=kOutput, calls=%fused_computation.3 | convolution fusion | flops 4294967296 | bytes 25690112 | tf_op jit(solution)/shard_map/dot_general | solution.py:14
  450.7 0.0 copy-done.2
  450.7 0.3 fusion.1
  450.9 0.8 copy.10
  (1 shorter events, 0.0 us)
Async XLA Ops:
  7.2 1.0 copy-start
  7.2 55.0 %all-gather.5.cloned.1.call-start = ((), (), s32[]{:S(2)}) async-start(), calls=%async_computation.1 | async-start | bytes 2359296 | tf_op jit(solution)/shard_map/all_gather | solution.py:26
  7.9 203.5 %all-reduce.3.cloned.1.call-start = ((), (), s32[]{:S(2)}) async-start(), calls=%async_computation.2 | async-start | bytes 8650752 | tf_op jit(solution)/shard_map/psum | solution.py:38
  68.8 0.9 copy-start.3
  69.7 1.6 copy-start.1
  69.7 370.4 %all-gather.3.cloned.1.call-start = ((), (), s32[]{:S(2)}) async-start(), calls=%async_computation | async-start | bytes 18874368 | tf_op jit(solution)/shard_map/all_gather | solution.py:25
  214.9 235.8 %copy-start.2 = (bf16[512,64]{0,1:T(8,128)(2,1)S(1)}, bf16[512,64]{0,1:T(8,128)(2,1)}, u32[]{:S(2)}) copy-start(bf16[512,64]{0,1:T(8,128)(2,1)} %param.10) | copy-start | bytes 196612
Sparse Core Ops, SparseCore 0:
  10.2 51.9 all-gather.4
  69.8 141.5 all-reduce.2
  213.8 226.2 all-gather.2
where the time goes:
time: 459 us; the launch traced here: 458 us
  waiting for transfers between devices  410 us (89%)
  matrix products  25.5 us (6%)
  between operations  13.8 us (3%)
  other arithmetic  6.58 us (1%)
    all_gather x1, waiting for transfers between devices, shards(): lax.all_gather(weight, 'fsdp', axis=1, tiled=True)  225 us
    psum x1, waiting for transfers between devices, shards(): total_a, total_b = lax.psum((term_a, term_b), ('dp', 'fsdp'))  137 us
    all_gather x1, waiting for transfers between devices, shards(): lax.all_gather(adapter_up, 'fsdp', axis=1, tiled=True)  46.8 us
    dot_general x2, matrix products, contract_cols(): lax.dot_general(left, right, (((1,), (1,)), ((), ())), preferred_element_...  17.2 us
  transfers between devices with their start and end apart: 3, of which 3 were waited for; matrix products, arithmetic and copies ran while one was open for 3% of the time, Pallas kernels for 0%

commit v1 on v0

v1 whole, which is shorter than its diff:
```python
import jax
import jax.numpy as jnp
import numpy as np
from jax import lax
from jax.experimental import pallas as pl
from jax.experimental.pallas import tpu as pltpu
from jax.sharding import PartitionSpec as P

BLOCK = 128
F32 = jnp.float32
BF16 = jnp.bfloat16
MIB = 1 << 20
VMEM_MIB = 50


def nt(left, right):
    return lax.dot_general(left, right, (((1,), (1,)), ((), ())), preferred_element_type=F32)


def nn(left, right):
    return jnp.dot(left, right, preferred_element_type=F32)


def tn(left, right):
    return lax.dot_general(left, right, (((0,), (0,)), ((), ())), preferred_element_type=F32)


def params(mib):
    return pltpu.CompilerParams(vmem_limit_bytes=mib * MIB)


def cost(flops, nbytes):
    return pl.CostEstimate(flops=flops, bytes_accessed=nbytes, transcendentals=0)


def together(*arrays):
    return lax.optimization_barrier(arrays)


def assemble(*outputs):
    pieces = [piece for output in outputs for piece in output]
    where = [
        (at, sum(count for _, _, count in output[:k]))
        for at, output in enumerate(outputs)
        for k in range(len(output))
    ]

    def body(*refs):
        ins, outs, semaphore = refs[: len(pieces)], refs[len(pieces) : -1], refs[-1]
        copies = [
            pltpu.make_async_copy(
                ins[k].at[pl.ds(start, count)], outs[to].at[pl.ds(row, count)], semaphore.at[k]
            )
            for k, ((_, start, count), (to, row)) in enumerate(zip(pieces, where))
        ]
        for copy in copies:
            copy.start()
        for copy in copies:
            copy.wait()

    return pl.pallas_call(
        body,
        in_specs=[pl.BlockSpec(memory_space=pl.ANY)] * len(pieces),
        out_specs=[pl.BlockSpec(memory_space=pl.ANY)] * len(outputs),
        out_shape=[
            jax.ShapeDtypeStruct((sum(c for _, _, c in output), output[0][0].shape[1]), BF16)
            for output in outputs
        ],
        scratch_shapes=[pltpu.SemaphoreType.DMA((len(pieces),))],
        compiler_params=params(1),
        cost_estimate=cost(0, 4 * sum(c * a.shape[1] for a, _, c in pieces)),
        name="assemble",
    )(*[a for a, _, _ in pieces])


def terms_b(info, cotangent, partner, low, low_partner, n):
    tokens, columns = cotangent.shape
    part = columns // n // 2
    span = part // 2
    rank = low.shape[0]

    def body(info, mine, partner, low, low_partner, keep, send):
        x = info[1]

        def term(which):
            here = pl.ds(pl.multiple_of(which * span, BLOCK), span)
            return nn(low[...], mine[:, here]) + nn(low_partner[...], partner[:, here])

        keep[...] = term(x)
        send[...] = term(1 - x).astype(send.dtype)

    return pl.pallas_call(
        body,
        grid_spec=pltpu.PrefetchScalarGridSpec(
            num_scalar_prefetch=1,
            grid=(n,),
            in_specs=[pl.BlockSpec((tokens, part), lambda j, info: (0, 2 * info[2 + j] + info[0]))] * 2
            + [pl.BlockSpec((rank, tokens), lambda j, info: (0, 0))] * 2,
            out_specs=[pl.BlockSpec((rank, span), lambda j, info: (0, info[2 + n + j]))] * 2,
        ),
        out_shape=[
            jax.ShapeDtypeStruct((rank, n * span), F32),
            jax.ShapeDtypeStruct((rank, n * span), BF16),
        ],
        compiler_params=params(VMEM_MIB),
        cost_estimate=cost(4 * tokens * rank * n * part, tokens * n * part * 4),
        name="terms_b",
    )(info, cotangent, partner, low, low_partner)


def products(info, first, cotangent, partner, pieces, begun, n, name):
    tokens, columns = cotangent.shape
    part = columns // n // 2
    steps = len(pieces)
    arrays = [rows[0] for piece in pieces for rows in piece]
    specs = [
        pl.BlockSpec((block, part), lambda j, info, which=which: (which, 0))
        for piece in pieces
        for _, block, which, _ in piece
    ]
    width = sum(rows.stop - rows.start for _, _, _, rows in pieces[0])
    old = [] if begun is None else [begun]
    whole = pl.BlockSpec((2 * tokens, width), lambda j, info: (0, 0))

    def body(info, mine, partner, *refs):
        row_refs, old_refs, (out, weight) = refs[: len(arrays)], refs[len(arrays) : -2], refs[-2:]
        at = pl.program_id(0)

        @pl.when(at == 0)
        def _():
            out[...] = old_refs[0][...] if old_refs else jnp.zeros_like(out)

        taken = 0
        for j, piece in enumerate(pieces):

            @pl.when(at == j)
            def _(piece=piece, taken=taken):
                start = 0
                for k, (_, _, _, rows) in enumerate(piece):
                    count = rows.stop - rows.start
                    weight[pl.ds(start, count), :] = row_refs[taken + k][pl.ds(rows.start, count), :]
                    start += count
                if start < width:
                    weight[pl.ds(start, width - start), :] = jnp.zeros((width - start, part), BF16)

            taken += len(piece)

        out[:tokens, :] += nt(mine[...], weight[...])
        out[tokens:, :] += nt(partner[...], weight[...])

    return pl.pallas_call(
        body,
        grid_spec=pltpu.PrefetchScalarGridSpec(
            num_scalar_prefetch=1,
            grid=(steps,),
            in_specs=[pl.BlockSpec((tokens, part), lambda j, info: (0, 2 * info[first + j] + info[0]))]
            * 2
            + specs
            + [whole] * len(old),
            out_specs=whole,
            scratch_shapes=[pltpu.VMEM((width, part), BF16)],
        ),
        out_shape=jax.ShapeDtypeStruct((2 * tokens, width), F32),
        compiler_params=params(VMEM_MIB),
        cost_estimate=cost(
            4 * steps * tokens * width * part, steps * part * (4 * tokens + 2 * width) + 8 * tokens * width
        ),
        name=name,
    )(info, cotangent, partner, *arrays, *old)


def finish(info, mine, other, factor, part):
    rank, wide = mine.shape
    span = wide - part

    def body(info, factor, mine, other, grad_b, grad_a):
        scale = factor[0]

        def put(first, second):
            grad_b[:, :part] = first[:, :part] * scale
            grad_b[:, part:] = second[:, :part] * scale
            grad_a[:, :span] = first[:, part:] * scale
            grad_a[:, span:] = second[:, part:] * scale

        @pl.when(info[0] == 0)
        def _():
            put(mine, other)

        @pl.when(info[0] != 0)
        def _():
            put(other, mine)

    whole = pl.BlockSpec((rank, wide), lambda i, info: (0, 0))
    return pl.pallas_call(
        body,
        grid_spec=pltpu.PrefetchScalarGridSpec(
            num_scalar_prefetch=1,
            grid=(1,),
            in_specs=[pl.BlockSpec(memory_space=pltpu.SMEM), whole, whole],
            out_specs=[
                pl.BlockSpec((rank, 2 * part), lambda i, info: (0, 0)),
                pl.BlockSpec((rank, 2 * span), lambda i, info: (0, 0)),
            ],
        ),
        out_shape=[
            jax.ShapeDtypeStruct((rank, 2 * part), F32),
            jax.ShapeDtypeStruct((rank, 2 * span), F32),
        ],
        compiler_params=params(8),
        cost_estimate=cost(0, 16 * rank * wide),
        name="finish",
    )(info, factor, mine, other)


def make(mesh):
    n = mesh.shape["fsdp"]
    dp = mesh.shape["dp"]
    half = n // 2
    order = list(range(0, n, 2)) + list(range(n - 1, 0, -2))
    bits = n.bit_length() - 1

    def forward(a):
        return lax.ppermute(a, "fsdp", [(order[i], order[(i + 1) % n]) for i in range(n)])

    def backward(a):
        return lax.ppermute(a, "fsdp", [(order[(i + 1) % n], order[i]) for i in range(n)])

    def over(a, axis, bit):
        return lax.ppermute(a, axis, [(i, i ^ bit) for i in range(mesh.shape[axis])])

    def shards(latent, cotangent, quant, scales, adapter_down, adapter_up):
        tokens = cotangent.shape[0]
        width, own = quant.shape
        rank = adapter_up.shape[0]
        part = own // 2
        given = width * 3 // 8
        ring = width - given
        device = lax.axis_index("dp")
        core = device & 1
        x = (device >> 1) & 1
        me = lax.axis_index("fsdp")
        place = jnp.where(me & 1 == 0, me >> 1, n - 1 - (me >> 1))

        def shard(offset):
            spot = (place + offset + n) & (n - 1)
            return jnp.where(spot < half, 2 * spot, 2 * (n - 1 - spot) + 1)

        offsets = [s * h for h in range(1, half) for s in (-1, 1)]
        offsets = [0] + offsets[:-2] + [-half] + offsets[-2:]
        shard_of = shard(np.array(offsets, np.int32))
        flipped = sum(((shard_of >> k) & 1) << (bits - 1 - k) for k in range(bits))
        info = jnp.concatenate([jnp.stack([core, x]), shard_of, flipped]).astype(jnp.int32)

        my_quant = lax.dynamic_slice_in_dim(quant, core * part, part, 1)
        my_scales = lax.dynamic_slice_in_dim(scales, core * (part // BLOCK), part // BLOCK, 1)
        my_up = lax.dynamic_slice_in_dim(adapter_up, core * part, part, 1)
        weight = (
            my_quant.astype(F32) * jnp.repeat(jnp.repeat(my_scales, BLOCK, axis=0), BLOCK, axis=1)
        ).astype(BF16)
        shared = weight[given:ring]
        ends = (weight[:given], weight[ring:])
        chunk = jnp.concatenate([my_up, jnp.where(x == 0, ends[0], ends[1]), shared], axis=0)
        missing = jnp.where(x == 0, ends[1], ends[0])

        stay = rank + given
        cut = max(given, ring // 2)

        def give(front, rear):
            return over(jnp.concatenate([front[rank:stay], rear[rank:stay]], axis=0), "dp", 2)

        partner = over(cotangent, "dp", 1)
        latent_partner = over(latent, "dp", 1)
        chunks, gifts = {0: chunk}, {}

        span = width // 2
        halves = jnp.concatenate(
            [lax.dynamic_slice_in_dim(a, core * span, span, 1) for a in (latent, latent_partner)], axis=0
        )

        low, low_partner = [
            lax.dot_general(adapter_down, a, (((0,), (1,)), ((), ())), preferred_element_type=F32).astype(BF16)
            for a in (latent, latent_partner)
        ]
        total_b, send = terms_b(info, cotangent, partner, low, low_partner, n)
        arrived = over(send, "dp", 2)

        chunks[-1], chunks[1] = together(forward(chunk), backward(chunk), send)[:2]
        far_up = lax.ppermute(
            together(my_up, chunks[1])[0], "fsdp", [(order[i], order[(i + half) % n]) for i in range(n)]
        )
        chunks[-2], chunks[2] = forward(chunks[-1]), backward(chunks[1])

        def ups_of(hop):
            return [[(chunks[s * hop], rank, 0, range(rank))] for s in (-1, 1)]

        def product(first, pieces, begun, name):
            return products(info, 2 + first, cotangent, partner, pieces, begun, n, name)

        sums = product(0, [[(chunk, rank, 0, range(rank))]] + ups_of(1), None, "through_first")
        front, rear, arrived, sums = together(chunks[-1], chunks[1], arrived, sums)
        gifts[1] = give(front, rear)

        def rows_of(hop):
            return [
                [
                    (chunks[s * hop], rank + ring, 0, range(rank, rank + ring)),
                    (gifts[hop], given, (s + 1) // 2, range(given)),
                ]
                for s in (-1, 1)
            ]

        own = [
            (chunk, rank + ring, 0, range(rank, rank + ring)),
            (missing, given, 0, range(given)),
        ]
        def halve(total, bit):
            size = total.shape[1] // 2
            side = (me // bit) & 1
            return (
                lax.dynamic_slice_in_dim(total, (1 - side) * size, size, 1).astype(BF16),
                lax.dynamic_slice_in_dim(total, side * size, size, 1),
            )

        sent, total_b = halve(total_b + arrived.astype(F32), 1)

        done = product(0, [own] + rows_of(1), None, "first")
        for hop in range(3, half):
            chunks[-hop], chunks[hop] = forward(chunks[1 - hop]), backward(chunks[hop - 1])
            gifts[hop - 1] = give(chunks[1 - hop], chunks[hop - 1])
            if hop < half - 1:
                chunks[-hop], chunks[hop], gifts[hop - 1], done = together(
                    chunks[-hop], chunks[hop], gifts[hop - 1], done
                )
                done = product(2 * hop - 3, rows_of(hop - 1), done, "middle")

        pieces = []
        for k in range(2, half - 1):
            pieces += ups_of(k)
        pieces += [[(far_up, rank, 0, range(rank))]]
        sums = product(3, pieces, sums, "through_second")
        part_b = over(together(sent, chunks[-2])[0], "fsdp", 1)
        hop = half - 1
        chunks[-hop], chunks[hop], done, sums = together(chunks[-hop], chunks[hop], done, sums)
        gift, front, rear = assemble(
            [(chunks[k * hop], rank, given) for k in (-1, 1)],
            [(chunks[-hop], rank, cut)],
            [(chunks[hop], rank + cut, ring - cut)],
        )
        gifts[hop] = over(gift, "dp", 2)
        sums, gift = together(sums, gift)
        both_sums = product(2 * hop, ups_of(hop), sums, "through_last")
        others = over(both_sums, "dp", 1)
        part_b = together(part_b, both_sums)[0]
        swapped = jnp.concatenate([others[tokens:], others[:tokens]], axis=0)
        through = (both_sums + swapped).astype(BF16)

        total_a = tn(through, halves)
        through = through[:tokens]
        part_a = over(total_a, "fsdp", 1)
        done = product(2 * hop - 3, rows_of(hop - 1), done, "middle")

        total_a, total_b = total_a + part_a, total_b + part_b.astype(F32)
        sent, total_b = halve(total_b, 2)
        front, rear, total_a, sent, done = together(
            forward(front), backward(rear), total_a, sent, done
        )
        gifts[half] = over(front[:given], "dp", 2)
        part_a, part_b = over(total_a, "fsdp", 2), over(sent, "fsdp", 2)
        part_a, part_b, done, gifts[hop] = together(part_a, part_b, done, gifts[hop])
        total_a, total_b = total_a + part_a, total_b + part_b.astype(F32)
        done = product(2 * half - 2, rows_of(half - 1), done, "late")
        bit = 4
        while bit < n:
            total_a = total_a + over(total_a, "fsdp", bit)
            sent, total_b = halve(total_b, bit)
            total_b = total_b + over(sent, "fsdp", bit).astype(F32)
            bit *= 2
        bit = 4
        while bit < dp:
            total_a = total_a + over(total_a, "dp", bit)
            total_b = total_b + over(total_b, "dp", bit)
            bit *= 2
        total_a, total_b, gifts[half], done = together(total_a, total_b, gifts[half], done)
        totals = jnp.concatenate([total_b, total_a], axis=1)
        others = over(totals, "dp", 2)
        last = [
            (front, cut, 0, range(cut)),
            (rear, ring - cut, 0, range(ring - cut)),
            (gifts[half], given, 0, range(given)),
        ]
        done = product(2 * half - 3, [last], done, "last")
        others, swapped = together(others, over(done[tokens:], "dp", 1))
        other_b, total_a = others[:, : part // 2], total_a + others[:, part // 2 :]
        low_x, high_x = jnp.where(x == 0, total_b, other_b), jnp.where(x == 0, other_b, total_b)
        ends = jnp.concatenate([low_x, high_x, total_a], axis=1)
        other_ends = over(ends, "dp", 1)
        factor = 1.0 / jnp.sqrt(F32(tokens * dp * n))
        grad_b, grad_a = finish(info, ends, other_ends, factor.reshape(1), part)
        grad_a = grad_a.T

        frozen = done[:tokens] + swapped
        begin, middle, end = frozen[:, :given], frozen[:, given:ring], frozen[:, ring:]
        frozen = jnp.concatenate(
            [jnp.where(x == 0, begin, end), middle, jnp.where(x == 0, end, begin)], axis=1
        )
        latent_gradient = (frozen + nt(through, adapter_down)).astype(BF16)
        return (latent_gradient, grad_a, grad_b)

    return shards


def solution(mesh):
    placed = (
        P(("dp", "fsdp"), None),
        P(("dp", "fsdp"), None),
        P(None, "fsdp"),
        P(None, "fsdp"),
        P(),
        P(None, "fsdp"),
    )
    return jax.shard_map(
        make(mesh),
        mesh=mesh,
        in_specs=placed,
        out_specs=(P(("dp", "fsdp"), None), P(), P(None, "fsdp")),
        check_vma=False,
    )
```

time: 459 us -> 118 us (0.26)
  waiting for transfers between devices: 410 us -> 29.8 us
  Pallas kernels: 0 us -> 37.5 us
  starting transfers between devices: 0.12 us -> 34.6 us
  matrix products: 25.5 us -> 1.52 us
  between operations: 13.8 us -> 1.17 us
  local copies, waits for them, and re-layouts: 2.52 us -> 8.59 us
    all_gather x2 -> x0, waiting for transfers between devices: 272 us -> none  [the longest x1 225 us: shards(): lax.all_gather(weight, 'fsdp', axis=1, tiled=True)]
    psum x1 -> x0, waiting for transfers between devices: 137 us -> none  [shards(): total_a, total_b = lax.psum((term_a, term_b), ('dp', 'fsdp'))]
    pallas_call x0 -> x10, Pallas kernels: none -> 37.5 us  [the longest x7 27 us: products(): pl.pallas_call(body, grid_spec=pltpu.PrefetchScalarGridSpec(num_scalar_pr...]
    ppermute x0 -> x26, starting transfers between devices: none -> 34.6 us  [the longest x17 19.7 us: over(): lax.ppermute(a, axis, [(i, i ^ bit) for i in range(mesh.shape[axis])])]
    ppermute x0 -> x26, waiting for transfers between devices: none -> 29.8 us  [the longest x17 24.9 us: over(): lax.ppermute(a, axis, [(i, i ^ bit) for i in range(mesh.shape[axis])])]
    dot_general x5 -> x4, matrix products: 25.5 us -> 1.52 us  [the longest x1 0.93 us: nt(): lax.dot_general(left, right, (((1,), (1,)), ((), ())), preferred_element_...]
  transfers between devices with their start and end apart: 3 -> 26, of which waited for: 3 -> 11; matrix products, arithmetic and copies ran while one was open for 3% -> 9% of each run, Pallas kernels for 0% -> 29%
where the time goes in v1:
time: 118 us; the launch traced here: 117 us
  Pallas kernels  37.5 us (32%)
  starting transfers between devices  34.6 us (29%)
  waiting for transfers between devices  29.8 us (25%)
  local copies, waits for them, and re-layouts  8.59 us (7%)
  other arithmetic  4.24 us (4%)
  matrix products  1.52 us (1%)
    pallas_call x7, Pallas kernels, products(): pl.pallas_call(body, grid_spec=pltpu.PrefetchScalarGridSpec(num_scalar_pr...  27 us
    ppermute x17, waiting for transfers between devices, over(): lax.ppermute(a, axis, [(i, i ^ bit) for i in range(mesh.shape[axis])])  24.9 us
    ppermute x17, starting transfers between devices, over(): lax.ppermute(a, axis, [(i, i ^ bit) for i in range(mesh.shape[axis])])  19.7 us
    pallas_call x1, Pallas kernels, terms_b(): pl.pallas_call(body, grid_spec=pltpu.PrefetchScalarGridSpec(num_scalar_pr...  8.17 us
    ppermute x4, starting transfers between devices, backward(): lax.ppermute(a, 'fsdp', [(order[(i + 1) % n], order[i]) for i in range(n)])  6.36 us
    ppermute x4, starting transfers between devices, forward(): lax.ppermute(a, 'fsdp', [(order[i], order[(i + 1) % n]) for i in range(n)])  4.9 us
    ppermute x1, starting transfers between devices, shards(): lax.ppermute(together(my_up, chunks[1])[0], 'fsdp', [(order[i], order[(i...  3.61 us
    ppermute x4, waiting for transfers between devices, forward(): lax.ppermute(a, 'fsdp', [(order[i], order[(i + 1) % n]) for i in range(n)])  3.54 us
  transfers between devices with their start and end apart: 26, of which 11 were waited for; matrix products, arithmetic and copies ran while one was open for 9% of the time, Pallas kernels for 29%

profile of v1, /device:TPU:0, one launch (start us, length us, event | category | flops | bytes accessed | tf_op | source)
XLA Modules:
  0.0 117.4 jit_solution(7719162054110527764)
XLA Ops:
  0.7 0.5 collective-permute-start
  1.2 0.9 constant_dynamic-slice_fusion.2
  2.1 0.6 broadcast_in_dim.7
  2.7 0.6 fusion
  3.4 0.8 broadcast_select_fusion
  4.3 2.6 %collective-permute-start.2 = (bf16[384,1024]{1,0:T(8,128)(2,1)S(1)}, bf16[384,1024]{1,0:T(8,128)(2,1)S(1)}, u32[]{:S(2)}, u32[]{:S(2)}) collective-permute-start(bf16[384,1024]{1,0:T(8,128)(2,1)S(1)} %pad_maximum_fusion.refs_0_), channel_id=1, source_target_pairs={{2,0},{4,2},{6,4},{7,6},{5,7},{3,5},{1,3},{0,1},{10,8},{12,10},{14... | collective-permute-start | bytes 2359304 | tf_op jit(solution)/shard_map/ppermute | solution.py:226
  6.9 0.1 collective-permute-start.1
  7.1 0.1 pad_add_fusion.info
  7.2 0.2 convolution_convert_fusion.1.low
  7.4 7.0 %collective-permute-done.3 = bf16[256,512]{1,0:T(8,128)(2,1)S(1)} collective-permute-done((bf16[256,512]{1,0:T(8,128)(2,1)S(1)}, bf16[256,512]{1,0:T(8,128)(2,1)S(1)}, u32[]{:S(2)}, u32[]{:S(2)}) %collective-permute-start.3) | collective-permute-done | bytes 262176 | tf_op jit(solution)/shard_map/ppermute | solution.py:229
  14.3 0.2 convolution_convert_fusion.low_partner
  14.5 8.2 %terms_b.1 = (f32[64,4096]{1,0:T(8,128)S(1)}, bf16[64,4096]{1,0:T(8,128)(2,1)}) custom-call(s32[18]{0:T(128)S(1)} %pad_add_fusion.info, bf16[256,16384]{1,0:T(8,128)(2,1)} %mine.15, bf16[256,16384]{1,0:T(8,128)(2,1)} %collective-permute-done.partner, bf16[64,256]{1,0:T(8,128)(2,1)S(1)} %convolution_convert_fusion.1.low, ...), custom_call_target="tpu_custom_call" | custom-call | flops 536870912 | bytes 8388608 | tf_op jit(solution)/shard_map/terms_b/pallas_call | solution.py:92
  22.7 1.0 copy-done.7
  23.7 1.3 %collective-permute-done.2.refs_2_.refs_4_ = bf16[384,1024]{1,0:T(8,128)(2,1)S(1)} collective-permute-done((bf16[384,1024]{1,0:T(8,128)(2,1)S(1)}, bf16[384,1024]{1,0:T(8,128)(2,1)S(1)}, u32[]{:S(2)}, u32[]{:S(2)}) %collective-permute-start.2) | collective-permute-done | bytes 786464 | tf_op jit(solution)/shard_map/ppermute | solution.py:226
  25.0 1.4 %collective-permute-done.1.refs_1_.refs_2_ = bf16[384,1024]{1,0:T(8,128)(2,1)S(1)} collective-permute-done((bf16[384,1024]{1,0:T(8,128)(2,1)S(1)}, bf16[384,1024]{1,0:T(8,128)(2,1)S(1)}, u32[]{:S(2)}, u32[]{:S(2)}) %collective-permute-start.1) | collective-permute-done | bytes 786464 | tf_op jit(solution)/shard_map/ppermute | solution.py:223
  26.4 0.4 collective-permute-start.4
  26.8 1.6 %collective-permute-start.6 = (bf16[384,1024]{1,0:T(8,128)(2,1)S(1)}, bf16[384,1024]{1,0:T(8,128)(2,1)}, u32[]{:S(2)}, u32[]{:S(2)}) collective-permute-start(bf16[384,1024]{1,0:T(8,128)(2,1)S(1)} %collective-permute-done.2.refs_2_.refs_4_), channel_id=1, source_target_pairs={{2,0},{4,2},{6,4},{7,6},{5,7},{3,5},{1,3},{0,1},{10,8},{12,10},{14... | collective-permute-start | bytes 2359304 | tf_op jit(solution)/shard_map/ppermute | solution.py:226
  28.4 1.5 %collective-permute-start.8 = (bf16[64,4096]{1,0:T(8,128)(2,1)}, bf16[64,4096]{1,0:T(8,128)(2,1)}, u32[]{:S(2)}, u32[]{:S(2)}) collective-permute-start(bf16[64,4096]{1,0:T(8,128)(2,1)} %get-tuple-element.39), channel_id=1, source_target_pairs={{0,16},{8,24},{16,0},{24,8},{1,17},{9,25},{17,1},{25,9},{2,18},{10... | collective-permute-start | bytes 1572872 | tf_op jit(solution)/shard_map/ppermute | solution.py:229
  29.9 0.9 constant_dynamic-slice_fusion.1
  30.8 0.9 constant_dynamic-slice_fusion
  31.8 3.6 %collective-permute-start.10 = (bf16[64,1024]{1,0:T(8,128)(2,1)}, bf16[64,1024]{1,0:T(8,128)(2,1)S(1)}, u32[]{:S(2)}, u32[]{:S(2)}) collective-permute-start(bf16[64,1024]{1,0:T(8,128)(2,1)} %copy-done.16), channel_id=1, source_target_pairs={{0,7},{2,5},{4,3},{6,1},{7,0},{5,2},{3,4},{1,6},{8,15},{10,13},{12... | collective-permute-start | bytes 393224 | tf_op jit(solution)/shard_map/ppermute | solution.py:288
  35.4 3.9 %through_first.1.refs_3_ = f32[512,64]{1,0:T(8,128)S(1)} custom-call(s32[18]{0:T(128)S(1)} %pad_add_fusion.info, bf16[256,16384]{1,0:T(8,128)(2,1)} %mine.15, bf16[256,16384]{1,0:T(8,128)(2,1)} %collective-permute-done.partner, bf16[384,1024]{1,0:T(8,128)(2,1)S(1)} %pad_maximum_fusion.refs_0_, bf16[384,1024]{1,0:T(8,128)(2,1)S(1)} %collective-permute-done.1.refs_1_.refs_2_, ...), custom_call_target="tpu_custom_call" | custom-call | flops 201326592 | bytes 3670016 | tf_op jit(solution)/shard_map/through_first/pallas_call | solution.py:151
  39.3 1.9 %collective-permute-done.8 = bf16[64,4096]{1,0:T(8,128)(2,1)} collective-permute-done((bf16[64,4096]{1,0:T(8,128)(2,1)}, bf16[64,4096]{1,0:T(8,128)(2,1)}, u32[]{:S(2)}, u32[]{:S(2)}) %collective-permute-start.8) | collective-permute-done | bytes 524320 | tf_op jit(solution)/shard_map/ppermute | solution.py:229
  41.4 1.6 %collective-permute-start.9 = (bf16[384,1024]{1,0:T(8,128)(2,1)S(1)}, bf16[384,1024]{1,0:T(8,128)(2,1)S(1)}, u32[]{:S(2)}, u32[]{:S(2)}) collective-permute-start(bf16[384,1024]{1,0:T(8,128)(2,1)S(1)} %pad_maximum_fusion.1), channel_id=1, source_target_pairs={{0,16},{8,24},{16,0},{24,8},{1,17},{9,25},{17,1},{25,9},{2,18},{10... | collective-permute-start | bytes 2359304 | tf_op jit(solution)/shard_map/ppermute | solution.py:229
  42.9 2.1 %collective-permute-done.4.refs_0_ = bf16[384,1024]{1,0:T(8,128)(2,1)S(1)} collective-permute-done((bf16[384,1024]{1,0:T(8,128)(2,1)S(1)}, bf16[384,1024]{1,0:T(8,128)(2,1)S(1)}, u32[]{:S(2)}, u32[]{:S(2)}) %collective-permute-start.4) | collective-permute-done | bytes 786464 | tf_op jit(solution)/shard_map/ppermute | solution.py:223
  45.1 3.9 %collective-permute-start.5 = (bf16[384,1024]{1,0:T(8,128)(2,1)S(1)}, bf16[384,1024]{1,0:T(8,128)(2,1)S(1)}, u32[]{:S(2)}, u32[]{:S(2)}) collective-permute-start(bf16[384,1024]{1,0:T(8,128)(2,1)S(1)} %collective-permute-done.4.refs_0_), channel_id=1, source_target_pairs={{0,2},{2,4},{4,6},{6,7},{7,5},{5,3},{3,1},{1,0},{8,10},{10,12},{12... | collective-permute-start | bytes 2359304 | tf_op jit(solution)/shard_map/ppermute | solution.py:223
  49.0 1.2 convert_add_fusion
  50.2 3.3 %collective-permute-start.15 = (bf16[64,2048]{1,0:T(8,128)(2,1)S(1)}, bf16[64,2048]{1,0:T(8,128)(2,1)S(1)}, u32[]{:S(2)}, u32[]{:S(2)}) collective-permute-start(bf16[64,2048]{1,0:T(8,128)(2,1)S(1)} %dynamic-slice_convert_fusion), channel_id=1, source_target_pairs={{0,1},{1,0},{2,3},{3,2},{4,5},{5,4},{6,7},{7,6},{8,9},{9,8},{10,11... | collective-permute-start | bytes 786440 | tf_op jit(solution)/shard_map/ppermute | solution.py:229
  53.5 1.0 slice.74
  54.7 1.6 %collective-permute-start.16 = (bf16[384,1024]{1,0:T(8,128)(2,1)S(1)}, bf16[384,1024]{1,0:T(8,128)(2,1)S(1)}, u32[]{:S(2)}, u32[]{:S(2)}) collective-permute-start(bf16[384,1024]{1,0:T(8,128)(2,1)S(1)} %pad_maximum_fusion.2), channel_id=1, source_target_pairs={{0,16},{8,24},{16,0},{24,8},{1,17},{9,25},{17,1},{25,9},{2,18},{10... | collective-permute-start | bytes 2359304 | tf_op jit(solution)/shard_map/ppermute | solution.py:229
  56.2 3.9 %through_second.1.refs_2_ = f32[512,64]{1,0:T(8,128)S(1)} custom-call(s32[18]{0:T(128)S(1)} %pad_add_fusion.info, bf16[256,16384]{1,0:T(8,128)(2,1)} %mine.15, bf16[256,16384]{1,0:T(8,128)(2,1)} %collective-permute-done.partner, bf16[384,1024]{1,0:T(8,128)(2,1)S(1)} %collective-permute-done.4.refs_0_, ...), custom_call_target="tpu_custom_call" | custom-call | flops 201326592 | bytes 3670016 | tf_op jit(solution)/shard_map/through_second/pallas_call | solution.py:151
  60.2 1.7 %collective-permute-done.9.refs_3_.refs_5_ = bf16[384,1024]{1,0:T(8,128)(2,1)S(1)} collective-permute-done((bf16[384,1024]{1,0:T(8,128)(2,1)S(1)}, bf16[384,1024]{1,0:T(8,128)(2,1)S(1)}, u32[]{:S(2)}, u32[]{:S(2)}) %collective-permute-start.9) | collective-permute-done | bytes 786464 | tf_op jit(solution)/shard_map/ppermute | solution.py:229
  61.9 5.7 %first.1.refs_4_ = f32[512,512]{1,0:T(8,128)} custom-call(s32[18]{0:T(128)S(1)} %pad_add_fusion.info, bf16[256,16384]{1,0:T(8,128)(2,1)} %mine.15, bf16[256,16384]{1,0:T(8,128)(2,1)} %collective-permute-done.partner, bf16[384,1024]{1,0:T(8,128)(2,1)S(1)} %pad_maximum_fusion.refs_0_, bf16[192,1024]{1,0:T(8,128)(2,1)S(1)} %copy-done.6, ...), custom_call_target="tpu_custom_call" | custom-call | flops 1610612736 | bytes 7340032 | tf_op jit(solution)/shard_map/first/pallas_call | solution.py:151
  67.6 0.9 assemble.1
  68.5 1.6 %collective-permute-start.19 = (bf16[384,1024]{1,0:T(8,128)(2,1)}, bf16[384,1024]{1,0:T(8,128)(2,1)S(1)}, u32[]{:S(2)}, u32[]{:S(2)}) collective-permute-start(bf16[384,1024]{1,0:T(8,128)(2,1)} %get-tuple-element.51), channel_id=1, source_target_pairs={{0,16},{8,24},{16,0},{24,8},{1,17},{9,25},{17,1},{25,9},{2,18},{10... | collective-permute-start | bytes 2359304 | tf_op jit(solution)/shard_map/ppermute | solution.py:229
  70.1 2.7 %through_last.1 = f32[512,64]{1,0:T(8,128)S(1)} custom-call(s32[18]{0:T(128)S(1)} %pad_add_fusion.info, bf16[256,16384]{1,0:T(8,128)(2,1)} %mine.15, bf16[256,16384]{1,0:T(8,128)(2,1)} %collective-permute-done.partner, bf16[384,1024]{1,0:T(8,128)(2,1)S(1)} %collective-permute-done.5.refs_0_.refs_2_, ...), custom_call_target="tpu_custom_call" | custom-call | flops 134217728 | bytes 2490368 | tf_op jit(solution)/shard_map/through_last/pallas_call | solution.py:151
  72.9 2.1 %collective-permute-start.12 = (bf16[128,1024]{1,0:T(8,128)(2,1)S(1)}, bf16[128,1024]{1,0:T(8,128)(2,1)S(1)}, u32[]{:S(2)}, u32[]{:S(2)}) collective-permute-start(bf16[128,1024]{1,0:T(8,128)(2,1)S(1)} %get-tuple-element.49), channel_id=1, source_target_pairs={{2,0},{4,2},{6,4},{7,6},{5,7},{3,5},{1,3},{0,1},{10,8},{12,10},{14... | collective-permute-start | bytes 786440 | tf_op jit(solution)/shard_map/ppermute | solution.py:226
  75.1 0.4 collective-permute-start.11
  75.6 0.7 dynamic-slice_convert_fusion.1
  76.4 0.2 fusion.3
  76.6 1.6 %collective-permute-start.14 = (f32[64,256]{1,0:T(8,128)S(1)}, f32[64,256]{1,0:T(8,128)S(1)}, u32[]{:S(2)}, u32[]{:S(2)}) collective-permute-start(f32[64,256]{1,0:T(8,128)S(1)} %fusion.3), channel_id=1, source_target_pairs={{0,1},{1,0},{2,3},{3,2},{4,5},{5,4},{6,7},{7,6},{8,9},{9,8},{10,11... | collective-permute-start | bytes 196616 | tf_op jit(solution)/shard_map/ppermute | solution.py:229
  78.2 0.5 collective-permute-done.16.refs_1_.refs_3_
  78.8 4.2 %middle.1.refs_4_ = f32[512,512]{1,0:T(8,128)S(1)} custom-call(s32[18]{0:T(128)S(1)} %pad_add_fusion.info, bf16[256,16384]{1,0:T(8,128)(2,1)} %mine.15, bf16[256,16384]{1,0:T(8,128)(2,1)} %collective-permute-done.partner, bf16[384,1024]{1,0:T(8,128)(2,1)S(1)} %collective-permute-done.4.refs_0_, ...), custom_call_target="tpu_custom_call" | custom-call | flops 1073741824 | bytes 5242880 | tf_op jit(solution)/shard_map/middle/pallas_call | solution.py:151
  83.0 1.0 copy-done.5
  83.9 3.7 %collective-permute-done.14 = f32[64,256]{1,0:T(8,128)S(1)} collective-permute-done((f32[64,256]{1,0:T(8,128)S(1)}, f32[64,256]{1,0:T(8,128)S(1)}, u32[]{:S(2)}, u32[]{:S(2)}) %collective-permute-start.14) | collective-permute-done | bytes 65568 | tf_op jit(solution)/shard_map/ppermute | solution.py:229
  87.7 0.7 copy-done.9
  88.4 2.0 %collective-permute-start.17 = (f32[64,256]{1,0:T(8,128)S(1)}, f32[64,256]{1,0:T(8,128)S(1)}, u32[]{:S(2)}, u32[]{:S(2)}) collective-permute-start(f32[64,256]{1,0:T(8,128)S(1)} %add.93), channel_id=1, source_target_pairs={{0,2},{1,3},{2,0},{3,1},{4,6},{5,7},{6,4},{7,5},{8,10},{9,11},{10,... | collective-permute-start | bytes 196616 | tf_op jit(solution)/shard_map/ppermute | solution.py:229
  90.4 0.6 collective-permute-start.22
  91.0 3.8 %collective-permute-done.17 = f32[64,256]{1,0:T(8,128)S(1)} collective-permute-done((f32[64,256]{1,0:T(8,128)S(1)}, f32[64,256]{1,0:T(8,128)S(1)}, u32[]{:S(2)}, u32[]{:S(2)}) %collective-permute-start.17) | collective-permute-done | bytes 65568 | tf_op jit(solution)/shard_map/ppermute | solution.py:229
  94.8 1.0 convert_add_fusion.2
  95.9 2.5 %collective-permute-start.21 = (bf16[64,512]{1,0:T(8,128)(2,1)S(1)}, bf16[64,512]{1,0:T(8,128)(2,1)S(1)}, u32[]{:S(2)}, u32[]{:S(2)}) collective-permute-start(bf16[64,512]{1,0:T(8,128)(2,1)S(1)} %dynamic-slice_convert_fusion.2), channel_id=1, source_target_pairs={{0,4},{1,5},{2,6},{3,7},{4,0},{5,1},{6,2},{7,3},{8,12},{9,13},{10,... | collective-permute-start | bytes 196616 | tf_op jit(solution)/shard_map/ppermute | solution.py:229
  98.4 0.5 collective-permute-start.20
  98.9 4.0 %late.1.refs_3_ = f32[512,512]{1,0:T(8,128)S(1)} custom-call(s32[18]{0:T(128)S(1)} %pad_add_fusion.info, bf16[256,16384]{1,0:T(8,128)(2,1)} %mine.15, bf16[256,16384]{1,0:T(8,128)(2,1)} %collective-permute-done.partner, bf16[384,1024]{1,0:T(8,128)(2,1)S(1)} %collective-permute-done.5.refs_0_.refs_2_, ...), custom_call_target="tpu_custom_call" | custom-call | flops 1073741824 | bytes 5242880 | tf_op jit(solution)/shard_map/late/pallas_call | solution.py:151
  102.8 0.7 collective-permute-done.20
  103.6 2.6 %last.1 = f32[512,512]{1,0:T(8,128)S(1)} custom-call(s32[18]{0:T(128)S(1)} %pad_add_fusion.info, bf16[256,16384]{1,0:T(8,128)(2,1)} %mine.15, bf16[256,16384]{1,0:T(8,128)(2,1)} %collective-permute-done.partner, bf16[192,1024]{1,0:T(8,128)(2,1)} %collective-permute-done.11.refs_0_, bf16[128,1024]{1,0:T(8,128)(2,1)S(1)} %copy-done.10, ...), custom_call_target="tpu_custom_call" | custom-call | flops 536870912 | bytes 3145728 | tf_op jit(solution)/shard_map/last/pallas_call | solution.py:151
  106.3 0.1 collective-permute-start.24
  106.4 2.1 %collective-permute-start.23 = (f32[64,768]{1,0:T(8,128)S(1)}, f32[64,768]{1,0:T(8,128)S(1)}, u32[]{:S(2)}, u32[]{:S(2)}) collective-permute-start(f32[64,768]{1,0:T(8,128)S(1)} %pad_maximum_fusion.4), channel_id=1, source_target_pairs={{0,16},{8,24},{16,0},{24,8},{1,17},{9,25},{17,1},{25,9},{2,18},{10... | collective-permute-start | bytes 589832 | tf_op jit(solution)/shard_map/ppermute | solution.py:229
  108.5 5.6 %collective-permute-done.23 = f32[64,768]{1,0:T(8,128)S(1)} collective-permute-done((f32[64,768]{1,0:T(8,128)S(1)}, f32[64,768]{1,0:T(8,128)S(1)}, u32[]{:S(2)}, u32[]{:S(2)}) %collective-permute-start.23) | collective-permute-done | bytes 196640 | tf_op jit(solution)/shard_map/ppermute | solution.py:229
  114.2 0.1 slice_add_fusion
  114.4 0.1 slice_select_fusion.1
  114.5 0.1 slice.79
  114.6 0.5 copy-done.18
  115.1 0.9 fusion.1
  116.0 1.4 %finish.1 = (f32[64,2048]{1,0:T(8,128)}, f32[64,512]{1,0:T(8,128)}) custom-call(s32[18]{0:T(128)S(1)} %pad_add_fusion.info, f32[1]{0:T(128)} %constant.69.clone.1.factor, f32[64,1280]{1,0:T(8,128)S(1)} %pad_maximum_fusion.3.mine, f32[64,1280]{1,0:T(8,128)S(1)} %collective-permute-done.25.other), custom_call_target="tpu_custom_call" | custom-call | bytes 1310720 | tf_op jit(solution)/shard_map/finish/pallas_call | solution.py:194
  (80 shorter events, 1.0 us)
Async XLA Ops:
  0.6 2.7 %copy-start = (bf16[64,2048]{1,0:T(8,128)(2,1)S(1)}, bf16[64,2048]{1,0:T(8,128)(2,1)}, u32[]{:S(2)}) copy-start(bf16[64,2048]{1,0:T(8,128)(2,1)} %param.12) | copy-start | bytes 786436
  0.6 2.1 %copy-start.15 = (bf16[512,2048]{1,0:T(8,128)(2,1)S(1)}, bf16[512,2048]{1,0:T(8,128)(2,1)}, u32[]{:S(2)}) copy-start(bf16[512,2048]{1,0:T(8,128)(2,1)} %param.9) | copy-start | bytes 6291460
  0.7 13.9 %collective-permute-start = (bf16[256,16384]{1,0:T(8,128)(2,1)}, bf16[256,16384]{1,0:T(8,128)(2,1)}, u32[]{:S(2)}, u32[]{:S(2)}) collective-permute-start(bf16[256,16384]{1,0:T(8,128)(2,1)} %mine.15), channel_id=1, source_target_pairs={{0,8},{8,0},{16,24},{24,16},{1,9},{9,1},{17,25},{25,17},{2,10},{10... | collective-permute-start | bytes 25165832 | tf_op jit(solution)/shard_map/ppermute | solution.py:229
  3.4 0.9 copy-start.16
  3.4 3.7 %copy-start.12 = (bf16[256,512]{1,0:T(8,128)(2,1)S(1)}, bf16[256,512]{1,0:T(8,128)(2,1)}, u32[]{:S(2)}) copy-start(bf16[256,512]{1,0:T(8,128)(2,1)} %param.7) | copy-start | bytes 786436
  3.4 3.7 %copy-start.19 = (s32[8]{0:T(128)S(1)}, s32[8]{0:T(128)}, u32[]{:S(2)}) copy-start(s32[8]{0:T(128)} %constant.70.clone) | copy-start | bytes 100
  3.4 3.8 %copy-start.14 = (bf16[512,64]{0,1:T(8,128)(2,1)S(1)}, bf16[512,64]{0,1:T(8,128)(2,1)}, u32[]{:S(2)}) copy-start(bf16[512,64]{0,1:T(8,128)(2,1)} %param.11) | copy-start | bytes 196612
  4.3 20.7 %collective-permute-start.2 = (bf16[384,1024]{1,0:T(8,128)(2,1)S(1)}, bf16[384,1024]{1,0:T(8,128)(2,1)S(1)}, u32[]{:S(2)}, u32[]{:S(2)}) collective-permute-start(bf16[384,1024]{1,0:T(8,128)(2,1)S(1)} %pad_maximum_fusion.refs_0_), channel_id=1, source_target_pairs={{2,0},{4,2},{6,4},{7,6},{5,7},{3,5},{1,3},{0,1},{10,8},{12,10},{14... | collective-permute-start | bytes 2359304 | tf_op jit(solution)/shard_map/ppermute | solution.py:226
  6.9 19.5 %collective-permute-start.1 = (bf16[384,1024]{1,0:T(8,128)(2,1)S(1)}, bf16[384,1024]{1,0:T(8,128)(2,1)S(1)}, u32[]{:S(2)}, u32[]{:S(2)}) collective-permute-start(bf16[384,1024]{1,0:T(8,128)(2,1)S(1)} %pad_maximum_fusion.refs_0_), channel_id=1, source_target_pairs={{0,2},{2,4},{4,6},{6,7},{7,5},{5,3},{3,1},{1,0},{8,10},{10,12},{12... | collective-permute-start | bytes 2359304 | tf_op jit(solution)/shard_map/ppermute | solution.py:223
  7.0 7.3 %collective-permute-start.3 = (bf16[256,512]{1,0:T(8,128)(2,1)S(1)}, bf16[256,512]{1,0:T(8,128)(2,1)S(1)}, u32[]{:S(2)}, u32[]{:S(2)}) collective-permute-start(bf16[256,512]{1,0:T(8,128)(2,1)S(1)} %copy-done.12), channel_id=1, source_target_pairs={{0,8},{8,0},{16,24},{24,16},{1,9},{9,1},{17,25},{25,17},{2,10},{10... | collective-permute-start | bytes 786440 | tf_op jit(solution)/shard_map/ppermute | solution.py:229
  14.3 8.4 %copy-start.13 = (bf16[256,512]{1,0:T(8,128)(2,1)}, bf16[256,512]{1,0:T(8,128)(2,1)S(1)}, u32[]{:S(2)}) copy-start(bf16[256,512]{1,0:T(8,128)(2,1)S(1)} %collective-permute-done.3) | copy-start | bytes 786436
  22.7 1.0 copy-start.7
  25.0 16.3 %copy-start.1 = (bf16[384,1024]{1,0:T(8,128)(2,1)}, bf16[384,1024]{1,0:T(8,128)(2,1)S(1)}, u32[]{:S(2)}) copy-start(bf16[384,1024]{1,0:T(8,128)(2,1)S(1)} %collective-permute-done.2.refs_2_.refs_4_) | copy-start | bytes 2359300
  26.4 14.8 %copy-start.3 = (bf16[384,1024]{1,0:T(8,128)(2,1)}, bf16[384,1024]{1,0:T(8,128)(2,1)S(1)}, u32[]{:S(2)}) copy-start(bf16[384,1024]{1,0:T(8,128)(2,1)S(1)} %collective-permute-done.1.refs_1_.refs_2_) | copy-start | bytes 2359300
  26.4 18.7 %collective-permute-start.4 = (bf16[384,1024]{1,0:T(8,128)(2,1)S(1)}, bf16[384,1024]{1,0:T(8,128)(2,1)S(1)}, u32[]{:S(2)}, u32[]{:S(2)}) collective-permute-start(bf16[384,1024]{1,0:T(8,128)(2,1)S(1)} %collective-permute-done.1.refs_1_.refs_2_), channel_id=1, source_target_pairs={{0,2},{2,4},{4,6},{6,7},{7,5},{5,3},{3,1},{1,0},{8,10},{10,12},{12... | collective-permute-start | bytes 2359304 | tf_op jit(solution)/shard_map/ppermute | solution.py:223
  26.8 22.2 %collective-permute-start.6 = (bf16[384,1024]{1,0:T(8,128)(2,1)S(1)}, bf16[384,1024]{1,0:T(8,128)(2,1)}, u32[]{:S(2)}, u32[]{:S(2)}) collective-permute-start(bf16[384,1024]{1,0:T(8,128)(2,1)S(1)} %collective-permute-done.2.refs_2_.refs_4_), channel_id=1, source_target_pairs={{2,0},{4,2},{6,4},{7,6},{5,7},{3,5},{1,3},{0,1},{10,8},{12,10},{14... | collective-permute-start | bytes 2359304 | tf_op jit(solution)/shard_map/ppermute | solution.py:226
  28.4 12.8 %collective-permute-start.8 = (bf16[64,4096]{1,0:T(8,128)(2,1)}, bf16[64,4096]{1,0:T(8,128)(2,1)}, u32[]{:S(2)}, u32[]{:S(2)}) collective-permute-start(bf16[64,4096]{1,0:T(8,128)(2,1)} %get-tuple-element.39), channel_id=1, source_target_pairs={{0,16},{8,24},{16,0},{24,8},{1,17},{9,25},{17,1},{25,9},{2,18},{10... | collective-permute-start | bytes 1572872 | tf_op jit(solution)/shard_map/ppermute | solution.py:229
  31.8 22.9 %collective-permute-start.10 = (bf16[64,1024]{1,0:T(8,128)(2,1)}, bf16[64,1024]{1,0:T(8,128)(2,1)S(1)}, u32[]{:S(2)}, u32[]{:S(2)}) collective-permute-start(bf16[64,1024]{1,0:T(8,128)(2,1)} %copy-done.16), channel_id=1, source_target_pairs={{0,7},{2,5},{4,3},{6,1},{7,0},{5,2},{3,4},{1,6},{8,15},{10,13},{12... | collective-permute-start | bytes 393224 | tf_op jit(solution)/shard_map/ppermute | solution.py:288
  39.3 9.7 %copy-start.8 = (f32[64,4096]{1,0:T(8,128)S(1)}, f32[64,4096]{1,0:T(8,128)}, u32[]{:S(2)}) copy-start(f32[64,4096]{1,0:T(8,128)} %copy-done.7) | copy-start | bytes 3145732
  41.4 20.5 %collective-permute-start.9 = (bf16[384,1024]{1,0:T(8,128)(2,1)S(1)}, bf16[384,1024]{1,0:T(8,128)(2,1)S(1)}, u32[]{:S(2)}, u32[]{:S(2)}) collective-permute-start(bf16[384,1024]{1,0:T(8,128)(2,1)S(1)} %pad_maximum_fusion.1), channel_id=1, source_target_pairs={{0,16},{8,24},{16,0},{24,8},{1,17},{9,25},{17,1},{25,9},{2,18},{10... | collective-permute-start | bytes 2359304 | tf_op jit(solution)/shard_map/ppermute | solution.py:229
  45.1 22.5 %collective-permute-start.5 = (bf16[384,1024]{1,0:T(8,128)(2,1)S(1)}, bf16[384,1024]{1,0:T(8,128)(2,1)S(1)}, u32[]{:S(2)}, u32[]{:S(2)}) collective-permute-start(bf16[384,1024]{1,0:T(8,128)(2,1)S(1)} %collective-permute-done.4.refs_0_), channel_id=1, source_target_pairs={{0,2},{2,4},{4,6},{6,7},{7,5},{5,3},{3,1},{1,0},{8,10},{10,12},{12... | collective-permute-start | bytes 2359304 | tf_op jit(solution)/shard_map/ppermute | solution.py:223
  49.0 18.6 %collective-permute-start.7 = (bf16[384,1024]{1,0:T(8,128)(2,1)}, bf16[384,1024]{1,0:T(8,128)(2,1)S(1)}, u32[]{:S(2)}, u32[]{:S(2)}) collective-permute-start(bf16[384,1024]{1,0:T(8,128)(2,1)} %collective-permute-done.6.refs_1_.refs_2_), channel_id=1, source_target_pairs={{2,0},{4,2},{6,4},{7,6},{5,7},{3,5},{1,3},{0,1},{10,8},{12,10},{14... | collective-permute-start | bytes 2359304 | tf_op jit(solution)/shard_map/ppermute | solution.py:226
  50.2 22.7 %collective-permute-start.15 = (bf16[64,2048]{1,0:T(8,128)(2,1)S(1)}, bf16[64,2048]{1,0:T(8,128)(2,1)S(1)}, u32[]{:S(2)}, u32[]{:S(2)}) collective-permute-start(bf16[64,2048]{1,0:T(8,128)(2,1)S(1)} %dynamic-slice_convert_fusion), channel_id=1, source_target_pairs={{0,1},{1,0},{2,3},{3,2},{4,5},{5,4},{6,7},{7,6},{8,9},{9,8},{10,11... | collective-permute-start | bytes 786440 | tf_op jit(solution)/shard_map/ppermute | solution.py:229
  54.6 7.3 %copy-start.2 = (bf16[384,1024]{1,0:T(8,128)(2,1)S(1)}, bf16[384,1024]{1,0:T(8,128)(2,1)}, u32[]{:S(2)}) copy-start(bf16[384,1024]{1,0:T(8,128)(2,1)} %copy-done.1) | copy-start | bytes 2359300
  54.6 7.3 %copy-start.4 = (bf16[384,1024]{1,0:T(8,128)(2,1)S(1)}, bf16[384,1024]{1,0:T(8,128)(2,1)}, u32[]{:S(2)}) copy-start(bf16[384,1024]{1,0:T(8,128)(2,1)} %copy-done.3) | copy-start | bytes 2359300
  54.7 7.3 %copy-start.6 = (bf16[192,1024]{1,0:T(8,128)(2,1)S(1)}, bf16[192,1024]{1,0:T(8,128)(2,1)}, u32[]{:S(2)}) copy-start(bf16[192,1024]{1,0:T(8,128)(2,1)} %get-tuple-element.77.refs_1_) | copy-start | bytes 1179652
  54.7 24.1 %collective-permute-start.16 = (bf16[384,1024]{1,0:T(8,128)(2,1)S(1)}, bf16[384,1024]{1,0:T(8,128)(2,1)S(1)}, u32[]{:S(2)}, u32[]{:S(2)}) collective-permute-start(bf16[384,1024]{1,0:T(8,128)(2,1)S(1)} %pad_maximum_fusion.2), channel_id=1, source_target_pairs={{0,16},{8,24},{16,0},{24,8},{1,17},{9,25},{17,1},{25,9},{2,18},{10... | collective-permute-start | bytes 2359304 | tf_op jit(solution)/shard_map/ppermute | solution.py:229
  68.5 26.3 %collective-permute-start.19 = (bf16[384,1024]{1,0:T(8,128)(2,1)}, bf16[384,1024]{1,0:T(8,128)(2,1)S(1)}, u32[]{:S(2)}, u32[]{:S(2)}) collective-permute-start(bf16[384,1024]{1,0:T(8,128)(2,1)} %get-tuple-element.51), channel_id=1, source_target_pairs={{0,16},{8,24},{16,0},{24,8},{1,17},{9,25},{17,1},{25,9},{2,18},{10... | collective-permute-start | bytes 2359304 | tf_op jit(solution)/shard_map/ppermute | solution.py:229
  72.8 3.5 %collective-permute-start.13 = (f32[512,64]{1,0:T(8,128)S(1)}, f32[512,64]{1,0:T(8,128)S(1)}, u32[]{:S(2)}, u32[]{:S(2)}) collective-permute-start(f32[512,64]{1,0:T(8,128)S(1)} %through_last.1), channel_id=1, source_target_pairs={{0,8},{8,0},{16,24},{24,16},{1,9},{9,1},{17,25},{25,17},{2,10},{10... | collective-permute-start | bytes 393224 | tf_op jit(solution)/shard_map/ppermute | solution.py:229
  72.9 14.7 %collective-permute-start.12 = (bf16[128,1024]{1,0:T(8,128)(2,1)S(1)}, bf16[128,1024]{1,0:T(8,128)(2,1)S(1)}, u32[]{:S(2)}, u32[]{:S(2)}) collective-permute-start(bf16[128,1024]{1,0:T(8,128)(2,1)S(1)} %get-tuple-element.49), channel_id=1, source_target_pairs={{2,0},{4,2},{6,4},{7,6},{5,7},{3,5},{1,3},{0,1},{10,8},{12,10},{14... | collective-permute-start | bytes 786440 | tf_op jit(solution)/shard_map/ppermute | solution.py:226
  75.1 13.3 %collective-permute-start.11 = (bf16[192,1024]{1,0:T(8,128)(2,1)S(1)}, bf16[192,1024]{1,0:T(8,128)(2,1)}, u32[]{:S(2)}, u32[]{:S(2)}) collective-permute-start(bf16[192,1024]{1,0:T(8,128)(2,1)S(1)} %get-tuple-element.48), channel_id=1, source_target_pairs={{0,2},{2,4},{4,6},{6,7},{7,5},{5,3},{3,1},{1,0},{8,10},{10,12},{12... | collective-permute-start | bytes 1179656 | tf_op jit(solution)/shard_map/ppermute | solution.py:223
  75.6 2.7 %copy-start.11 = (f32[64,2048]{1,0:T(8,128)}, f32[64,2048]{1,0:T(8,128)S(1)}, u32[]{:S(2)}) copy-start(f32[64,2048]{1,0:T(8,128)S(1)} %convert_add_fusion.1) | copy-start | bytes 1572868
  76.4 1.9 %copy-start.17 = (bf16[512,64]{1,0:T(8,128)(2,1)}, bf16[512,64]{1,0:T(8,128)(2,1)S(1)}, u32[]{:S(2)}) copy-start(bf16[512,64]{1,0:T(8,128)(2,1)S(1)} %fusion.2) | copy-start | bytes 196612
  76.6 11.0 %collective-permute-start.14 = (f32[64,256]{1,0:T(8,128)S(1)}, f32[64,256]{1,0:T(8,128)S(1)}, u32[]{:S(2)}, u32[]{:S(2)}) collective-permute-start(f32[64,256]{1,0:T(8,128)S(1)} %fusion.3), channel_id=1, source_target_pairs={{0,1},{1,0},{2,3},{3,2},{4,5},{5,4},{6,7},{7,6},{8,9},{9,8},{10,11... | collective-permute-start | bytes 196616 | tf_op jit(solution)/shard_map/ppermute | solution.py:229
  82.9 1.0 copy-start.5
  87.7 0.7 copy-start.9
  88.4 6.5 %collective-permute-start.18 = (bf16[64,1024]{1,0:T(8,128)(2,1)}, bf16[64,1024]{1,0:T(8,128)(2,1)S(1)}, u32[]{:S(2)}, u32[]{:S(2)}) collective-permute-start(bf16[64,1024]{1,0:T(8,128)(2,1)} %dynamic-slice_convert_fusion.1), channel_id=1, source_target_pairs={{0,2},{1,3},{2,0},{3,1},{4,6},{5,7},{6,4},{7,5},{8,10},{9,11},{10,... | collective-permute-start | bytes 393224 | tf_op jit(solution)/shard_map/ppermute | solution.py:229
  88.4 6.4 %collective-permute-start.17 = (f32[64,256]{1,0:T(8,128)S(1)}, f32[64,256]{1,0:T(8,128)S(1)}, u32[]{:S(2)}, u32[]{:S(2)}) collective-permute-start(f32[64,256]{1,0:T(8,128)S(1)} %add.93), channel_id=1, source_target_pairs={{0,2},{1,3},{2,0},{3,1},{4,6},{5,7},{6,4},{7,5},{8,10},{9,11},{10,... | collective-permute-start | bytes 196616 | tf_op jit(solution)/shard_map/ppermute | solution.py:229
  90.4 13.2 %collective-permute-start.22 = (bf16[192,1024]{1,0:T(8,128)(2,1)}, bf16[192,1024]{1,0:T(8,128)(2,1)S(1)}, u32[]{:S(2)}, u32[]{:S(2)}) collective-permute-start(bf16[192,1024]{1,0:T(8,128)(2,1)} %collective-permute-done.11.refs_0_), channel_id=1, source_target_pairs={{0,16},{8,24},{16,0},{24,8},{1,17},{9,25},{17,1},{25,9},{2,18},{10... | collective-permute-start | bytes 1179656 | tf_op jit(solution)/shard_map/ppermute | solution.py:229
  95.9 7.8 %copy-start.10 = (bf16[128,1024]{1,0:T(8,128)(2,1)S(1)}, bf16[128,1024]{1,0:T(8,128)(2,1)}, u32[]{:S(2)}) copy-start(bf16[128,1024]{1,0:T(8,128)(2,1)} %copy-done.9) | copy-start | bytes 786436
  95.9 7.7 %collective-permute-start.21 = (bf16[64,512]{1,0:T(8,128)(2,1)S(1)}, bf16[64,512]{1,0:T(8,128)(2,1)S(1)}, u32[]{:S(2)}, u32[]{:S(2)}) collective-permute-start(bf16[64,512]{1,0:T(8,128)(2,1)S(1)} %dynamic-slice_convert_fusion.2), channel_id=1, source_target_pairs={{0,4},{1,5},{2,6},{3,7},{4,0},{5,1},{6,2},{7,3},{8,12},{9,13},{10,... | collective-permute-start | bytes 196616 | tf_op jit(solution)/shard_map/ppermute | solution.py:229
  98.4 5.2 %collective-permute-start.20 = (f32[64,256]{1,0:T(8,128)S(1)}, f32[64,256]{1,0:T(8,128)S(1)}, u32[]{:S(2)}, u32[]{:S(2)}) collective-permute-start(f32[64,256]{1,0:T(8,128)S(1)} %add.99), channel_id=1, source_target_pairs={{0,4},{1,5},{2,6},{3,7},{4,0},{5,1},{6,2},{7,3},{8,12},{9,13},{10,... | collective-permute-start | bytes 196616 | tf_op jit(solution)/shard_map/ppermute | solution.py:229
  106.3 7.8 %collective-permute-start.24 = (f32[256,512]{1,0:T(8,128)S(1)}, f32[256,512]{1,0:T(8,128)S(1)}, u32[]{:S(2)}, u32[]{:S(2)}) collective-permute-start(f32[256,512]{1,0:T(8,128)S(1)} %slice.76), channel_id=1, source_target_pairs={{0,8},{8,0},{16,24},{24,16},{1,9},{9,1},{17,25},{25,17},{2,10},{10... | collective-permute-start | bytes 1572872 | tf_op jit(solution)/shard_map/ppermute | solution.py:229
  106.4 7.7 %collective-permute-start.23 = (f32[64,768]{1,0:T(8,128)S(1)}, f32[64,768]{1,0:T(8,128)S(1)}, u32[]{:S(2)}, u32[]{:S(2)}) collective-permute-start(f32[64,768]{1,0:T(8,128)S(1)} %pad_maximum_fusion.4), channel_id=1, source_target_pairs={{0,16},{8,24},{16,0},{24,8},{1,17},{9,25},{17,1},{25,9},{2,18},{10... | collective-permute-start | bytes 589832 | tf_op jit(solution)/shard_map/ppermute | solution.py:229
  114.1 0.9 copy-start.18
  114.3 1.7 %collective-permute-start.25 = (f32[64,1280]{1,0:T(8,128)S(1)}, f32[64,1280]{1,0:T(8,128)S(1)}, u32[]{:S(2)}, u32[]{:S(2)}) collective-permute-start(f32[64,1280]{1,0:T(8,128)S(1)} %pad_maximum_fusion.3.mine), channel_id=1, source_target_pairs={{0,8},{8,0},{16,24},{24,16},{1,9},{9,1},{17,25},{25,17},{2,10},{10... | collective-permute-start | bytes 983048 | tf_op jit(solution)/shard_map/ppermute | solution.py:229

commit v2 on v1

--- a/solution.py
+++ b/solution.py
@@ -389,7 +389,7 @@
             (gifts[half], given, 0, range(given)),
         ]
         done = product(2 * half - 3, [last], done, "last")
-        others, swapped = together(others, over(done[tokens:], "dp", 1))
+        others, done = together(others, done)
         other_b, total_a = others[:, : part // 2], total_a + others[:, part // 2 :]
         low_x, high_x = jnp.where(x == 0, total_b, other_b), jnp.where(x == 0, other_b, total_b)
         ends = jnp.concatenate([low_x, high_x, total_a], axis=1)
@@ -398,7 +398,7 @@
         grad_b, grad_a = finish(info, ends, other_ends, factor.reshape(1), part)
         grad_a = grad_a.T
 
-        frozen = done[:tokens] + swapped
+        frozen = done[:tokens] + over(done[tokens:], "dp", 1)
         begin, middle, end = frozen[:, :given], frozen[:, given:ring], frozen[:, ring:]
         frozen = jnp.concatenate(
             [jnp.where(x == 0, begin, end), middle, jnp.where(x == 0, end, begin)], axis=1

time: 118 us -> 116 us (0.983)
  waiting for transfers between devices: 29.8 us -> 27.1 us
    ppermute x17, waiting for transfers between devices: 24.9 us -> 22.2 us  [over(): lax.ppermute(a, axis, [(i, i ^ bit) for i in range(mesh.shape[axis])])]
  transfers between devices with their start and end apart: 26 -> 26, of which waited for: 11 -> 12; matrix products, arithmetic and copies ran while one was open for 9% -> 9% of each run, Pallas kernels for 29% -> 33%
where the time goes in v2:
time: 116 us; the launch traced here: 115 us
  Pallas kernels  37.5 us (32%)
  starting transfers between devices  35 us (30%)
  waiting for transfers between devices  27.1 us (23%)
  local copies, waits for them, and re-layouts  8.7 us (7%)
  other arithmetic  4.24 us (4%)
  matrix products  1.52 us (1%)
    pallas_call x7, Pallas kernels, products(): pl.pallas_call(body, grid_spec=pltpu.PrefetchScalarGridSpec(num_scalar_pr...  27 us
    ppermute x17, waiting for transfers between devices, over(): lax.ppermute(a, axis, [(i, i ^ bit) for i in range(mesh.shape[axis])])  22.2 us
    ppermute x17, starting transfers between devices, over(): lax.ppermute(a, axis, [(i, i ^ bit) for i in range(mesh.shape[axis])])  20.2 us
    pallas_call x1, Pallas kernels, terms_b(): pl.pallas_call(body, grid_spec=pltpu.PrefetchScalarGridSpec(num_scalar_pr...  8.17 us
    ppermute x4, starting transfers between devices, backward(): lax.ppermute(a, 'fsdp', [(order[(i + 1) % n], order[i]) for i in range(n)])  6.36 us
    ppermute x4, starting transfers between devices, forward(): lax.ppermute(a, 'fsdp', [(order[i], order[(i + 1) % n]) for i in range(n)])  4.9 us
    ppermute x1, starting transfers between devices, shards(): lax.ppermute(together(my_up, chunks[1])[0], 'fsdp', [(order[i], order[(i...  3.61 us
    ppermute x4, waiting for transfers between devices, forward(): lax.ppermute(a, 'fsdp', [(order[i], order[(i + 1) % n]) for i in range(n)])  3.54 us
  transfers between devices with their start and end apart: 26, of which 12 were waited for; matrix products, arithmetic and copies ran while one was open for 9% of the time, Pallas kernels for 33%

profile of v2, /device:TPU:0, one launch (start us, length us, event | category | flops | bytes accessed | tf_op | source)
XLA Modules:
  0.0 115.2 jit_solution(5195901680078438286)
XLA Ops:
  0.7 0.5 collective-permute-start.2
  1.2 0.9 constant_dynamic-slice_fusion.2
  2.1 0.6 broadcast_in_dim.7
  2.7 0.6 fusion
  3.4 0.8 broadcast_select_fusion
  4.3 2.6 %collective-permute-start.1 = (bf16[384,1024]{1,0:T(8,128)(2,1)S(1)}, bf16[384,1024]{1,0:T(8,128)(2,1)S(1)}, u32[]{:S(2)}, u32[]{:S(2)}) collective-permute-start(bf16[384,1024]{1,0:T(8,128)(2,1)S(1)} %pad_maximum_fusion.refs_0_), channel_id=1, source_target_pairs={{2,0},{4,2},{6,4},{7,6},{5,7},{3,5},{1,3},{0,1},{10,8},{12,10},{14... | collective-permute-start | bytes 2359304 | tf_op jit(solution)/shard_map/ppermute | solution.py:226
  6.9 0.1 collective-permute-start
  7.2 0.2 convolution_convert_fusion.1.low
  7.4 7.0 %collective-permute-done.3 = bf16[256,512]{1,0:T(8,128)(2,1)S(1)} collective-permute-done((bf16[256,512]{1,0:T(8,128)(2,1)S(1)}, bf16[256,512]{1,0:T(8,128)(2,1)S(1)}, u32[]{:S(2)}, u32[]{:S(2)}) %collective-permute-start.3) | collective-permute-done | bytes 262176 | tf_op jit(solution)/shard_map/ppermute | solution.py:229
  14.3 0.2 convolution_convert_fusion.low_partner
  14.5 8.2 %terms_b.1 = (f32[64,4096]{1,0:T(8,128)S(1)}, bf16[64,4096]{1,0:T(8,128)(2,1)}) custom-call(s32[18]{0:T(128)S(1)} %pad_add_fusion.info, bf16[256,16384]{1,0:T(8,128)(2,1)} %mine.15, bf16[256,16384]{1,0:T(8,128)(2,1)} %collective-permute-done.2.partner, bf16[64,256]{1,0:T(8,128)(2,1)S(1)} %convolution_convert_fusion.1.low, ...), custom_call_target="tpu_custom_call" | custom-call | flops 536870912 | bytes 8388608 | tf_op jit(solution)/shard_map/terms_b/pallas_call | solution.py:92
  22.7 1.0 copy-done.7
  23.7 1.3 %collective-permute-done.1.refs_2_.refs_4_ = bf16[384,1024]{1,0:T(8,128)(2,1)S(1)} collective-permute-done((bf16[384,1024]{1,0:T(8,128)(2,1)S(1)}, bf16[384,1024]{1,0:T(8,128)(2,1)S(1)}, u32[]{:S(2)}, u32[]{:S(2)}) %collective-permute-start.1) | collective-permute-done | bytes 786464 | tf_op jit(solution)/shard_map/ppermute | solution.py:226
  25.0 1.4 %collective-permute-done.refs_1_.refs_2_ = bf16[384,1024]{1,0:T(8,128)(2,1)S(1)} collective-permute-done((bf16[384,1024]{1,0:T(8,128)(2,1)S(1)}, bf16[384,1024]{1,0:T(8,128)(2,1)S(1)}, u32[]{:S(2)}, u32[]{:S(2)}) %collective-permute-start) | collective-permute-done | bytes 786464 | tf_op jit(solution)/shard_map/ppermute | solution.py:223
  26.4 0.4 collective-permute-start.4
  26.8 1.6 %collective-permute-start.6 = (bf16[384,1024]{1,0:T(8,128)(2,1)S(1)}, bf16[384,1024]{1,0:T(8,128)(2,1)}, u32[]{:S(2)}, u32[]{:S(2)}) collective-permute-start(bf16[384,1024]{1,0:T(8,128)(2,1)S(1)} %collective-permute-done.1.refs_2_.refs_4_), channel_id=1, source_target_pairs={{2,0},{4,2},{6,4},{7,6},{5,7},{3,5},{1,3},{0,1},{10,8},{12,10},{14... | collective-permute-start | bytes 2359304 | tf_op jit(solution)/shard_map/ppermute | solution.py:226
  28.4 1.5 %collective-permute-start.8 = (bf16[64,4096]{1,0:T(8,128)(2,1)}, bf16[64,4096]{1,0:T(8,128)(2,1)}, u32[]{:S(2)}, u32[]{:S(2)}) collective-permute-start(bf16[64,4096]{1,0:T(8,128)(2,1)} %get-tuple-element.39), channel_id=1, source_target_pairs={{0,16},{8,24},{16,0},{24,8},{1,17},{9,25},{17,1},{25,9},{2,18},{10... | collective-permute-start | bytes 1572872 | tf_op jit(solution)/shard_map/ppermute | solution.py:229
  29.9 0.9 constant_dynamic-slice_fusion.1
  30.8 0.9 constant_dynamic-slice_fusion
  31.8 3.6 %collective-permute-start.10 = (bf16[64,1024]{1,0:T(8,128)(2,1)}, bf16[64,1024]{1,0:T(8,128)(2,1)S(1)}, u32[]{:S(2)}, u32[]{:S(2)}) collective-permute-start(bf16[64,1024]{1,0:T(8,128)(2,1)} %copy-done.16), channel_id=1, source_target_pairs={{0,7},{2,5},{4,3},{6,1},{7,0},{5,2},{3,4},{1,6},{8,15},{10,13},{12... | collective-permute-start | bytes 393224 | tf_op jit(solution)/shard_map/ppermute | solution.py:288
  35.4 3.9 %through_first.1.refs_3_ = f32[512,64]{1,0:T(8,128)S(1)} custom-call(s32[18]{0:T(128)S(1)} %pad_add_fusion.info, bf16[256,16384]{1,0:T(8,128)(2,1)} %mine.15, bf16[256,16384]{1,0:T(8,128)(2,1)} %collective-permute-done.2.partner, bf16[384,1024]{1,0:T(8,128)(2,1)S(1)} %pad_maximum_fusion.refs_0_, bf16[384,1024]{1,0:T(8,128)(2,1)S(1)} %collective-permute-done.refs_1_.refs_2_, ...), custom_call_target="tpu_custom_call" | custom-call | flops 201326592 | bytes 3670016 | tf_op jit(solution)/shard_map/through_first/pallas_call | solution.py:151
  39.3 1.9 %collective-permute-done.8 = bf16[64,4096]{1,0:T(8,128)(2,1)} collective-permute-done((bf16[64,4096]{1,0:T(8,128)(2,1)}, bf16[64,4096]{1,0:T(8,128)(2,1)}, u32[]{:S(2)}, u32[]{:S(2)}) %collective-permute-start.8) | collective-permute-done | bytes 524320 | tf_op jit(solution)/shard_map/ppermute | solution.py:229
  41.4 1.6 %collective-permute-start.9 = (bf16[384,1024]{1,0:T(8,128)(2,1)S(1)}, bf16[384,1024]{1,0:T(8,128)(2,1)S(1)}, u32[]{:S(2)}, u32[]{:S(2)}) collective-permute-start(bf16[384,1024]{1,0:T(8,128)(2,1)S(1)} %pad_maximum_fusion.1), channel_id=1, source_target_pairs={{0,16},{8,24},{16,0},{24,8},{1,17},{9,25},{17,1},{25,9},{2,18},{10... | collective-permute-start | bytes 2359304 | tf_op jit(solution)/shard_map/ppermute | solution.py:229
  42.9 2.1 %collective-permute-done.4.refs_0_ = bf16[384,1024]{1,0:T(8,128)(2,1)S(1)} collective-permute-done((bf16[384,1024]{1,0:T(8,128)(2,1)S(1)}, bf16[384,1024]{1,0:T(8,128)(2,1)S(1)}, u32[]{:S(2)}, u32[]{:S(2)}) %collective-permute-start.4) | collective-permute-done | bytes 786464 | tf_op jit(solution)/shard_map/ppermute | solution.py:223
  45.1 3.9 %collective-permute-start.5 = (bf16[384,1024]{1,0:T(8,128)(2,1)S(1)}, bf16[384,1024]{1,0:T(8,128)(2,1)S(1)}, u32[]{:S(2)}, u32[]{:S(2)}) collective-permute-start(bf16[384,1024]{1,0:T(8,128)(2,1)S(1)} %collective-permute-done.4.refs_0_), channel_id=1, source_target_pairs={{0,2},{2,4},{4,6},{6,7},{7,5},{5,3},{3,1},{1,0},{8,10},{10,12},{12... | collective-permute-start | bytes 2359304 | tf_op jit(solution)/shard_map/ppermute | solution.py:223
  49.0 1.2 %convert_add_fusion = f32[64,4096]{1,0:T(8,128)S(1)} fusion(f32[64,4096]{1,0:T(8,128)S(1)} %copy-done.8, bf16[64,4096]{1,0:T(8,128)(2,1)} %collective-permute-done.8), kind=kLoop, calls=%fused_computation.4 | loop fusion | flops 524288 | bytes 2621440 | tf_op jit(solution)/shard_map/add | solution.py:324
  50.2 3.3 %collective-permute-start.15 = (bf16[64,2048]{1,0:T(8,128)(2,1)S(1)}, bf16[64,2048]{1,0:T(8,128)(2,1)S(1)}, u32[]{:S(2)}, u32[]{:S(2)}) collective-permute-start(bf16[64,2048]{1,0:T(8,128)(2,1)S(1)} %dynamic-slice_convert_fusion), channel_id=1, source_target_pairs={{0,1},{1,0},{2,3},{3,2},{4,5},{5,4},{6,7},{7,6},{8,9},{9,8},{10,11... | collective-permute-start | bytes 786440 | tf_op jit(solution)/shard_map/ppermute | solution.py:229
  53.5 1.0 slice.74
  54.7 1.6 %collective-permute-start.16 = (bf16[384,1024]{1,0:T(8,128)(2,1)S(1)}, bf16[384,1024]{1,0:T(8,128)(2,1)S(1)}, u32[]{:S(2)}, u32[]{:S(2)}) collective-permute-start(bf16[384,1024]{1,0:T(8,128)(2,1)S(1)} %pad_maximum_fusion.2), channel_id=1, source_target_pairs={{0,16},{8,24},{16,0},{24,8},{1,17},{9,25},{17,1},{25,9},{2,18},{10... | collective-permute-start | bytes 2359304 | tf_op jit(solution)/shard_map/ppermute | solution.py:229
  56.2 3.9 %through_second.1.refs_2_ = f32[512,64]{1,0:T(8,128)S(1)} custom-call(s32[18]{0:T(128)S(1)} %pad_add_fusion.info, bf16[256,16384]{1,0:T(8,128)(2,1)} %mine.15, bf16[256,16384]{1,0:T(8,128)(2,1)} %collective-permute-done.2.partner, bf16[384,1024]{1,0:T(8,128)(2,1)S(1)} %collective-permute-done.4.refs_0_, ...), custom_call_target="tpu_custom_call" | custom-call | flops 201326592 | bytes 3670016 | tf_op jit(solution)/shard_map/through_second/pallas_call | solution.py:151
  60.2 1.7 %collective-permute-done.9.refs_3_.refs_5_ = bf16[384,1024]{1,0:T(8,128)(2,1)S(1)} collective-permute-done((bf16[384,1024]{1,0:T(8,128)(2,1)S(1)}, bf16[384,1024]{1,0:T(8,128)(2,1)S(1)}, u32[]{:S(2)}, u32[]{:S(2)}) %collective-permute-start.9) | collective-permute-done | bytes 786464 | tf_op jit(solution)/shard_map/ppermute | solution.py:229
  61.9 5.7 %first.1.refs_4_ = f32[512,512]{1,0:T(8,128)} custom-call(s32[18]{0:T(128)S(1)} %pad_add_fusion.info, bf16[256,16384]{1,0:T(8,128)(2,1)} %mine.15, bf16[256,16384]{1,0:T(8,128)(2,1)} %collective-permute-done.2.partner, bf16[384,1024]{1,0:T(8,128)(2,1)S(1)} %pad_maximum_fusion.refs_0_, bf16[192,1024]{1,0:T(8,128)(2,1)S(1)} %copy-done.6, ...), custom_call_target="tpu_custom_call" | custom-call | flops 1610612736 | bytes 7340032 | tf_op jit(solution)/shard_map/first/pallas_call | solution.py:151
  67.6 0.9 assemble.1
  68.5 1.6 %collective-permute-start.19 = (bf16[384,1024]{1,0:T(8,128)(2,1)}, bf16[384,1024]{1,0:T(8,128)(2,1)S(1)}, u32[]{:S(2)}, u32[]{:S(2)}) collective-permute-start(bf16[384,1024]{1,0:T(8,128)(2,1)} %get-tuple-element.51), channel_id=1, source_target_pairs={{0,16},{8,24},{16,0},{24,8},{1,17},{9,25},{17,1},{25,9},{2,18},{10... | collective-permute-start | bytes 2359304 | tf_op jit(solution)/shard_map/ppermute | solution.py:229
  70.1 2.7 %through_last.1 = f32[512,64]{1,0:T(8,128)S(1)} custom-call(s32[18]{0:T(128)S(1)} %pad_add_fusion.info, bf16[256,16384]{1,0:T(8,128)(2,1)} %mine.15, bf16[256,16384]{1,0:T(8,128)(2,1)} %collective-permute-done.2.partner, bf16[384,1024]{1,0:T(8,128)(2,1)S(1)} %collective-permute-done.5.refs_0_.refs_2_, ...), custom_call_target="tpu_custom_call" | custom-call | flops 134217728 | bytes 2490368 | tf_op jit(solution)/shard_map/through_last/pallas_call | solution.py:151
  72.9 2.1 %collective-permute-start.12 = (bf16[128,1024]{1,0:T(8,128)(2,1)S(1)}, bf16[128,1024]{1,0:T(8,128)(2,1)S(1)}, u32[]{:S(2)}, u32[]{:S(2)}) collective-permute-start(bf16[128,1024]{1,0:T(8,128)(2,1)S(1)} %get-tuple-element.49), channel_id=1, source_target_pairs={{2,0},{4,2},{6,4},{7,6},{5,7},{3,5},{1,3},{0,1},{10,8},{12,10},{14... | collective-permute-start | bytes 786440 | tf_op jit(solution)/shard_map/ppermute | solution.py:226
  75.1 0.4 collective-permute-start.11
  75.6 0.7 dynamic-slice_convert_fusion.1
  76.4 0.2 fusion.3
  76.6 1.6 %collective-permute-start.14 = (f32[64,256]{1,0:T(8,128)S(1)}, f32[64,256]{1,0:T(8,128)S(1)}, u32[]{:S(2)}, u32[]{:S(2)}) collective-permute-start(f32[64,256]{1,0:T(8,128)S(1)} %fusion.3), channel_id=1, source_target_pairs={{0,1},{1,0},{2,3},{3,2},{4,5},{5,4},{6,7},{7,6},{8,9},{9,8},{10,11... | collective-permute-start | bytes 196616 | tf_op jit(solution)/shard_map/ppermute | solution.py:229
  78.2 0.5 collective-permute-done.16.refs_1_.refs_3_
  78.8 4.2 %middle.1.refs_4_ = f32[512,512]{1,0:T(8,128)S(1)} custom-call(s32[18]{0:T(128)S(1)} %pad_add_fusion.info, bf16[256,16384]{1,0:T(8,128)(2,1)} %mine.15, bf16[256,16384]{1,0:T(8,128)(2,1)} %collective-permute-done.2.partner, bf16[384,1024]{1,0:T(8,128)(2,1)S(1)} %collective-permute-done.4.refs_0_, ...), custom_call_target="tpu_custom_call" | custom-call | flops 1073741824 | bytes 5242880 | tf_op jit(solution)/shard_map/middle/pallas_call | solution.py:151
  83.0 1.0 copy-done.5
  83.9 3.7 %collective-permute-done.14 = f32[64,256]{1,0:T(8,128)S(1)} collective-permute-done((f32[64,256]{1,0:T(8,128)S(1)}, f32[64,256]{1,0:T(8,128)S(1)}, u32[]{:S(2)}, u32[]{:S(2)}) %collective-permute-start.14) | collective-permute-done | bytes 65568 | tf_op jit(solution)/shard_map/ppermute | solution.py:229
  87.7 0.7 copy-done.9
  88.4 2.0 %collective-permute-start.17 = (f32[64,256]{1,0:T(8,128)S(1)}, f32[64,256]{1,0:T(8,128)S(1)}, u32[]{:S(2)}, u32[]{:S(2)}) collective-permute-start(f32[64,256]{1,0:T(8,128)S(1)} %add.93), channel_id=1, source_target_pairs={{0,2},{1,3},{2,0},{3,1},{4,6},{5,7},{6,4},{7,5},{8,10},{9,11},{10,... | collective-permute-start | bytes 196616 | tf_op jit(solution)/shard_map/ppermute | solution.py:229
  90.4 0.6 collective-permute-start.22
  91.0 3.8 %collective-permute-done.17 = f32[64,256]{1,0:T(8,128)S(1)} collective-permute-done((f32[64,256]{1,0:T(8,128)S(1)}, f32[64,256]{1,0:T(8,128)S(1)}, u32[]{:S(2)}, u32[]{:S(2)}) %collective-permute-start.17) | collective-permute-done | bytes 65568 | tf_op jit(solution)/shard_map/ppermute | solution.py:229
  94.8 1.0 convert_add_fusion.2
  95.9 2.5 %collective-permute-start.21 = (bf16[64,512]{1,0:T(8,128)(2,1)S(1)}, bf16[64,512]{1,0:T(8,128)(2,1)S(1)}, u32[]{:S(2)}, u32[]{:S(2)}) collective-permute-start(bf16[64,512]{1,0:T(8,128)(2,1)S(1)} %dynamic-slice_convert_fusion.2), channel_id=1, source_target_pairs={{0,4},{1,5},{2,6},{3,7},{4,0},{5,1},{6,2},{7,3},{8,12},{9,13},{10,... | collective-permute-start | bytes 196616 | tf_op jit(solution)/shard_map/ppermute | solution.py:229
  98.4 0.5 collective-permute-start.20
  98.9 4.0 %late.1.refs_3_ = f32[512,512]{1,0:T(8,128)S(1)} custom-call(s32[18]{0:T(128)S(1)} %pad_add_fusion.info, bf16[256,16384]{1,0:T(8,128)(2,1)} %mine.15, bf16[256,16384]{1,0:T(8,128)(2,1)} %collective-permute-done.2.partner, bf16[384,1024]{1,0:T(8,128)(2,1)S(1)} %collective-permute-done.5.refs_0_.refs_2_, ...), custom_call_target="tpu_custom_call" | custom-call | flops 1073741824 | bytes 5242880 | tf_op jit(solution)/shard_map/late/pallas_call | solution.py:151
  102.8 0.7 collective-permute-done.20
  103.6 2.1 %collective-permute-start.23 = (f32[64,768]{1,0:T(8,128)S(1)}, f32[64,768]{1,0:T(8,128)S(1)}, u32[]{:S(2)}, u32[]{:S(2)}) collective-permute-start(f32[64,768]{1,0:T(8,128)S(1)} %pad_maximum_fusion.4), channel_id=1, source_target_pairs={{0,16},{8,24},{16,0},{24,8},{1,17},{9,25},{17,1},{25,9},{2,18},{10... | collective-permute-start | bytes 589832 | tf_op jit(solution)/shard_map/ppermute | solution.py:229
  105.8 2.6 %last.1 = f32[512,512]{1,0:T(8,128)S(1)} custom-call(s32[18]{0:T(128)S(1)} %pad_add_fusion.info, bf16[256,16384]{1,0:T(8,128)(2,1)} %mine.15, bf16[256,16384]{1,0:T(8,128)(2,1)} %collective-permute-done.2.partner, bf16[192,1024]{1,0:T(8,128)(2,1)} %collective-permute-done.11.refs_0_, bf16[128,1024]{1,0:T(8,128)(2,1)S(1)} %copy-done.10, ...), custom_call_target="tpu_custom_call" | custom-call | flops 536870912 | bytes 3145728 | tf_op jit(solution)/shard_map/last/pallas_call | solution.py:151
  108.4 1.0 collective-permute-done.23
  109.6 0.6 collective-permute-start.25
  110.2 1.8 %collective-permute-done.25.other = f32[64,1280]{1,0:T(8,128)S(1)} collective-permute-done((f32[64,1280]{1,0:T(8,128)S(1)}, f32[64,1280]{1,0:T(8,128)S(1)}, u32[]{:S(2)}, u32[]{:S(2)}) %collective-permute-start.25) | collective-permute-done | bytes 327712 | tf_op jit(solution)/shard_map/ppermute | solution.py:229
  112.0 1.4 %finish.1 = (f32[64,2048]{1,0:T(8,128)}, f32[64,512]{1,0:T(8,128)}) custom-call(s32[18]{0:T(128)S(1)} %pad_add_fusion.info, f32[1]{0:T(128)} %constant.69.clone.1.factor, f32[64,1280]{1,0:T(8,128)S(1)} %pad_maximum_fusion.3.mine, f32[64,1280]{1,0:T(8,128)S(1)} %collective-permute-done.25.other), custom_call_target="tpu_custom_call" | custom-call | bytes 1310720 | tf_op jit(solution)/shard_map/finish/pallas_call | solution.py:194
  113.4 0.1 slice_add_fusion
  113.5 0.1 slice.77
  113.6 0.1 slice_select_fusion.1
  113.7 0.6 copy-done.18
  114.3 0.9 fusion.1
  (80 shorter events, 1.0 us)
Async XLA Ops:
  0.6 2.7 %copy-start = (bf16[64,2048]{1,0:T(8,128)(2,1)S(1)}, bf16[64,2048]{1,0:T(8,128)(2,1)}, u32[]{:S(2)}) copy-start(bf16[64,2048]{1,0:T(8,128)(2,1)} %param.12) | copy-start | bytes 786436
  0.6 2.1 %copy-start.15 = (bf16[512,2048]{1,0:T(8,128)(2,1)S(1)}, bf16[512,2048]{1,0:T(8,128)(2,1)}, u32[]{:S(2)}) copy-start(bf16[512,2048]{1,0:T(8,128)(2,1)} %param.9) | copy-start | bytes 6291460
  0.7 13.9 %collective-permute-start.2 = (bf16[256,16384]{1,0:T(8,128)(2,1)}, bf16[256,16384]{1,0:T(8,128)(2,1)}, u32[]{:S(2)}, u32[]{:S(2)}) collective-permute-start(bf16[256,16384]{1,0:T(8,128)(2,1)} %mine.15), channel_id=1, source_target_pairs={{0,8},{8,0},{16,24},{24,16},{1,9},{9,1},{17,25},{25,17},{2,10},{10... | collective-permute-start | bytes 25165832 | tf_op jit(solution)/shard_map/ppermute | solution.py:229
  3.4 0.9 copy-start.16
  3.4 3.7 %copy-start.12 = (bf16[256,512]{1,0:T(8,128)(2,1)S(1)}, bf16[256,512]{1,0:T(8,128)(2,1)}, u32[]{:S(2)}) copy-start(bf16[256,512]{1,0:T(8,128)(2,1)} %param.7) | copy-start | bytes 786436
  3.4 3.7 %copy-start.19 = (s32[8]{0:T(128)S(1)}, s32[8]{0:T(128)}, u32[]{:S(2)}) copy-start(s32[8]{0:T(128)} %constant.70.clone) | copy-start | bytes 100
  3.4 3.8 %copy-start.14 = (bf16[512,64]{0,1:T(8,128)(2,1)S(1)}, bf16[512,64]{0,1:T(8,128)(2,1)}, u32[]{:S(2)}) copy-start(bf16[512,64]{0,1:T(8,128)(2,1)} %param.11) | copy-start | bytes 196612
  4.3 20.7 %collective-permute-start.1 = (bf16[384,1024]{1,0:T(8,128)(2,1)S(1)}, bf16[384,1024]{1,0:T(8,128)(2,1)S(1)}, u32[]{:S(2)}, u32[]{:S(2)}) collective-permute-start(bf16[384,1024]{1,0:T(8,128)(2,1)S(1)} %pad_maximum_fusion.refs_0_), channel_id=1, source_target_pairs={{2,0},{4,2},{6,4},{7,6},{5,7},{3,5},{1,3},{0,1},{10,8},{12,10},{14... | collective-permute-start | bytes 2359304 | tf_op jit(solution)/shard_map/ppermute | solution.py:226
  6.9 19.5 %collective-permute-start = (bf16[384,1024]{1,0:T(8,128)(2,1)S(1)}, bf16[384,1024]{1,0:T(8,128)(2,1)S(1)}, u32[]{:S(2)}, u32[]{:S(2)}) collective-permute-start(bf16[384,1024]{1,0:T(8,128)(2,1)S(1)} %pad_maximum_fusion.refs_0_), channel_id=1, source_target_pairs={{0,2},{2,4},{4,6},{6,7},{7,5},{5,3},{3,1},{1,0},{8,10},{10,12},{12... | collective-permute-start | bytes 2359304 | tf_op jit(solution)/shard_map/ppermute | solution.py:223
  7.0 7.3 %collective-permute-start.3 = (bf16[256,512]{1,0:T(8,128)(2,1)S(1)}, bf16[256,512]{1,0:T(8,128)(2,1)S(1)}, u32[]{:S(2)}, u32[]{:S(2)}) collective-permute-start(bf16[256,512]{1,0:T(8,128)(2,1)S(1)} %copy-done.12), channel_id=1, source_target_pairs={{0,8},{8,0},{16,24},{24,16},{1,9},{9,1},{17,25},{25,17},{2,10},{10... | collective-permute-start | bytes 786440 | tf_op jit(solution)/shard_map/ppermute | solution.py:229
  14.3 8.4 %copy-start.13 = (bf16[256,512]{1,0:T(8,128)(2,1)}, bf16[256,512]{1,0:T(8,128)(2,1)S(1)}, u32[]{:S(2)}) copy-start(bf16[256,512]{1,0:T(8,128)(2,1)S(1)} %collective-permute-done.3) | copy-start | bytes 786436
  22.7 1.0 copy-start.7
  25.0 16.3 %copy-start.1 = (bf16[384,1024]{1,0:T(8,128)(2,1)}, bf16[384,1024]{1,0:T(8,128)(2,1)S(1)}, u32[]{:S(2)}) copy-start(bf16[384,1024]{1,0:T(8,128)(2,1)S(1)} %collective-permute-done.1.refs_2_.refs_4_) | copy-start | bytes 2359300
  26.4 14.8 %copy-start.3 = (bf16[384,1024]{1,0:T(8,128)(2,1)}, bf16[384,1024]{1,0:T(8,128)(2,1)S(1)}, u32[]{:S(2)}) copy-start(bf16[384,1024]{1,0:T(8,128)(2,1)S(1)} %collective-permute-done.refs_1_.refs_2_) | copy-start | bytes 2359300
  26.4 18.7 %collective-permute-start.4 = (bf16[384,1024]{1,0:T(8,128)(2,1)S(1)}, bf16[384,1024]{1,0:T(8,128)(2,1)S(1)}, u32[]{:S(2)}, u32[]{:S(2)}) collective-permute-start(bf16[384,1024]{1,0:T(8,128)(2,1)S(1)} %collective-permute-done.refs_1_.refs_2_), channel_id=1, source_target_pairs={{0,2},{2,4},{4,6},{6,7},{7,5},{5,3},{3,1},{1,0},{8,10},{10,12},{12... | collective-permute-start | bytes 2359304 | tf_op jit(solution)/shard_map/ppermute | solution.py:223
  26.8 22.2 %collective-permute-start.6 = (bf16[384,1024]{1,0:T(8,128)(2,1)S(1)}, bf16[384,1024]{1,0:T(8,128)(2,1)}, u32[]{:S(2)}, u32[]{:S(2)}) collective-permute-start(bf16[384,1024]{1,0:T(8,128)(2,1)S(1)} %collective-permute-done.1.refs_2_.refs_4_), channel_id=1, source_target_pairs={{2,0},{4,2},{6,4},{7,6},{5,7},{3,5},{1,3},{0,1},{10,8},{12,10},{14... | collective-permute-start | bytes 2359304 | tf_op jit(solution)/shard_map/ppermute | solution.py:226
  28.4 12.8 %collective-permute-start.8 = (bf16[64,4096]{1,0:T(8,128)(2,1)}, bf16[64,4096]{1,0:T(8,128)(2,1)}, u32[]{:S(2)}, u32[]{:S(2)}) collective-permute-start(bf16[64,4096]{1,0:T(8,128)(2,1)} %get-tuple-element.39), channel_id=1, source_target_pairs={{0,16},{8,24},{16,0},{24,8},{1,17},{9,25},{17,1},{25,9},{2,18},{10... | collective-permute-start | bytes 1572872 | tf_op jit(solution)/shard_map/ppermute | solution.py:229
  31.8 22.9 %collective-permute-start.10 = (bf16[64,1024]{1,0:T(8,128)(2,1)}, bf16[64,1024]{1,0:T(8,128)(2,1)S(1)}, u32[]{:S(2)}, u32[]{:S(2)}) collective-permute-start(bf16[64,1024]{1,0:T(8,128)(2,1)} %copy-done.16), channel_id=1, source_target_pairs={{0,7},{2,5},{4,3},{6,1},{7,0},{5,2},{3,4},{1,6},{8,15},{10,13},{12... | collective-permute-start | bytes 393224 | tf_op jit(solution)/shard_map/ppermute | solution.py:288
  39.3 9.7 %copy-start.8 = (f32[64,4096]{1,0:T(8,128)S(1)}, f32[64,4096]{1,0:T(8,128)}, u32[]{:S(2)}) copy-start(f32[64,4096]{1,0:T(8,128)} %copy-done.7) | copy-start | bytes 3145732
  41.4 20.5 %collective-permute-start.9 = (bf16[384,1024]{1,0:T(8,128)(2,1)S(1)}, bf16[384,1024]{1,0:T(8,128)(2,1)S(1)}, u32[]{:S(2)}, u32[]{:S(2)}) collective-permute-start(bf16[384,1024]{1,0:T(8,128)(2,1)S(1)} %pad_maximum_fusion.1), channel_id=1, source_target_pairs={{0,16},{8,24},{16,0},{24,8},{1,17},{9,25},{17,1},{25,9},{2,18},{10... | collective-permute-start | bytes 2359304 | tf_op jit(solution)/shard_map/ppermute | solution.py:229
  45.1 22.5 %collective-permute-start.5 = (bf16[384,1024]{1,0:T(8,128)(2,1)S(1)}, bf16[384,1024]{1,0:T(8,128)(2,1)S(1)}, u32[]{:S(2)}, u32[]{:S(2)}) collective-permute-start(bf16[384,1024]{1,0:T(8,128)(2,1)S(1)} %collective-permute-done.4.refs_0_), channel_id=1, source_target_pairs={{0,2},{2,4},{4,6},{6,7},{7,5},{5,3},{3,1},{1,0},{8,10},{10,12},{12... | collective-permute-start | bytes 2359304 | tf_op jit(solution)/shard_map/ppermute | solution.py:223
  49.0 18.6 %collective-permute-start.7 = (bf16[384,1024]{1,0:T(8,128)(2,1)}, bf16[384,1024]{1,0:T(8,128)(2,1)S(1)}, u32[]{:S(2)}, u32[]{:S(2)}) collective-permute-start(bf16[384,1024]{1,0:T(8,128)(2,1)} %collective-permute-done.6.refs_1_.refs_2_), channel_id=1, source_target_pairs={{2,0},{4,2},{6,4},{7,6},{5,7},{3,5},{1,3},{0,1},{10,8},{12,10},{14... | collective-permute-start | bytes 2359304 | tf_op jit(solution)/shard_map/ppermute | solution.py:226
  50.2 22.7 %collective-permute-start.15 = (bf16[64,2048]{1,0:T(8,128)(2,1)S(1)}, bf16[64,2048]{1,0:T(8,128)(2,1)S(1)}, u32[]{:S(2)}, u32[]{:S(2)}) collective-permute-start(bf16[64,2048]{1,0:T(8,128)(2,1)S(1)} %dynamic-slice_convert_fusion), channel_id=1, source_target_pairs={{0,1},{1,0},{2,3},{3,2},{4,5},{5,4},{6,7},{7,6},{8,9},{9,8},{10,11... | collective-permute-start | bytes 786440 | tf_op jit(solution)/shard_map/ppermute | solution.py:229
  54.6 7.3 %copy-start.2 = (bf16[384,1024]{1,0:T(8,128)(2,1)S(1)}, bf16[384,1024]{1,0:T(8,128)(2,1)}, u32[]{:S(2)}) copy-start(bf16[384,1024]{1,0:T(8,128)(2,1)} %copy-done.1) | copy-start | bytes 2359300
  54.6 7.3 %copy-start.4 = (bf16[384,1024]{1,0:T(8,128)(2,1)S(1)}, bf16[384,1024]{1,0:T(8,128)(2,1)}, u32[]{:S(2)}) copy-start(bf16[384,1024]{1,0:T(8,128)(2,1)} %copy-done.3) | copy-start | bytes 2359300
  54.7 7.3 %copy-start.6 = (bf16[192,1024]{1,0:T(8,128)(2,1)S(1)}, bf16[192,1024]{1,0:T(8,128)(2,1)}, u32[]{:S(2)}) copy-start(bf16[192,1024]{1,0:T(8,128)(2,1)} %get-tuple-element.77.refs_1_) | copy-start | bytes 1179652
  54.7 24.1 %collective-permute-start.16 = (bf16[384,1024]{1,0:T(8,128)(2,1)S(1)}, bf16[384,1024]{1,0:T(8,128)(2,1)S(1)}, u32[]{:S(2)}, u32[]{:S(2)}) collective-permute-start(bf16[384,1024]{1,0:T(8,128)(2,1)S(1)} %pad_maximum_fusion.2), channel_id=1, source_target_pairs={{0,16},{8,24},{16,0},{24,8},{1,17},{9,25},{17,1},{25,9},{2,18},{10... | collective-permute-start | bytes 2359304 | tf_op jit(solution)/shard_map/ppermute | solution.py:229
  68.5 26.3 %collective-permute-start.19 = (bf16[384,1024]{1,0:T(8,128)(2,1)}, bf16[384,1024]{1,0:T(8,128)(2,1)S(1)}, u32[]{:S(2)}, u32[]{:S(2)}) collective-permute-start(bf16[384,1024]{1,0:T(8,128)(2,1)} %get-tuple-element.51), channel_id=1, source_target_pairs={{0,16},{8,24},{16,0},{24,8},{1,17},{9,25},{17,1},{25,9},{2,18},{10... | collective-permute-start | bytes 2359304 | tf_op jit(solution)/shard_map/ppermute | solution.py:229
  72.8 3.5 %collective-permute-start.13 = (f32[512,64]{1,0:T(8,128)S(1)}, f32[512,64]{1,0:T(8,128)S(1)}, u32[]{:S(2)}, u32[]{:S(2)}) collective-permute-start(f32[512,64]{1,0:T(8,128)S(1)} %through_last.1), channel_id=1, source_target_pairs={{0,8},{8,0},{16,24},{24,16},{1,9},{9,1},{17,25},{25,17},{2,10},{10... | collective-permute-start | bytes 393224 | tf_op jit(solution)/shard_map/ppermute | solution.py:229
  72.9 14.7 %collective-permute-start.12 = (bf16[128,1024]{1,0:T(8,128)(2,1)S(1)}, bf16[128,1024]{1,0:T(8,128)(2,1)S(1)}, u32[]{:S(2)}, u32[]{:S(2)}) collective-permute-start(bf16[128,1024]{1,0:T(8,128)(2,1)S(1)} %get-tuple-element.49), channel_id=1, source_target_pairs={{2,0},{4,2},{6,4},{7,6},{5,7},{3,5},{1,3},{0,1},{10,8},{12,10},{14... | collective-permute-start | bytes 786440 | tf_op jit(solution)/shard_map/ppermute | solution.py:226
  75.1 13.3 %collective-permute-start.11 = (bf16[192,1024]{1,0:T(8,128)(2,1)S(1)}, bf16[192,1024]{1,0:T(8,128)(2,1)}, u32[]{:S(2)}, u32[]{:S(2)}) collective-permute-start(bf16[192,1024]{1,0:T(8,128)(2,1)S(1)} %get-tuple-element.48), channel_id=1, source_target_pairs={{0,2},{2,4},{4,6},{6,7},{7,5},{5,3},{3,1},{1,0},{8,10},{10,12},{12... | collective-permute-start | bytes 1179656 | tf_op jit(solution)/shard_map/ppermute | solution.py:223
  75.6 2.7 %copy-start.11 = (f32[64,2048]{1,0:T(8,128)}, f32[64,2048]{1,0:T(8,128)S(1)}, u32[]{:S(2)}) copy-start(f32[64,2048]{1,0:T(8,128)S(1)} %convert_add_fusion.1) | copy-start | bytes 1572868
  76.4 1.9 %copy-start.17 = (bf16[512,64]{1,0:T(8,128)(2,1)}, bf16[512,64]{1,0:T(8,128)(2,1)S(1)}, u32[]{:S(2)}) copy-start(bf16[512,64]{1,0:T(8,128)(2,1)S(1)} %fusion.2) | copy-start | bytes 196612
  76.6 11.1 %collective-permute-start.14 = (f32[64,256]{1,0:T(8,128)S(1)}, f32[64,256]{1,0:T(8,128)S(1)}, u32[]{:S(2)}, u32[]{:S(2)}) collective-permute-start(f32[64,256]{1,0:T(8,128)S(1)} %fusion.3), channel_id=1, source_target_pairs={{0,1},{1,0},{2,3},{3,2},{4,5},{5,4},{6,7},{7,6},{8,9},{9,8},{10,11... | collective-permute-start | bytes 196616 | tf_op jit(solution)/shard_map/ppermute | solution.py:229
  82.9 1.0 copy-start.5
  87.7 0.7 copy-start.9
  88.4 6.5 %collective-permute-start.18 = (bf16[64,1024]{1,0:T(8,128)(2,1)}, bf16[64,1024]{1,0:T(8,128)(2,1)S(1)}, u32[]{:S(2)}, u32[]{:S(2)}) collective-permute-start(bf16[64,1024]{1,0:T(8,128)(2,1)} %dynamic-slice_convert_fusion.1), channel_id=1, source_target_pairs={{0,2},{1,3},{2,0},{3,1},{4,6},{5,7},{6,4},{7,5},{8,10},{9,11},{10,... | collective-permute-start | bytes 393224 | tf_op jit(solution)/shard_map/ppermute | solution.py:229
  88.4 6.4 %collective-permute-start.17 = (f32[64,256]{1,0:T(8,128)S(1)}, f32[64,256]{1,0:T(8,128)S(1)}, u32[]{:S(2)}, u32[]{:S(2)}) collective-permute-start(f32[64,256]{1,0:T(8,128)S(1)} %add.93), channel_id=1, source_target_pairs={{0,2},{1,3},{2,0},{3,1},{4,6},{5,7},{6,4},{7,5},{8,10},{9,11},{10,... | collective-permute-start | bytes 196616 | tf_op jit(solution)/shard_map/ppermute | solution.py:229
  90.4 13.2 %collective-permute-start.22 = (bf16[192,1024]{1,0:T(8,128)(2,1)}, bf16[192,1024]{1,0:T(8,128)(2,1)S(1)}, u32[]{:S(2)}, u32[]{:S(2)}) collective-permute-start(bf16[192,1024]{1,0:T(8,128)(2,1)} %collective-permute-done.11.refs_0_), channel_id=1, source_target_pairs={{0,16},{8,24},{16,0},{24,8},{1,17},{9,25},{17,1},{25,9},{2,18},{10... | collective-permute-start | bytes 1179656 | tf_op jit(solution)/shard_map/ppermute | solution.py:229
  95.9 9.9 %copy-start.10 = (bf16[128,1024]{1,0:T(8,128)(2,1)S(1)}, bf16[128,1024]{1,0:T(8,128)(2,1)}, u32[]{:S(2)}) copy-start(bf16[128,1024]{1,0:T(8,128)(2,1)} %copy-done.9) | copy-start | bytes 786436
  95.9 7.7 %collective-permute-start.21 = (bf16[64,512]{1,0:T(8,128)(2,1)S(1)}, bf16[64,512]{1,0:T(8,128)(2,1)S(1)}, u32[]{:S(2)}, u32[]{:S(2)}) collective-permute-start(bf16[64,512]{1,0:T(8,128)(2,1)S(1)} %dynamic-slice_convert_fusion.2), channel_id=1, source_target_pairs={{0,4},{1,5},{2,6},{3,7},{4,0},{5,1},{6,2},{7,3},{8,12},{9,13},{10,... | collective-permute-start | bytes 196616 | tf_op jit(solution)/shard_map/ppermute | solution.py:229
  98.4 5.2 %collective-permute-start.20 = (f32[64,256]{1,0:T(8,128)S(1)}, f32[64,256]{1,0:T(8,128)S(1)}, u32[]{:S(2)}, u32[]{:S(2)}) collective-permute-start(f32[64,256]{1,0:T(8,128)S(1)} %add.99), channel_id=1, source_target_pairs={{0,4},{1,5},{2,6},{3,7},{4,0},{5,1},{6,2},{7,3},{8,12},{9,13},{10,... | collective-permute-start | bytes 196616 | tf_op jit(solution)/shard_map/ppermute | solution.py:229
  103.6 5.8 %collective-permute-start.23 = (f32[64,768]{1,0:T(8,128)S(1)}, f32[64,768]{1,0:T(8,128)S(1)}, u32[]{:S(2)}, u32[]{:S(2)}) collective-permute-start(f32[64,768]{1,0:T(8,128)S(1)} %pad_maximum_fusion.4), channel_id=1, source_target_pairs={{0,16},{8,24},{16,0},{24,8},{1,17},{9,25},{17,1},{25,9},{2,18},{10... | collective-permute-start | bytes 589832 | tf_op jit(solution)/shard_map/ppermute | solution.py:229
  109.5 3.9 %collective-permute-start.24 = (f32[256,512]{1,0:T(8,128)S(1)}, f32[256,512]{1,0:T(8,128)S(1)}, u32[]{:S(2)}, u32[]{:S(2)}) collective-permute-start(f32[256,512]{1,0:T(8,128)S(1)} %slice.61), channel_id=1, source_target_pairs={{0,8},{8,0},{16,24},{24,16},{1,9},{9,1},{17,25},{25,17},{2,10},{10... | collective-permute-start | bytes 1572872 | tf_op jit(solution)/shard_map/ppermute | solution.py:229
  109.6 2.3 %collective-permute-start.25 = (f32[64,1280]{1,0:T(8,128)S(1)}, f32[64,1280]{1,0:T(8,128)S(1)}, u32[]{:S(2)}, u32[]{:S(2)}) collective-permute-start(f32[64,1280]{1,0:T(8,128)S(1)} %pad_maximum_fusion.3.mine), channel_id=1, source_target_pairs={{0,8},{8,0},{16,24},{24,16},{1,9},{9,1},{17,25},{25,17},{2,10},{10... | collective-permute-start | bytes 983048 | tf_op jit(solution)/shard_map/ppermute | solution.py:229
  113.4 0.9 copy-start.18

commit v3 on v2

--- a/solution.py
+++ b/solution.py
@@ -233,7 +233,7 @@
         width, own = quant.shape
         rank = adapter_up.shape[0]
         part = own // 2
-        given = width * 3 // 8
+        given = width * 11 // 32
         ring = width - given
         device = lax.axis_index("dp")
         core = device & 1

time: 116 us -> 117 us (level)
  waiting for transfers between devices: 27.1 us -> 29.3 us
  starting transfers between devices: 35 us -> 33.8 us
    ppermute x4, waiting for transfers between devices: 3.54 us -> 6.26 us  [forward(): lax.ppermute(a, 'fsdp', [(order[i], order[(i + 1) % n]) for i in range(n)])]
    ppermute x17, starting transfers between devices: 20.2 us -> 18.8 us  [over(): lax.ppermute(a, axis, [(i, i ^ bit) for i in range(mesh.shape[axis])])]
    unnamed x40 -> x42, local copies, waits for them, and re-layouts: 3.27 us -> 3.8 us
  transfers between devices with their start and end apart: 26 -> 26, of which waited for: 12 -> 12; matrix products, arithmetic and copies ran while one was open for 9% -> 8% of each run, Pallas kernels for 33% -> 32%
where the time goes in v3:
time: 117 us
  Pallas kernels  37.5 us (32%)
  starting transfers between devices  33.8 us (29%)
  waiting for transfers between devices  29.3 us (25%)
  local copies, waits for them, and re-layouts  9.24 us (8%)
  other arithmetic  4.2 us (4%)
  matrix products  1.55 us (1%)
    pallas_call x7, Pallas kernels, products(): pl.pallas_call(body, grid_spec=pltpu.PrefetchScalarGridSpec(num_scalar_pr...  27 us
    ppermute x17, waiting for transfers between devices, over(): lax.ppermute(a, axis, [(i, i ^ bit) for i in range(mesh.shape[axis])])  21.3 us
    ppermute x17, starting transfers between devices, over(): lax.ppermute(a, axis, [(i, i ^ bit) for i in range(mesh.shape[axis])])  18.8 us
    pallas_call x1, Pallas kernels, terms_b(): pl.pallas_call(body, grid_spec=pltpu.PrefetchScalarGridSpec(num_scalar_pr...  8.16 us
    ppermute x4, starting transfers between devices, backward(): lax.ppermute(a, 'fsdp', [(order[(i + 1) % n], order[i]) for i in range(n)])  6.65 us
    ppermute x4, waiting for transfers between devices, forward(): lax.ppermute(a, 'fsdp', [(order[i], order[(i + 1) % n]) for i in range(n)])  6.26 us
    ppermute x4, starting transfers between devices, forward(): lax.ppermute(a, 'fsdp', [(order[i], order[(i + 1) % n]) for i in range(n)])  4.75 us
    unnamed x42, local copies, waits for them, and re-layouts  3.8 us
  transfers between devices with their start and end apart: 26, of which 12 were waited for; matrix products, arithmetic and copies ran while one was open for 8% of the time, Pallas kernels for 32%

profile of v3, /device:TPU:0, one launch (start us, length us, event | category | flops | bytes accessed | tf_op | source)
XLA Modules:
  0.0 116.7 jit_solution(6371578208865024483)
XLA Ops:
  0.7 0.5 collective-permute-start.2
  1.2 0.9 constant_dynamic-slice_fusion.2
  2.1 0.6 broadcast_in_dim.7
  2.7 0.6 fusion
  3.4 0.8 broadcast_select_fusion
  4.3 2.6 %collective-permute-start.1 = (bf16[400,1024]{1,0:T(8,128)(2,1)S(1)}, bf16[400,1024]{1,0:T(8,128)(2,1)S(1)}, u32[]{:S(2)}, u32[]{:S(2)}) collective-permute-start(bf16[400,1024]{1,0:T(8,128)(2,1)S(1)} %pad_maximum_fusion.refs_0_), channel_id=1, source_target_pairs={{2,0},{4,2},{6,4},{7,6},{5,7},{3,5},{1,3},{0,1},{10,8},{12,10},{14... | collective-permute-start | bytes 2457608 | tf_op jit(solution)/shard_map/ppermute | solution.py:226
  6.9 0.1 collective-permute-start
  7.2 0.2 convolution_convert_fusion.1.low
  7.4 7.0 %collective-permute-done.3 = bf16[256,512]{1,0:T(8,128)(2,1)S(1)} collective-permute-done((bf16[256,512]{1,0:T(8,128)(2,1)S(1)}, bf16[256,512]{1,0:T(8,128)(2,1)S(1)}, u32[]{:S(2)}, u32[]{:S(2)}) %collective-permute-start.3) | collective-permute-done | bytes 262176 | tf_op jit(solution)/shard_map/ppermute | solution.py:229
  14.3 0.2 convolution_convert_fusion.low_partner
  14.5 0.5 copy-done.13
  15.0 8.2 %terms_b.1 = (f32[64,4096]{1,0:T(8,128)S(1)}, bf16[64,4096]{1,0:T(8,128)(2,1)}) custom-call(s32[18]{0:T(128)S(1)} %pad_add_fusion.info, bf16[256,16384]{1,0:T(8,128)(2,1)} %mine.15, bf16[256,16384]{1,0:T(8,128)(2,1)} %collective-permute-done.2.partner, bf16[64,256]{1,0:T(8,128)(2,1)S(1)} %convolution_convert_fusion.1.low, ...), custom_call_target="tpu_custom_call" | custom-call | flops 536870912 | bytes 8388608 | tf_op jit(solution)/shard_map/terms_b/pallas_call | solution.py:92
  23.2 1.0 copy-done.7
  24.2 1.5 %collective-permute-done.1.refs_2_.refs_4_ = bf16[400,1024]{1,0:T(8,128)(2,1)S(1)} collective-permute-done((bf16[400,1024]{1,0:T(8,128)(2,1)S(1)}, bf16[400,1024]{1,0:T(8,128)(2,1)S(1)}, u32[]{:S(2)}, u32[]{:S(2)}) %collective-permute-start.1) | collective-permute-done | bytes 819232 | tf_op jit(solution)/shard_map/ppermute | solution.py:226
  25.7 1.4 %collective-permute-done.refs_1_.refs_2_ = bf16[400,1024]{1,0:T(8,128)(2,1)S(1)} collective-permute-done((bf16[400,1024]{1,0:T(8,128)(2,1)S(1)}, bf16[400,1024]{1,0:T(8,128)(2,1)S(1)}, u32[]{:S(2)}, u32[]{:S(2)}) %collective-permute-start) | collective-permute-done | bytes 819232 | tf_op jit(solution)/shard_map/ppermute | solution.py:223
  27.1 0.4 collective-permute-start.4
  27.5 1.6 %collective-permute-start.6 = (bf16[400,1024]{1,0:T(8,128)(2,1)S(1)}, bf16[400,1024]{1,0:T(8,128)(2,1)}, u32[]{:S(2)}, u32[]{:S(2)}) collective-permute-start(bf16[400,1024]{1,0:T(8,128)(2,1)S(1)} %collective-permute-done.1.refs_2_.refs_4_), channel_id=1, source_target_pairs={{2,0},{4,2},{6,4},{7,6},{5,7},{3,5},{1,3},{0,1},{10,8},{12,10},{14... | collective-permute-start | bytes 2457608 | tf_op jit(solution)/shard_map/ppermute | solution.py:226
  29.1 1.5 %collective-permute-start.8 = (bf16[64,4096]{1,0:T(8,128)(2,1)}, bf16[64,4096]{1,0:T(8,128)(2,1)}, u32[]{:S(2)}, u32[]{:S(2)}) collective-permute-start(bf16[64,4096]{1,0:T(8,128)(2,1)} %get-tuple-element.39), channel_id=1, source_target_pairs={{0,16},{8,24},{16,0},{24,8},{1,17},{9,25},{17,1},{25,9},{2,18},{10... | collective-permute-start | bytes 1572872 | tf_op jit(solution)/shard_map/ppermute | solution.py:229
  30.6 0.9 constant_dynamic-slice_fusion.1
  31.5 0.9 constant_dynamic-slice_fusion
  32.4 3.6 %collective-permute-start.10 = (bf16[64,1024]{1,0:T(8,128)(2,1)}, bf16[64,1024]{1,0:T(8,128)(2,1)S(1)}, u32[]{:S(2)}, u32[]{:S(2)}) collective-permute-start(bf16[64,1024]{1,0:T(8,128)(2,1)} %copy-done.17), channel_id=1, source_target_pairs={{0,7},{2,5},{4,3},{6,1},{7,0},{5,2},{3,4},{1,6},{8,15},{10,13},{12... | collective-permute-start | bytes 393224 | tf_op jit(solution)/shard_map/ppermute | solution.py:288
  36.0 3.9 %through_first.1.refs_3_ = f32[512,64]{1,0:T(8,128)S(1)} custom-call(s32[18]{0:T(128)S(1)} %pad_add_fusion.info, bf16[256,16384]{1,0:T(8,128)(2,1)} %mine.15, bf16[256,16384]{1,0:T(8,128)(2,1)} %collective-permute-done.2.partner, bf16[400,1024]{1,0:T(8,128)(2,1)S(1)} %pad_maximum_fusion.refs_0_, bf16[400,1024]{1,0:T(8,128)(2,1)S(1)} %collective-permute-done.refs_1_.refs_2_, ...), custom_call_target="tpu_custom_call" | custom-call | flops 201326592 | bytes 3670016 | tf_op jit(solution)/shard_map/through_first/pallas_call | solution.py:151
  40.0 1.9 %collective-permute-done.8 = bf16[64,4096]{1,0:T(8,128)(2,1)} collective-permute-done((bf16[64,4096]{1,0:T(8,128)(2,1)}, bf16[64,4096]{1,0:T(8,128)(2,1)}, u32[]{:S(2)}, u32[]{:S(2)}) %collective-permute-start.8) | collective-permute-done | bytes 524320 | tf_op jit(solution)/shard_map/ppermute | solution.py:229
  42.0 1.6 %collective-permute-start.9 = (bf16[352,1024]{1,0:T(8,128)(2,1)S(1)}, bf16[352,1024]{1,0:T(8,128)(2,1)S(1)}, u32[]{:S(2)}, u32[]{:S(2)}) collective-permute-start(bf16[352,1024]{1,0:T(8,128)(2,1)S(1)} %pad_maximum_fusion.1), channel_id=1, source_target_pairs={{0,16},{8,24},{16,0},{24,8},{1,17},{9,25},{17,1},{25,9},{2,18},{10... | collective-permute-start | bytes 2162696 | tf_op jit(solution)/shard_map/ppermute | solution.py:229
  43.6 2.8 %collective-permute-done.4.refs_0_ = bf16[400,1024]{1,0:T(8,128)(2,1)S(1)} collective-permute-done((bf16[400,1024]{1,0:T(8,128)(2,1)S(1)}, bf16[400,1024]{1,0:T(8,128)(2,1)S(1)}, u32[]{:S(2)}, u32[]{:S(2)}) %collective-permute-start.4) | collective-permute-done | bytes 819232 | tf_op jit(solution)/shard_map/ppermute | solution.py:223
  46.4 4.0 %collective-permute-start.5 = (bf16[400,1024]{1,0:T(8,128)(2,1)S(1)}, bf16[400,1024]{1,0:T(8,128)(2,1)S(1)}, u32[]{:S(2)}, u32[]{:S(2)}) collective-permute-start(bf16[400,1024]{1,0:T(8,128)(2,1)S(1)} %collective-permute-done.4.refs_0_), channel_id=1, source_target_pairs={{0,2},{2,4},{4,6},{6,7},{7,5},{5,3},{3,1},{1,0},{8,10},{10,12},{12... | collective-permute-start | bytes 2457608 | tf_op jit(solution)/shard_map/ppermute | solution.py:223
  50.4 1.2 convert_add_fusion
  51.6 3.2 %collective-permute-start.15 = (bf16[64,2048]{1,0:T(8,128)(2,1)S(1)}, bf16[64,2048]{1,0:T(8,128)(2,1)S(1)}, u32[]{:S(2)}, u32[]{:S(2)}) collective-permute-start(bf16[64,2048]{1,0:T(8,128)(2,1)S(1)} %dynamic-slice_convert_fusion), channel_id=1, source_target_pairs={{0,1},{1,0},{2,3},{3,2},{4,5},{5,4},{6,7},{7,6},{8,9},{9,8},{10,11... | collective-permute-start | bytes 786440 | tf_op jit(solution)/shard_map/ppermute | solution.py:229
  54.9 1.0 slice.74
  56.0 1.6 %collective-permute-start.16 = (bf16[352,1024]{1,0:T(8,128)(2,1)S(1)}, bf16[352,1024]{1,0:T(8,128)(2,1)S(1)}, u32[]{:S(2)}, u32[]{:S(2)}) collective-permute-start(bf16[352,1024]{1,0:T(8,128)(2,1)S(1)} %pad_maximum_fusion.2), channel_id=1, source_target_pairs={{0,16},{8,24},{16,0},{24,8},{1,17},{9,25},{17,1},{25,9},{2,18},{10... | collective-permute-start | bytes 2162696 | tf_op jit(solution)/shard_map/ppermute | solution.py:229
  57.6 3.9 %through_second.1.refs_2_ = f32[512,64]{1,0:T(8,128)S(1)} custom-call(s32[18]{0:T(128)S(1)} %pad_add_fusion.info, bf16[256,16384]{1,0:T(8,128)(2,1)} %mine.15, bf16[256,16384]{1,0:T(8,128)(2,1)} %collective-permute-done.2.partner, bf16[400,1024]{1,0:T(8,128)(2,1)S(1)} %collective-permute-done.4.refs_0_, ...), custom_call_target="tpu_custom_call" | custom-call | flops 201326592 | bytes 3670016 | tf_op jit(solution)/shard_map/through_second/pallas_call | solution.py:151
  61.6 5.7 %first.1.refs_4_ = f32[512,512]{1,0:T(8,128)} custom-call(s32[18]{0:T(128)S(1)} %pad_add_fusion.info, bf16[256,16384]{1,0:T(8,128)(2,1)} %mine.15, bf16[256,16384]{1,0:T(8,128)(2,1)} %collective-permute-done.2.partner, bf16[400,1024]{1,0:T(8,128)(2,1)S(1)} %pad_maximum_fusion.refs_0_, bf16[176,1024]{1,0:T(8,128)(2,1)S(1)} %copy-done.6, ...), custom_call_target="tpu_custom_call" | custom-call | flops 1610612736 | bytes 7340032 | tf_op jit(solution)/shard_map/first/pallas_call | solution.py:151
  67.2 2.0 %collective-permute-done.5.refs_0_.refs_2_ = bf16[400,1024]{1,0:T(8,128)(2,1)S(1)} collective-permute-done((bf16[400,1024]{1,0:T(8,128)(2,1)S(1)}, bf16[400,1024]{1,0:T(8,128)(2,1)S(1)}, u32[]{:S(2)}, u32[]{:S(2)}) %collective-permute-start.5) | collective-permute-done | bytes 819232 | tf_op jit(solution)/shard_map/ppermute | solution.py:223
  69.3 0.3 collective-permute-done.7.refs_1_.refs_3_.refs_2_
  69.5 0.9 assemble.1
  70.4 1.4 %collective-permute-start.19 = (bf16[352,1024]{1,0:T(8,128)(2,1)}, bf16[352,1024]{1,0:T(8,128)(2,1)S(1)}, u32[]{:S(2)}, u32[]{:S(2)}) collective-permute-start(bf16[352,1024]{1,0:T(8,128)(2,1)} %get-tuple-element.51), channel_id=1, source_target_pairs={{0,16},{8,24},{16,0},{24,8},{1,17},{9,25},{17,1},{25,9},{2,18},{10... | collective-permute-start | bytes 2162696 | tf_op jit(solution)/shard_map/ppermute | solution.py:229
  71.9 2.7 %through_last.1 = f32[512,64]{1,0:T(8,128)S(1)} custom-call(s32[18]{0:T(128)S(1)} %pad_add_fusion.info, bf16[256,16384]{1,0:T(8,128)(2,1)} %mine.15, bf16[256,16384]{1,0:T(8,128)(2,1)} %collective-permute-done.2.partner, bf16[400,1024]{1,0:T(8,128)(2,1)S(1)} %collective-permute-done.5.refs_0_.refs_2_, ...), custom_call_target="tpu_custom_call" | custom-call | flops 134217728 | bytes 2490368 | tf_op jit(solution)/shard_map/through_last/pallas_call | solution.py:151
  74.7 2.4 %collective-permute-start.12 = (bf16[160,1024]{1,0:T(8,128)(2,1)S(1)}, bf16[160,1024]{1,0:T(8,128)(2,1)S(1)}, u32[]{:S(2)}, u32[]{:S(2)}) collective-permute-start(bf16[160,1024]{1,0:T(8,128)(2,1)S(1)} %get-tuple-element.49), channel_id=1, source_target_pairs={{2,0},{4,2},{6,4},{7,6},{5,7},{3,5},{1,3},{0,1},{10,8},{12,10},{14... | collective-permute-start | bytes 983048 | tf_op jit(solution)/shard_map/ppermute | solution.py:226
  77.1 0.2 collective-permute-start.11
  77.4 0.7 dynamic-slice_convert_fusion.1
  78.2 0.2 fusion.3
  78.5 1.9 %collective-permute-start.14 = (f32[64,256]{1,0:T(8,128)S(1)}, f32[64,256]{1,0:T(8,128)S(1)}, u32[]{:S(2)}, u32[]{:S(2)}) collective-permute-start(f32[64,256]{1,0:T(8,128)S(1)} %fusion.3), channel_id=1, source_target_pairs={{0,1},{1,0},{2,3},{3,2},{4,5},{5,4},{6,7},{7,6},{8,9},{9,8},{10,11... | collective-permute-start | bytes 196616 | tf_op jit(solution)/shard_map/ppermute | solution.py:229
  80.3 4.2 %middle.1.refs_4_ = f32[512,512]{1,0:T(8,128)S(1)} custom-call(s32[18]{0:T(128)S(1)} %pad_add_fusion.info, bf16[256,16384]{1,0:T(8,128)(2,1)} %mine.15, bf16[256,16384]{1,0:T(8,128)(2,1)} %collective-permute-done.2.partner, bf16[400,1024]{1,0:T(8,128)(2,1)S(1)} %collective-permute-done.4.refs_0_, ...), custom_call_target="tpu_custom_call" | custom-call | flops 1073741824 | bytes 5242880 | tf_op jit(solution)/shard_map/middle/pallas_call | solution.py:151
  84.5 1.0 copy-done.5
  85.5 3.5 %collective-permute-done.14 = f32[64,256]{1,0:T(8,128)S(1)} collective-permute-done((f32[64,256]{1,0:T(8,128)S(1)}, f32[64,256]{1,0:T(8,128)S(1)}, u32[]{:S(2)}, u32[]{:S(2)}) %collective-permute-start.14) | collective-permute-done | bytes 65568 | tf_op jit(solution)/shard_map/ppermute | solution.py:229
  89.1 0.7 copy-done.9
  89.8 2.0 %collective-permute-start.17 = (f32[64,256]{1,0:T(8,128)S(1)}, f32[64,256]{1,0:T(8,128)S(1)}, u32[]{:S(2)}, u32[]{:S(2)}) collective-permute-start(f32[64,256]{1,0:T(8,128)S(1)} %add.93), channel_id=1, source_target_pairs={{0,2},{1,3},{2,0},{3,1},{4,6},{5,7},{6,4},{7,5},{8,10},{9,11},{10,... | collective-permute-start | bytes 196616 | tf_op jit(solution)/shard_map/ppermute | solution.py:229
  91.8 0.6 collective-permute-start.22
  92.5 3.8 %collective-permute-done.17 = f32[64,256]{1,0:T(8,128)S(1)} collective-permute-done((f32[64,256]{1,0:T(8,128)S(1)}, f32[64,256]{1,0:T(8,128)S(1)}, u32[]{:S(2)}, u32[]{:S(2)}) %collective-permute-start.17) | collective-permute-done | bytes 65568 | tf_op jit(solution)/shard_map/ppermute | solution.py:229
  96.2 1.0 convert_add_fusion.2
  97.3 1.2 %collective-permute-start.21 = (bf16[64,512]{1,0:T(8,128)(2,1)S(1)}, bf16[64,512]{1,0:T(8,128)(2,1)S(1)}, u32[]{:S(2)}, u32[]{:S(2)}) collective-permute-start(bf16[64,512]{1,0:T(8,128)(2,1)S(1)} %dynamic-slice_convert_fusion.2), channel_id=1, source_target_pairs={{0,4},{1,5},{2,6},{3,7},{4,0},{5,1},{6,2},{7,3},{8,12},{9,13},{10,... | collective-permute-start | bytes 196616 | tf_op jit(solution)/shard_map/ppermute | solution.py:229
  98.5 1.8 %collective-permute-start.20 = (f32[64,256]{1,0:T(8,128)S(1)}, f32[64,256]{1,0:T(8,128)S(1)}, u32[]{:S(2)}, u32[]{:S(2)}) collective-permute-start(f32[64,256]{1,0:T(8,128)S(1)} %add.99), channel_id=1, source_target_pairs={{0,4},{1,5},{2,6},{3,7},{4,0},{5,1},{6,2},{7,3},{8,12},{9,13},{10,... | collective-permute-start | bytes 196616 | tf_op jit(solution)/shard_map/ppermute | solution.py:229
  100.3 3.9 %late.1.refs_3_ = f32[512,512]{1,0:T(8,128)S(1)} custom-call(s32[18]{0:T(128)S(1)} %pad_add_fusion.info, bf16[256,16384]{1,0:T(8,128)(2,1)} %mine.15, bf16[256,16384]{1,0:T(8,128)(2,1)} %collective-permute-done.2.partner, bf16[400,1024]{1,0:T(8,128)(2,1)S(1)} %collective-permute-done.5.refs_0_.refs_2_, ...), custom_call_target="tpu_custom_call" | custom-call | flops 1073741824 | bytes 5242880 | tf_op jit(solution)/shard_map/late/pallas_call | solution.py:151
  104.2 0.8 collective-permute-done.20
  105.1 0.7 collective-permute-start.23
  105.8 2.6 %last.1 = f32[512,512]{1,0:T(8,128)S(1)} custom-call(s32[18]{0:T(128)S(1)} %pad_add_fusion.info, bf16[256,16384]{1,0:T(8,128)(2,1)} %mine.15, bf16[256,16384]{1,0:T(8,128)(2,1)} %collective-permute-done.2.partner, bf16[176,1024]{1,0:T(8,128)(2,1)} %collective-permute-done.11.refs_0_, bf16[160,1024]{1,0:T(8,128)(2,1)S(1)} %copy-done.10, ...), custom_call_target="tpu_custom_call" | custom-call | flops 536870912 | bytes 3145728 | tf_op jit(solution)/shard_map/last/pallas_call | solution.py:151
  108.4 2.4 %collective-permute-done.23 = f32[64,768]{1,0:T(8,128)S(1)} collective-permute-done((f32[64,768]{1,0:T(8,128)S(1)}, f32[64,768]{1,0:T(8,128)S(1)}, u32[]{:S(2)}, u32[]{:S(2)}) %collective-permute-start.23) | collective-permute-done | bytes 196640 | tf_op jit(solution)/shard_map/ppermute | solution.py:229
  111.1 0.6 collective-permute-start.25
  111.6 1.8 %collective-permute-done.25.other = f32[64,1280]{1,0:T(8,128)S(1)} collective-permute-done((f32[64,1280]{1,0:T(8,128)S(1)}, f32[64,1280]{1,0:T(8,128)S(1)}, u32[]{:S(2)}, u32[]{:S(2)}) %collective-permute-start.25) | collective-permute-done | bytes 327712 | tf_op jit(solution)/shard_map/ppermute | solution.py:229
  113.4 1.4 %finish.1 = (f32[64,2048]{1,0:T(8,128)}, f32[64,512]{1,0:T(8,128)}) custom-call(s32[18]{0:T(128)S(1)} %pad_add_fusion.info, f32[1]{0:T(128)} %constant.69.clone.1.factor, f32[64,1280]{1,0:T(8,128)S(1)} %pad_maximum_fusion.3.mine, f32[64,1280]{1,0:T(8,128)S(1)} %collective-permute-done.25.other), custom_call_target="tpu_custom_call" | custom-call | bytes 1310720 | tf_op jit(solution)/shard_map/finish/pallas_call | solution.py:194
  114.9 0.1 slice.77
  115.1 0.1 slice_select_fusion.1
  115.2 0.5 copy-done.15
  115.8 1.0 fusion.1
  (82 shorter events, 1.2 us)
Async XLA Ops:
  0.6 2.7 %copy-start = (bf16[64,2048]{1,0:T(8,128)(2,1)S(1)}, bf16[64,2048]{1,0:T(8,128)(2,1)}, u32[]{:S(2)}) copy-start(bf16[64,2048]{1,0:T(8,128)(2,1)} %param.12) | copy-start | bytes 786436
  0.6 2.1 %copy-start.16 = (bf16[512,2048]{1,0:T(8,128)(2,1)S(1)}, bf16[512,2048]{1,0:T(8,128)(2,1)}, u32[]{:S(2)}) copy-start(bf16[512,2048]{1,0:T(8,128)(2,1)} %param.9) | copy-start | bytes 6291460
  0.7 14.4 %collective-permute-start.2 = (bf16[256,16384]{1,0:T(8,128)(2,1)}, bf16[256,16384]{1,0:T(8,128)(2,1)}, u32[]{:S(2)}, u32[]{:S(2)}) collective-permute-start(bf16[256,16384]{1,0:T(8,128)(2,1)} %mine.15), channel_id=1, source_target_pairs={{0,8},{8,0},{16,24},{24,16},{1,9},{9,1},{17,25},{25,17},{2,10},{10... | collective-permute-start | bytes 25165832 | tf_op jit(solution)/shard_map/ppermute | solution.py:229
  3.3 3.7 %copy-start.12 = (bf16[256,512]{1,0:T(8,128)(2,1)S(1)}, bf16[256,512]{1,0:T(8,128)(2,1)}, u32[]{:S(2)}) copy-start(bf16[256,512]{1,0:T(8,128)(2,1)} %param.7) | copy-start | bytes 786436
  3.3 3.7 %copy-start.20 = (s32[8]{0:T(128)S(1)}, s32[8]{0:T(128)}, u32[]{:S(2)}) copy-start(s32[8]{0:T(128)} %constant.70.clone) | copy-start | bytes 100
  3.4 3.8 %copy-start.14 = (bf16[512,64]{0,1:T(8,128)(2,1)S(1)}, bf16[512,64]{0,1:T(8,128)(2,1)}, u32[]{:S(2)}) copy-start(bf16[512,64]{0,1:T(8,128)(2,1)} %param.11) | copy-start | bytes 196612
  3.4 3.5 %copy-start.17 = (bf16[64,1024]{1,0:T(8,128)(2,1)}, bf16[64,1024]{1,0:T(8,128)(2,1)S(1)}, u32[]{:S(2)}) copy-start(bf16[64,1024]{1,0:T(8,128)(2,1)S(1)} %constant_dynamic-slice_fusion.3) | copy-start | bytes 393220
  4.3 21.4 %collective-permute-start.1 = (bf16[400,1024]{1,0:T(8,128)(2,1)S(1)}, bf16[400,1024]{1,0:T(8,128)(2,1)S(1)}, u32[]{:S(2)}, u32[]{:S(2)}) collective-permute-start(bf16[400,1024]{1,0:T(8,128)(2,1)S(1)} %pad_maximum_fusion.refs_0_), channel_id=1, source_target_pairs={{2,0},{4,2},{6,4},{7,6},{5,7},{3,5},{1,3},{0,1},{10,8},{12,10},{14... | collective-permute-start | bytes 2457608 | tf_op jit(solution)/shard_map/ppermute | solution.py:226
  6.9 20.2 %collective-permute-start = (bf16[400,1024]{1,0:T(8,128)(2,1)S(1)}, bf16[400,1024]{1,0:T(8,128)(2,1)S(1)}, u32[]{:S(2)}, u32[]{:S(2)}) collective-permute-start(bf16[400,1024]{1,0:T(8,128)(2,1)S(1)} %pad_maximum_fusion.refs_0_), channel_id=1, source_target_pairs={{0,2},{2,4},{4,6},{6,7},{7,5},{5,3},{3,1},{1,0},{8,10},{10,12},{12... | collective-permute-start | bytes 2457608 | tf_op jit(solution)/shard_map/ppermute | solution.py:223
  7.0 7.3 %collective-permute-start.3 = (bf16[256,512]{1,0:T(8,128)(2,1)S(1)}, bf16[256,512]{1,0:T(8,128)(2,1)S(1)}, u32[]{:S(2)}, u32[]{:S(2)}) collective-permute-start(bf16[256,512]{1,0:T(8,128)(2,1)S(1)} %copy-done.12), channel_id=1, source_target_pairs={{0,8},{8,0},{16,24},{24,16},{1,9},{9,1},{17,25},{25,17},{2,10},{10... | collective-permute-start | bytes 786440 | tf_op jit(solution)/shard_map/ppermute | solution.py:229
  14.3 0.7 copy-start.13
  23.2 1.0 copy-start.7
  25.7 16.3 %copy-start.1 = (bf16[400,1024]{1,0:T(8,128)(2,1)}, bf16[400,1024]{1,0:T(8,128)(2,1)S(1)}, u32[]{:S(2)}) copy-start(bf16[400,1024]{1,0:T(8,128)(2,1)S(1)} %collective-permute-done.1.refs_2_.refs_4_) | copy-start | bytes 2457604
  27.1 14.8 %copy-start.3 = (bf16[400,1024]{1,0:T(8,128)(2,1)}, bf16[400,1024]{1,0:T(8,128)(2,1)S(1)}, u32[]{:S(2)}) copy-start(bf16[400,1024]{1,0:T(8,128)(2,1)S(1)} %collective-permute-done.refs_1_.refs_2_) | copy-start | bytes 2457604
  27.1 19.4 %collective-permute-start.4 = (bf16[400,1024]{1,0:T(8,128)(2,1)S(1)}, bf16[400,1024]{1,0:T(8,128)(2,1)S(1)}, u32[]{:S(2)}, u32[]{:S(2)}) collective-permute-start(bf16[400,1024]{1,0:T(8,128)(2,1)S(1)} %collective-permute-done.refs_1_.refs_2_), channel_id=1, source_target_pairs={{0,2},{2,4},{4,6},{6,7},{7,5},{5,3},{3,1},{1,0},{8,10},{10,12},{12... | collective-permute-start | bytes 2457608 | tf_op jit(solution)/shard_map/ppermute | solution.py:223
  27.5 22.9 %collective-permute-start.6 = (bf16[400,1024]{1,0:T(8,128)(2,1)S(1)}, bf16[400,1024]{1,0:T(8,128)(2,1)}, u32[]{:S(2)}, u32[]{:S(2)}) collective-permute-start(bf16[400,1024]{1,0:T(8,128)(2,1)S(1)} %collective-permute-done.1.refs_2_.refs_4_), channel_id=1, source_target_pairs={{2,0},{4,2},{6,4},{7,6},{5,7},{3,5},{1,3},{0,1},{10,8},{12,10},{14... | collective-permute-start | bytes 2457608 | tf_op jit(solution)/shard_map/ppermute | solution.py:226
  29.1 12.8 %collective-permute-start.8 = (bf16[64,4096]{1,0:T(8,128)(2,1)}, bf16[64,4096]{1,0:T(8,128)(2,1)}, u32[]{:S(2)}, u32[]{:S(2)}) collective-permute-start(bf16[64,4096]{1,0:T(8,128)(2,1)} %get-tuple-element.39), channel_id=1, source_target_pairs={{0,16},{8,24},{16,0},{24,8},{1,17},{9,25},{17,1},{25,9},{2,18},{10... | collective-permute-start | bytes 1572872 | tf_op jit(solution)/shard_map/ppermute | solution.py:229
  32.4 23.6 %collective-permute-start.10 = (bf16[64,1024]{1,0:T(8,128)(2,1)}, bf16[64,1024]{1,0:T(8,128)(2,1)S(1)}, u32[]{:S(2)}, u32[]{:S(2)}) collective-permute-start(bf16[64,1024]{1,0:T(8,128)(2,1)} %copy-done.17), channel_id=1, source_target_pairs={{0,7},{2,5},{4,3},{6,1},{7,0},{5,2},{3,4},{1,6},{8,15},{10,13},{12... | collective-permute-start | bytes 393224 | tf_op jit(solution)/shard_map/ppermute | solution.py:288
  40.0 10.5 %copy-start.8 = (f32[64,4096]{1,0:T(8,128)S(1)}, f32[64,4096]{1,0:T(8,128)}, u32[]{:S(2)}) copy-start(f32[64,4096]{1,0:T(8,128)} %copy-done.7) | copy-start | bytes 3145732
  42.0 19.5 %collective-permute-start.9 = (bf16[352,1024]{1,0:T(8,128)(2,1)S(1)}, bf16[352,1024]{1,0:T(8,128)(2,1)S(1)}, u32[]{:S(2)}, u32[]{:S(2)}) collective-permute-start(bf16[352,1024]{1,0:T(8,128)(2,1)S(1)} %pad_maximum_fusion.1), channel_id=1, source_target_pairs={{0,16},{8,24},{16,0},{24,8},{1,17},{9,25},{17,1},{25,9},{2,18},{10... | collective-permute-start | bytes 2162696 | tf_op jit(solution)/shard_map/ppermute | solution.py:229
  46.4 22.8 %collective-permute-start.5 = (bf16[400,1024]{1,0:T(8,128)(2,1)S(1)}, bf16[400,1024]{1,0:T(8,128)(2,1)S(1)}, u32[]{:S(2)}, u32[]{:S(2)}) collective-permute-start(bf16[400,1024]{1,0:T(8,128)(2,1)S(1)} %collective-permute-done.4.refs_0_), channel_id=1, source_target_pairs={{0,2},{2,4},{4,6},{6,7},{7,5},{5,3},{3,1},{1,0},{8,10},{10,12},{12... | collective-permute-start | bytes 2457608 | tf_op jit(solution)/shard_map/ppermute | solution.py:223
  50.4 19.1 %collective-permute-start.7 = (bf16[400,1024]{1,0:T(8,128)(2,1)}, bf16[400,1024]{1,0:T(8,128)(2,1)S(1)}, u32[]{:S(2)}, u32[]{:S(2)}) collective-permute-start(bf16[400,1024]{1,0:T(8,128)(2,1)} %collective-permute-done.6.refs_1_.refs_2_), channel_id=1, source_target_pairs={{2,0},{4,2},{6,4},{7,6},{5,7},{3,5},{1,3},{0,1},{10,8},{12,10},{14... | collective-permute-start | bytes 2457608 | tf_op jit(solution)/shard_map/ppermute | solution.py:226
  51.6 23.1 %collective-permute-start.15 = (bf16[64,2048]{1,0:T(8,128)(2,1)S(1)}, bf16[64,2048]{1,0:T(8,128)(2,1)S(1)}, u32[]{:S(2)}, u32[]{:S(2)}) collective-permute-start(bf16[64,2048]{1,0:T(8,128)(2,1)S(1)} %dynamic-slice_convert_fusion), channel_id=1, source_target_pairs={{0,1},{1,0},{2,3},{3,2},{4,5},{5,4},{6,7},{7,6},{8,9},{9,8},{10,11... | collective-permute-start | bytes 786440 | tf_op jit(solution)/shard_map/ppermute | solution.py:229
  56.0 5.6 %copy-start.2 = (bf16[400,1024]{1,0:T(8,128)(2,1)S(1)}, bf16[400,1024]{1,0:T(8,128)(2,1)}, u32[]{:S(2)}) copy-start(bf16[400,1024]{1,0:T(8,128)(2,1)} %copy-done.1) | copy-start | bytes 2457604
  56.0 5.6 %copy-start.4 = (bf16[400,1024]{1,0:T(8,128)(2,1)S(1)}, bf16[400,1024]{1,0:T(8,128)(2,1)}, u32[]{:S(2)}) copy-start(bf16[400,1024]{1,0:T(8,128)(2,1)} %copy-done.3) | copy-start | bytes 2457604
  56.0 5.6 %copy-start.6 = (bf16[176,1024]{1,0:T(8,128)(2,1)S(1)}, bf16[176,1024]{1,0:T(8,128)(2,1)}, u32[]{:S(2)}) copy-start(bf16[176,1024]{1,0:T(8,128)(2,1)} %get-tuple-element.77.refs_1_) | copy-start | bytes 1081348
  56.0 24.3 %collective-permute-start.16 = (bf16[352,1024]{1,0:T(8,128)(2,1)S(1)}, bf16[352,1024]{1,0:T(8,128)(2,1)S(1)}, u32[]{:S(2)}, u32[]{:S(2)}) collective-permute-start(bf16[352,1024]{1,0:T(8,128)(2,1)S(1)} %pad_maximum_fusion.2), channel_id=1, source_target_pairs={{0,16},{8,24},{16,0},{24,8},{1,17},{9,25},{17,1},{25,9},{2,18},{10... | collective-permute-start | bytes 2162696 | tf_op jit(solution)/shard_map/ppermute | solution.py:229
  70.4 25.8 %collective-permute-start.19 = (bf16[352,1024]{1,0:T(8,128)(2,1)}, bf16[352,1024]{1,0:T(8,128)(2,1)S(1)}, u32[]{:S(2)}, u32[]{:S(2)}) collective-permute-start(bf16[352,1024]{1,0:T(8,128)(2,1)} %get-tuple-element.51), channel_id=1, source_target_pairs={{0,16},{8,24},{16,0},{24,8},{1,17},{9,25},{17,1},{25,9},{2,18},{10... | collective-permute-start | bytes 2162696 | tf_op jit(solution)/shard_map/ppermute | solution.py:229
  74.6 3.5 %collective-permute-start.13 = (f32[512,64]{1,0:T(8,128)S(1)}, f32[512,64]{1,0:T(8,128)S(1)}, u32[]{:S(2)}, u32[]{:S(2)}) collective-permute-start(f32[512,64]{1,0:T(8,128)S(1)} %through_last.1), channel_id=1, source_target_pairs={{0,8},{8,0},{16,24},{24,16},{1,9},{9,1},{17,25},{25,17},{2,10},{10... | collective-permute-start | bytes 393224 | tf_op jit(solution)/shard_map/ppermute | solution.py:229
  74.7 14.3 %collective-permute-start.12 = (bf16[160,1024]{1,0:T(8,128)(2,1)S(1)}, bf16[160,1024]{1,0:T(8,128)(2,1)S(1)}, u32[]{:S(2)}, u32[]{:S(2)}) collective-permute-start(bf16[160,1024]{1,0:T(8,128)(2,1)S(1)} %get-tuple-element.49), channel_id=1, source_target_pairs={{2,0},{4,2},{6,4},{7,6},{5,7},{3,5},{1,3},{0,1},{10,8},{12,10},{14... | collective-permute-start | bytes 983048 | tf_op jit(solution)/shard_map/ppermute | solution.py:226
  77.1 12.6 %collective-permute-start.11 = (bf16[176,1024]{1,0:T(8,128)(2,1)S(1)}, bf16[176,1024]{1,0:T(8,128)(2,1)}, u32[]{:S(2)}, u32[]{:S(2)}) collective-permute-start(bf16[176,1024]{1,0:T(8,128)(2,1)S(1)} %get-tuple-element.48), channel_id=1, source_target_pairs={{0,2},{2,4},{4,6},{6,7},{7,5},{5,3},{3,1},{1,0},{8,10},{10,12},{12... | collective-permute-start | bytes 1081352 | tf_op jit(solution)/shard_map/ppermute | solution.py:223
  77.4 2.9 %copy-start.11 = (f32[64,2048]{1,0:T(8,128)}, f32[64,2048]{1,0:T(8,128)S(1)}, u32[]{:S(2)}) copy-start(f32[64,2048]{1,0:T(8,128)S(1)} %convert_add_fusion.1) | copy-start | bytes 1572868
  78.2 2.1 %copy-start.18 = (bf16[512,64]{1,0:T(8,128)(2,1)}, bf16[512,64]{1,0:T(8,128)(2,1)S(1)}, u32[]{:S(2)}) copy-start(bf16[512,64]{1,0:T(8,128)(2,1)S(1)} %fusion.2) | copy-start | bytes 196612
  78.5 10.6 %collective-permute-start.14 = (f32[64,256]{1,0:T(8,128)S(1)}, f32[64,256]{1,0:T(8,128)S(1)}, u32[]{:S(2)}, u32[]{:S(2)}) collective-permute-start(f32[64,256]{1,0:T(8,128)S(1)} %fusion.3), channel_id=1, source_target_pairs={{0,1},{1,0},{2,3},{3,2},{4,5},{5,4},{6,7},{7,6},{8,9},{9,8},{10,11... | collective-permute-start | bytes 196616 | tf_op jit(solution)/shard_map/ppermute | solution.py:229
  84.5 1.0 copy-start.5
  89.0 0.7 copy-start.9
  89.8 6.5 %collective-permute-start.18 = (bf16[64,1024]{1,0:T(8,128)(2,1)}, bf16[64,1024]{1,0:T(8,128)(2,1)S(1)}, u32[]{:S(2)}, u32[]{:S(2)}) collective-permute-start(bf16[64,1024]{1,0:T(8,128)(2,1)} %dynamic-slice_convert_fusion.1), channel_id=1, source_target_pairs={{0,2},{1,3},{2,0},{3,1},{4,6},{5,7},{6,4},{7,5},{8,10},{9,11},{10,... | collective-permute-start | bytes 393224 | tf_op jit(solution)/shard_map/ppermute | solution.py:229
  89.8 6.4 %collective-permute-start.17 = (f32[64,256]{1,0:T(8,128)S(1)}, f32[64,256]{1,0:T(8,128)S(1)}, u32[]{:S(2)}, u32[]{:S(2)}) collective-permute-start(f32[64,256]{1,0:T(8,128)S(1)} %add.93), channel_id=1, source_target_pairs={{0,2},{1,3},{2,0},{3,1},{4,6},{5,7},{6,4},{7,5},{8,10},{9,11},{10,... | collective-permute-start | bytes 196616 | tf_op jit(solution)/shard_map/ppermute | solution.py:229
  91.8 13.3 %collective-permute-start.22 = (bf16[176,1024]{1,0:T(8,128)(2,1)}, bf16[176,1024]{1,0:T(8,128)(2,1)S(1)}, u32[]{:S(2)}, u32[]{:S(2)}) collective-permute-start(bf16[176,1024]{1,0:T(8,128)(2,1)} %collective-permute-done.11.refs_0_), channel_id=1, source_target_pairs={{0,16},{8,24},{16,0},{24,8},{1,17},{9,25},{17,1},{25,9},{2,18},{10... | collective-permute-start | bytes 1081352 | tf_op jit(solution)/shard_map/ppermute | solution.py:229
  97.3 8.5 %copy-start.10 = (bf16[160,1024]{1,0:T(8,128)(2,1)S(1)}, bf16[160,1024]{1,0:T(8,128)(2,1)}, u32[]{:S(2)}) copy-start(bf16[160,1024]{1,0:T(8,128)(2,1)} %copy-done.9) | copy-start | bytes 983044
  97.3 7.8 %collective-permute-start.21 = (bf16[64,512]{1,0:T(8,128)(2,1)S(1)}, bf16[64,512]{1,0:T(8,128)(2,1)S(1)}, u32[]{:S(2)}, u32[]{:S(2)}) collective-permute-start(bf16[64,512]{1,0:T(8,128)(2,1)S(1)} %dynamic-slice_convert_fusion.2), channel_id=1, source_target_pairs={{0,4},{1,5},{2,6},{3,7},{4,0},{5,1},{6,2},{7,3},{8,12},{9,13},{10,... | collective-permute-start | bytes 196616 | tf_op jit(solution)/shard_map/ppermute | solution.py:229
  98.5 6.5 %collective-permute-start.20 = (f32[64,256]{1,0:T(8,128)S(1)}, f32[64,256]{1,0:T(8,128)S(1)}, u32[]{:S(2)}, u32[]{:S(2)}) collective-permute-start(f32[64,256]{1,0:T(8,128)S(1)} %add.99), channel_id=1, source_target_pairs={{0,4},{1,5},{2,6},{3,7},{4,0},{5,1},{6,2},{7,3},{8,12},{9,13},{10,... | collective-permute-start | bytes 196616 | tf_op jit(solution)/shard_map/ppermute | solution.py:229
  105.1 5.7 %collective-permute-start.23 = (f32[64,768]{1,0:T(8,128)S(1)}, f32[64,768]{1,0:T(8,128)S(1)}, u32[]{:S(2)}, u32[]{:S(2)}) collective-permute-start(f32[64,768]{1,0:T(8,128)S(1)} %pad_maximum_fusion.4), channel_id=1, source_target_pairs={{0,16},{8,24},{16,0},{24,8},{1,17},{9,25},{17,1},{25,9},{2,18},{10... | collective-permute-start | bytes 589832 | tf_op jit(solution)/shard_map/ppermute | solution.py:229
  111.0 3.9 %collective-permute-start.24 = (f32[256,512]{1,0:T(8,128)S(1)}, f32[256,512]{1,0:T(8,128)S(1)}, u32[]{:S(2)}, u32[]{:S(2)}) collective-permute-start(f32[256,512]{1,0:T(8,128)S(1)} %slice.61), channel_id=1, source_target_pairs={{0,8},{8,0},{16,24},{24,16},{1,9},{9,1},{17,25},{25,17},{2,10},{10... | collective-permute-start | bytes 1572872 | tf_op jit(solution)/shard_map/ppermute | solution.py:229
  111.1 2.3 %collective-permute-start.25 = (f32[64,1280]{1,0:T(8,128)S(1)}, f32[64,1280]{1,0:T(8,128)S(1)}, u32[]{:S(2)}, u32[]{:S(2)}) collective-permute-start(f32[64,1280]{1,0:T(8,128)S(1)} %pad_maximum_fusion.3.mine), channel_id=1, source_target_pairs={{0,8},{8,0},{16,24},{24,16},{1,9},{9,1},{17,25},{25,17},{2,10},{10... | collective-permute-start | bytes 983048 | tf_op jit(solution)/shard_map/ppermute | solution.py:229
  114.8 0.8 copy-start.15
  114.8 0.9 copy-start.19

commit v4 on v2

--- a/solution.py
+++ b/solution.py
@@ -252,7 +252,7 @@
         info = jnp.concatenate([jnp.stack([core, x]), shard_of, flipped]).astype(jnp.int32)
 
         my_quant = lax.dynamic_slice_in_dim(quant, core * part, part, 1)
-        my_scales = lax.dynamic_slice_in_dim(scales, core * (part // BLOCK), part // BLOCK, 1)
+        my_scales = jnp.where(core == 0, scales[:, : part // BLOCK], scales[:, part // BLOCK :])
         my_up = lax.dynamic_slice_in_dim(adapter_up, core * part, part, 1)
         weight = (
             my_quant.astype(F32) * jnp.repeat(jnp.repeat(my_scales, BLOCK, axis=0), BLOCK, axis=1)

time: 116 us -> 116 us (level)
  no operation moved by 1% of the time
where the time goes in v4:
time: 116 us; the launch traced here: 115 us
  Pallas kernels  37.5 us (32%)
  starting transfers between devices  35.2 us (30%)
  waiting for transfers between devices  26.9 us (23%)
  local copies, waits for them, and re-layouts  7.8 us (7%)
  other arithmetic  5.15 us (4%)
  matrix products  1.52 us (1%)
    pallas_call x7, Pallas kernels, products(): pl.pallas_call(body, grid_spec=pltpu.PrefetchScalarGridSpec(num_scalar_pr...  27 us
    ppermute x17, waiting for transfers between devices, over(): lax.ppermute(a, axis, [(i, i ^ bit) for i in range(mesh.shape[axis])])  22 us
    ppermute x17, starting transfers between devices, over(): lax.ppermute(a, axis, [(i, i ^ bit) for i in range(mesh.shape[axis])])  20.4 us
    pallas_call x1, Pallas kernels, terms_b(): pl.pallas_call(body, grid_spec=pltpu.PrefetchScalarGridSpec(num_scalar_pr...  8.17 us
    ppermute x4, starting transfers between devices, backward(): lax.ppermute(a, 'fsdp', [(order[(i + 1) % n], order[i]) for i in range(n)])  6.36 us
    ppermute x4, starting transfers between devices, forward(): lax.ppermute(a, 'fsdp', [(order[i], order[(i + 1) % n]) for i in range(n)])  4.84 us
    ppermute x1, starting transfers between devices, shards(): lax.ppermute(together(my_up, chunks[1])[0], 'fsdp', [(order[i], order[(i...  3.61 us
    ppermute x4, waiting for transfers between devices, forward(): lax.ppermute(a, 'fsdp', [(order[i], order[(i + 1) % n]) for i in range(n)])  3.54 us
  transfers between devices with their start and end apart: 26, of which 12 were waited for; matrix products, arithmetic and copies ran while one was open for 9% of the time, Pallas kernels for 33%

profile of v4, /device:TPU:0, one launch (start us, length us, event | category | flops | bytes accessed | tf_op | source)
XLA Modules:
  0.0 115.2 jit_solution(10735330322305969332)
XLA Ops:
  0.7 0.5 collective-permute-start.2
  1.2 0.9 slice_select_fusion.4
  2.1 0.6 broadcast_in_dim.7
  2.7 0.6 fusion
  3.4 0.8 broadcast_select_fusion
  4.3 2.6 %collective-permute-start.1 = (bf16[384,1024]{1,0:T(8,128)(2,1)S(1)}, bf16[384,1024]{1,0:T(8,128)(2,1)S(1)}, u32[]{:S(2)}, u32[]{:S(2)}) collective-permute-start(bf16[384,1024]{1,0:T(8,128)(2,1)S(1)} %pad_maximum_fusion.refs_0_), channel_id=1, source_target_pairs={{2,0},{4,2},{6,4},{7,6},{5,7},{3,5},{1,3},{0,1},{10,8},{12,10},{14... | collective-permute-start | bytes 2359304 | tf_op jit(solution)/shard_map/ppermute | solution.py:226
  6.9 0.1 collective-permute-start
  7.3 0.2 convolution_convert_fusion.1.low
  7.5 6.9 %collective-permute-done.3 = bf16[256,512]{1,0:T(8,128)(2,1)S(1)} collective-permute-done((bf16[256,512]{1,0:T(8,128)(2,1)S(1)}, bf16[256,512]{1,0:T(8,128)(2,1)S(1)}, u32[]{:S(2)}, u32[]{:S(2)}) %collective-permute-start.3) | collective-permute-done | bytes 262176 | tf_op jit(solution)/shard_map/ppermute | solution.py:229
  14.3 0.2 convolution_convert_fusion.low_partner
  14.5 8.2 %terms_b.1 = (f32[64,4096]{1,0:T(8,128)S(1)}, bf16[64,4096]{1,0:T(8,128)(2,1)}) custom-call(s32[18]{0:T(128)S(1)} %pad_add_fusion.info, bf16[256,16384]{1,0:T(8,128)(2,1)} %mine.15, bf16[256,16384]{1,0:T(8,128)(2,1)} %collective-permute-done.2.partner, bf16[64,256]{1,0:T(8,128)(2,1)S(1)} %convolution_convert_fusion.1.low, ...), custom_call_target="tpu_custom_call" | custom-call | flops 536870912 | bytes 8388608 | tf_op jit(solution)/shard_map/terms_b/pallas_call | solution.py:92
  22.7 1.0 copy-done.7
  23.7 1.4 %collective-permute-done.1.refs_2_.refs_4_ = bf16[384,1024]{1,0:T(8,128)(2,1)S(1)} collective-permute-done((bf16[384,1024]{1,0:T(8,128)(2,1)S(1)}, bf16[384,1024]{1,0:T(8,128)(2,1)S(1)}, u32[]{:S(2)}, u32[]{:S(2)}) %collective-permute-start.1) | collective-permute-done | bytes 786464 | tf_op jit(solution)/shard_map/ppermute | solution.py:226
  25.1 1.4 %collective-permute-done.refs_1_.refs_2_ = bf16[384,1024]{1,0:T(8,128)(2,1)S(1)} collective-permute-done((bf16[384,1024]{1,0:T(8,128)(2,1)S(1)}, bf16[384,1024]{1,0:T(8,128)(2,1)S(1)}, u32[]{:S(2)}, u32[]{:S(2)}) %collective-permute-start) | collective-permute-done | bytes 786464 | tf_op jit(solution)/shard_map/ppermute | solution.py:223
  26.5 0.4 collective-permute-start.4
  26.9 1.6 %collective-permute-start.6 = (bf16[384,1024]{1,0:T(8,128)(2,1)S(1)}, bf16[384,1024]{1,0:T(8,128)(2,1)}, u32[]{:S(2)}, u32[]{:S(2)}) collective-permute-start(bf16[384,1024]{1,0:T(8,128)(2,1)S(1)} %collective-permute-done.1.refs_2_.refs_4_), channel_id=1, source_target_pairs={{2,0},{4,2},{6,4},{7,6},{5,7},{3,5},{1,3},{0,1},{10,8},{12,10},{14... | collective-permute-start | bytes 2359304 | tf_op jit(solution)/shard_map/ppermute | solution.py:226
  28.5 1.5 %collective-permute-start.8 = (bf16[64,4096]{1,0:T(8,128)(2,1)}, bf16[64,4096]{1,0:T(8,128)(2,1)}, u32[]{:S(2)}, u32[]{:S(2)}) collective-permute-start(bf16[64,4096]{1,0:T(8,128)(2,1)} %get-tuple-element.39), channel_id=1, source_target_pairs={{0,16},{8,24},{16,0},{24,8},{1,17},{9,25},{17,1},{25,9},{2,18},{10... | collective-permute-start | bytes 1572872 | tf_op jit(solution)/shard_map/ppermute | solution.py:229
  30.0 0.9 constant_dynamic-slice_fusion.1
  30.9 0.9 constant_dynamic-slice_fusion
  31.8 3.6 %collective-permute-start.10 = (bf16[64,1024]{1,0:T(8,128)(2,1)}, bf16[64,1024]{1,0:T(8,128)(2,1)S(1)}, u32[]{:S(2)}, u32[]{:S(2)}) collective-permute-start(bf16[64,1024]{1,0:T(8,128)(2,1)} %copy-done.16), channel_id=1, source_target_pairs={{0,7},{2,5},{4,3},{6,1},{7,0},{5,2},{3,4},{1,6},{8,15},{10,13},{12... | collective-permute-start | bytes 393224 | tf_op jit(solution)/shard_map/ppermute | solution.py:288
  35.4 3.9 %through_first.1.refs_3_ = f32[512,64]{1,0:T(8,128)S(1)} custom-call(s32[18]{0:T(128)S(1)} %pad_add_fusion.info, bf16[256,16384]{1,0:T(8,128)(2,1)} %mine.15, bf16[256,16384]{1,0:T(8,128)(2,1)} %collective-permute-done.2.partner, bf16[384,1024]{1,0:T(8,128)(2,1)S(1)} %pad_maximum_fusion.refs_0_, bf16[384,1024]{1,0:T(8,128)(2,1)S(1)} %collective-permute-done.refs_1_.refs_2_, ...), custom_call_target="tpu_custom_call" | custom-call | flops 201326592 | bytes 3670016 | tf_op jit(solution)/shard_map/through_first/pallas_call | solution.py:151
  39.4 2.0 %collective-permute-done.8 = bf16[64,4096]{1,0:T(8,128)(2,1)} collective-permute-done((bf16[64,4096]{1,0:T(8,128)(2,1)}, bf16[64,4096]{1,0:T(8,128)(2,1)}, u32[]{:S(2)}, u32[]{:S(2)}) %collective-permute-start.8) | collective-permute-done | bytes 524320 | tf_op jit(solution)/shard_map/ppermute | solution.py:229
  41.5 1.6 %collective-permute-start.9 = (bf16[384,1024]{1,0:T(8,128)(2,1)S(1)}, bf16[384,1024]{1,0:T(8,128)(2,1)S(1)}, u32[]{:S(2)}, u32[]{:S(2)}) collective-permute-start(bf16[384,1024]{1,0:T(8,128)(2,1)S(1)} %pad_maximum_fusion.1), channel_id=1, source_target_pairs={{0,16},{8,24},{16,0},{24,8},{1,17},{9,25},{17,1},{25,9},{2,18},{10... | collective-permute-start | bytes 2359304 | tf_op jit(solution)/shard_map/ppermute | solution.py:229
  43.0 2.1 %collective-permute-done.4.refs_0_ = bf16[384,1024]{1,0:T(8,128)(2,1)S(1)} collective-permute-done((bf16[384,1024]{1,0:T(8,128)(2,1)S(1)}, bf16[384,1024]{1,0:T(8,128)(2,1)S(1)}, u32[]{:S(2)}, u32[]{:S(2)}) %collective-permute-start.4) | collective-permute-done | bytes 786464 | tf_op jit(solution)/shard_map/ppermute | solution.py:223
  45.2 4.0 %collective-permute-start.5 = (bf16[384,1024]{1,0:T(8,128)(2,1)S(1)}, bf16[384,1024]{1,0:T(8,128)(2,1)S(1)}, u32[]{:S(2)}, u32[]{:S(2)}) collective-permute-start(bf16[384,1024]{1,0:T(8,128)(2,1)S(1)} %collective-permute-done.4.refs_0_), channel_id=1, source_target_pairs={{0,2},{2,4},{4,6},{6,7},{7,5},{5,3},{3,1},{1,0},{8,10},{10,12},{12... | collective-permute-start | bytes 2359304 | tf_op jit(solution)/shard_map/ppermute | solution.py:223
  49.1 1.2 %convert_add_fusion = f32[64,4096]{1,0:T(8,128)S(1)} fusion(f32[64,4096]{1,0:T(8,128)S(1)} %copy-done.8, bf16[64,4096]{1,0:T(8,128)(2,1)} %collective-permute-done.8), kind=kLoop, calls=%fused_computation.4 | loop fusion | flops 524288 | bytes 2621440 | tf_op jit(solution)/shard_map/add | solution.py:324
  50.3 3.3 %collective-permute-start.15 = (bf16[64,2048]{1,0:T(8,128)(2,1)S(1)}, bf16[64,2048]{1,0:T(8,128)(2,1)S(1)}, u32[]{:S(2)}, u32[]{:S(2)}) collective-permute-start(bf16[64,2048]{1,0:T(8,128)(2,1)S(1)} %dynamic-slice_convert_fusion), channel_id=1, source_target_pairs={{0,1},{1,0},{2,3},{3,2},{4,5},{5,4},{6,7},{7,6},{8,9},{9,8},{10,11... | collective-permute-start | bytes 786440 | tf_op jit(solution)/shard_map/ppermute | solution.py:229
  53.6 1.0 slice.82
  54.8 1.6 %collective-permute-start.16 = (bf16[384,1024]{1,0:T(8,128)(2,1)S(1)}, bf16[384,1024]{1,0:T(8,128)(2,1)S(1)}, u32[]{:S(2)}, u32[]{:S(2)}) collective-permute-start(bf16[384,1024]{1,0:T(8,128)(2,1)S(1)} %pad_maximum_fusion.2), channel_id=1, source_target_pairs={{0,16},{8,24},{16,0},{24,8},{1,17},{9,25},{17,1},{25,9},{2,18},{10... | collective-permute-start | bytes 2359304 | tf_op jit(solution)/shard_map/ppermute | solution.py:229
  56.3 4.0 %through_second.1.refs_2_ = f32[512,64]{1,0:T(8,128)S(1)} custom-call(s32[18]{0:T(128)S(1)} %pad_add_fusion.info, bf16[256,16384]{1,0:T(8,128)(2,1)} %mine.15, bf16[256,16384]{1,0:T(8,128)(2,1)} %collective-permute-done.2.partner, bf16[384,1024]{1,0:T(8,128)(2,1)S(1)} %collective-permute-done.4.refs_0_, ...), custom_call_target="tpu_custom_call" | custom-call | flops 201326592 | bytes 3670016 | tf_op jit(solution)/shard_map/through_second/pallas_call | solution.py:151
  60.3 1.7 %collective-permute-done.9.refs_3_.refs_5_ = bf16[384,1024]{1,0:T(8,128)(2,1)S(1)} collective-permute-done((bf16[384,1024]{1,0:T(8,128)(2,1)S(1)}, bf16[384,1024]{1,0:T(8,128)(2,1)S(1)}, u32[]{:S(2)}, u32[]{:S(2)}) %collective-permute-start.9) | collective-permute-done | bytes 786464 | tf_op jit(solution)/shard_map/ppermute | solution.py:229
  62.0 5.7 %first.1.refs_4_ = f32[512,512]{1,0:T(8,128)} custom-call(s32[18]{0:T(128)S(1)} %pad_add_fusion.info, bf16[256,16384]{1,0:T(8,128)(2,1)} %mine.15, bf16[256,16384]{1,0:T(8,128)(2,1)} %collective-permute-done.2.partner, bf16[384,1024]{1,0:T(8,128)(2,1)S(1)} %pad_maximum_fusion.refs_0_, bf16[192,1024]{1,0:T(8,128)(2,1)S(1)} %copy-done.6, ...), custom_call_target="tpu_custom_call" | custom-call | flops 1610612736 | bytes 7340032 | tf_op jit(solution)/shard_map/first/pallas_call | solution.py:151
  67.7 0.9 assemble.1
  68.6 1.6 %collective-permute-start.19 = (bf16[384,1024]{1,0:T(8,128)(2,1)}, bf16[384,1024]{1,0:T(8,128)(2,1)S(1)}, u32[]{:S(2)}, u32[]{:S(2)}) collective-permute-start(bf16[384,1024]{1,0:T(8,128)(2,1)} %get-tuple-element.51), channel_id=1, source_target_pairs={{0,16},{8,24},{16,0},{24,8},{1,17},{9,25},{17,1},{25,9},{2,18},{10... | collective-permute-start | bytes 2359304 | tf_op jit(solution)/shard_map/ppermute | solution.py:229
  70.2 2.7 %through_last.1 = f32[512,64]{1,0:T(8,128)S(1)} custom-call(s32[18]{0:T(128)S(1)} %pad_add_fusion.info, bf16[256,16384]{1,0:T(8,128)(2,1)} %mine.15, bf16[256,16384]{1,0:T(8,128)(2,1)} %collective-permute-done.2.partner, bf16[384,1024]{1,0:T(8,128)(2,1)S(1)} %collective-permute-done.5.refs_0_.refs_2_, ...), custom_call_target="tpu_custom_call" | custom-call | flops 134217728 | bytes 2490368 | tf_op jit(solution)/shard_map/through_last/pallas_call | solution.py:151
  73.0 2.1 %collective-permute-start.12 = (bf16[128,1024]{1,0:T(8,128)(2,1)S(1)}, bf16[128,1024]{1,0:T(8,128)(2,1)S(1)}, u32[]{:S(2)}, u32[]{:S(2)}) collective-permute-start(bf16[128,1024]{1,0:T(8,128)(2,1)S(1)} %get-tuple-element.49), channel_id=1, source_target_pairs={{2,0},{4,2},{6,4},{7,6},{5,7},{3,5},{1,3},{0,1},{10,8},{12,10},{14... | collective-permute-start | bytes 786440 | tf_op jit(solution)/shard_map/ppermute | solution.py:226
  75.1 0.4 collective-permute-start.11
  75.6 0.7 dynamic-slice_convert_fusion.1
  76.4 0.2 fusion.3
  76.6 1.7 %collective-permute-start.14 = (f32[64,256]{1,0:T(8,128)S(1)}, f32[64,256]{1,0:T(8,128)S(1)}, u32[]{:S(2)}, u32[]{:S(2)}) collective-permute-start(f32[64,256]{1,0:T(8,128)S(1)} %fusion.3), channel_id=1, source_target_pairs={{0,1},{1,0},{2,3},{3,2},{4,5},{5,4},{6,7},{7,6},{8,9},{9,8},{10,11... | collective-permute-start | bytes 196616 | tf_op jit(solution)/shard_map/ppermute | solution.py:229
  78.3 0.6 collective-permute-done.16.refs_1_.refs_3_
  78.9 4.2 %middle.1.refs_4_ = f32[512,512]{1,0:T(8,128)S(1)} custom-call(s32[18]{0:T(128)S(1)} %pad_add_fusion.info, bf16[256,16384]{1,0:T(8,128)(2,1)} %mine.15, bf16[256,16384]{1,0:T(8,128)(2,1)} %collective-permute-done.2.partner, bf16[384,1024]{1,0:T(8,128)(2,1)S(1)} %collective-permute-done.4.refs_0_, ...), custom_call_target="tpu_custom_call" | custom-call | flops 1073741824 | bytes 5242880 | tf_op jit(solution)/shard_map/middle/pallas_call | solution.py:151
  83.1 1.0 copy-done.5
  84.0 3.7 %collective-permute-done.14 = f32[64,256]{1,0:T(8,128)S(1)} collective-permute-done((f32[64,256]{1,0:T(8,128)S(1)}, f32[64,256]{1,0:T(8,128)S(1)}, u32[]{:S(2)}, u32[]{:S(2)}) %collective-permute-start.14) | collective-permute-done | bytes 65568 | tf_op jit(solution)/shard_map/ppermute | solution.py:229
  87.8 0.7 copy-done.9
  88.5 2.0 %collective-permute-start.17 = (f32[64,256]{1,0:T(8,128)S(1)}, f32[64,256]{1,0:T(8,128)S(1)}, u32[]{:S(2)}, u32[]{:S(2)}) collective-permute-start(f32[64,256]{1,0:T(8,128)S(1)} %add.89), channel_id=1, source_target_pairs={{0,2},{1,3},{2,0},{3,1},{4,6},{5,7},{6,4},{7,5},{8,10},{9,11},{10,... | collective-permute-start | bytes 196616 | tf_op jit(solution)/shard_map/ppermute | solution.py:229
  90.5 0.6 collective-permute-start.22
  91.1 3.8 %collective-permute-done.17 = f32[64,256]{1,0:T(8,128)S(1)} collective-permute-done((f32[64,256]{1,0:T(8,128)S(1)}, f32[64,256]{1,0:T(8,128)S(1)}, u32[]{:S(2)}, u32[]{:S(2)}) %collective-permute-start.17) | collective-permute-done | bytes 65568 | tf_op jit(solution)/shard_map/ppermute | solution.py:229
  94.9 1.0 convert_add_fusion.2
  95.9 2.3 %collective-permute-start.21 = (bf16[64,512]{1,0:T(8,128)(2,1)S(1)}, bf16[64,512]{1,0:T(8,128)(2,1)S(1)}, u32[]{:S(2)}, u32[]{:S(2)}) collective-permute-start(bf16[64,512]{1,0:T(8,128)(2,1)S(1)} %dynamic-slice_convert_fusion.2), channel_id=1, source_target_pairs={{0,4},{1,5},{2,6},{3,7},{4,0},{5,1},{6,2},{7,3},{8,12},{9,13},{10,... | collective-permute-start | bytes 196616 | tf_op jit(solution)/shard_map/ppermute | solution.py:229
  98.3 0.7 collective-permute-start.20
  98.9 3.9 %late.1.refs_3_ = f32[512,512]{1,0:T(8,128)S(1)} custom-call(s32[18]{0:T(128)S(1)} %pad_add_fusion.info, bf16[256,16384]{1,0:T(8,128)(2,1)} %mine.15, bf16[256,16384]{1,0:T(8,128)(2,1)} %collective-permute-done.2.partner, bf16[384,1024]{1,0:T(8,128)(2,1)S(1)} %collective-permute-done.5.refs_0_.refs_2_, ...), custom_call_target="tpu_custom_call" | custom-call | flops 1073741824 | bytes 5242880 | tf_op jit(solution)/shard_map/late/pallas_call | solution.py:151
  102.9 0.5 collective-permute-done.20
  103.5 2.2 %collective-permute-start.23 = (f32[64,768]{1,0:T(8,128)S(1)}, f32[64,768]{1,0:T(8,128)S(1)}, u32[]{:S(2)}, u32[]{:S(2)}) collective-permute-start(f32[64,768]{1,0:T(8,128)S(1)} %pad_maximum_fusion.4), channel_id=1, source_target_pairs={{0,16},{8,24},{16,0},{24,8},{1,17},{9,25},{17,1},{25,9},{2,18},{10... | collective-permute-start | bytes 589832 | tf_op jit(solution)/shard_map/ppermute | solution.py:229
  105.8 2.6 %last.1 = f32[512,512]{1,0:T(8,128)S(1)} custom-call(s32[18]{0:T(128)S(1)} %pad_add_fusion.info, bf16[256,16384]{1,0:T(8,128)(2,1)} %mine.15, bf16[256,16384]{1,0:T(8,128)(2,1)} %collective-permute-done.2.partner, bf16[192,1024]{1,0:T(8,128)(2,1)} %collective-permute-done.11.refs_0_, bf16[128,1024]{1,0:T(8,128)(2,1)S(1)} %copy-done.10, ...), custom_call_target="tpu_custom_call" | custom-call | flops 536870912 | bytes 3145728 | tf_op jit(solution)/shard_map/last/pallas_call | solution.py:151
  108.4 1.0 collective-permute-done.23
  109.6 0.6 collective-permute-start.25
  110.2 1.8 %collective-permute-done.25.other = f32[64,1280]{1,0:T(8,128)S(1)} collective-permute-done((f32[64,1280]{1,0:T(8,128)S(1)}, f32[64,1280]{1,0:T(8,128)S(1)}, u32[]{:S(2)}, u32[]{:S(2)}) %collective-permute-start.25) | collective-permute-done | bytes 327712 | tf_op jit(solution)/shard_map/ppermute | solution.py:229
  112.0 1.4 %finish.1 = (f32[64,2048]{1,0:T(8,128)}, f32[64,512]{1,0:T(8,128)}) custom-call(s32[18]{0:T(128)S(1)} %pad_add_fusion.info, f32[1]{0:T(128)} %constant.66.clone.1.factor, f32[64,1280]{1,0:T(8,128)S(1)} %pad_maximum_fusion.3.mine, f32[64,1280]{1,0:T(8,128)S(1)} %collective-permute-done.25.other), custom_call_target="tpu_custom_call" | custom-call | bytes 1310720 | tf_op jit(solution)/shard_map/finish/pallas_call | solution.py:194
  113.4 0.1 slice_add_fusion
  113.5 0.1 slice.85
  113.6 0.1 slice_select_fusion.1
  113.7 0.6 copy-done.18
  114.3 0.9 fusion.1
  (80 shorter events, 1.1 us)
Async XLA Ops:
  0.6 2.7 %copy-start = (bf16[64,2048]{1,0:T(8,128)(2,1)S(1)}, bf16[64,2048]{1,0:T(8,128)(2,1)}, u32[]{:S(2)}) copy-start(bf16[64,2048]{1,0:T(8,128)(2,1)} %param.12) | copy-start | bytes 786436
  0.6 2.1 %copy-start.15 = (bf16[512,2048]{1,0:T(8,128)(2,1)S(1)}, bf16[512,2048]{1,0:T(8,128)(2,1)}, u32[]{:S(2)}) copy-start(bf16[512,2048]{1,0:T(8,128)(2,1)} %param.9) | copy-start | bytes 6291460
  0.7 13.9 %collective-permute-start.2 = (bf16[256,16384]{1,0:T(8,128)(2,1)}, bf16[256,16384]{1,0:T(8,128)(2,1)}, u32[]{:S(2)}, u32[]{:S(2)}) collective-permute-start(bf16[256,16384]{1,0:T(8,128)(2,1)} %mine.15), channel_id=1, source_target_pairs={{0,8},{8,0},{16,24},{24,16},{1,9},{9,1},{17,25},{25,17},{2,10},{10... | collective-permute-start | bytes 25165832 | tf_op jit(solution)/shard_map/ppermute | solution.py:229
  3.4 0.9 copy-start.16
  3.4 3.7 %copy-start.12 = (bf16[256,512]{1,0:T(8,128)(2,1)S(1)}, bf16[256,512]{1,0:T(8,128)(2,1)}, u32[]{:S(2)}) copy-start(bf16[256,512]{1,0:T(8,128)(2,1)} %param.7) | copy-start | bytes 786436
  3.4 3.8 %copy-start.19 = (s32[8]{0:T(128)S(1)}, s32[8]{0:T(128)}, u32[]{:S(2)}) copy-start(s32[8]{0:T(128)} %constant.67.clone) | copy-start | bytes 100
  3.4 3.8 %copy-start.14 = (bf16[512,64]{0,1:T(8,128)(2,1)S(1)}, bf16[512,64]{0,1:T(8,128)(2,1)}, u32[]{:S(2)}) copy-start(bf16[512,64]{0,1:T(8,128)(2,1)} %param.11) | copy-start | bytes 196612
  4.3 20.8 %collective-permute-start.1 = (bf16[384,1024]{1,0:T(8,128)(2,1)S(1)}, bf16[384,1024]{1,0:T(8,128)(2,1)S(1)}, u32[]{:S(2)}, u32[]{:S(2)}) collective-permute-start(bf16[384,1024]{1,0:T(8,128)(2,1)S(1)} %pad_maximum_fusion.refs_0_), channel_id=1, source_target_pairs={{2,0},{4,2},{6,4},{7,6},{5,7},{3,5},{1,3},{0,1},{10,8},{12,10},{14... | collective-permute-start | bytes 2359304 | tf_op jit(solution)/shard_map/ppermute | solution.py:226
  6.9 19.5 %collective-permute-start = (bf16[384,1024]{1,0:T(8,128)(2,1)S(1)}, bf16[384,1024]{1,0:T(8,128)(2,1)S(1)}, u32[]{:S(2)}, u32[]{:S(2)}) collective-permute-start(bf16[384,1024]{1,0:T(8,128)(2,1)S(1)} %pad_maximum_fusion.refs_0_), channel_id=1, source_target_pairs={{0,2},{2,4},{4,6},{6,7},{7,5},{5,3},{3,1},{1,0},{8,10},{10,12},{12... | collective-permute-start | bytes 2359304 | tf_op jit(solution)/shard_map/ppermute | solution.py:223
  7.1 7.3 %collective-permute-start.3 = (bf16[256,512]{1,0:T(8,128)(2,1)S(1)}, bf16[256,512]{1,0:T(8,128)(2,1)S(1)}, u32[]{:S(2)}, u32[]{:S(2)}) collective-permute-start(bf16[256,512]{1,0:T(8,128)(2,1)S(1)} %copy-done.12), channel_id=1, source_target_pairs={{0,8},{8,0},{16,24},{24,16},{1,9},{9,1},{17,25},{25,17},{2,10},{10... | collective-permute-start | bytes 786440 | tf_op jit(solution)/shard_map/ppermute | solution.py:229
  14.3 8.4 %copy-start.13 = (bf16[256,512]{1,0:T(8,128)(2,1)}, bf16[256,512]{1,0:T(8,128)(2,1)S(1)}, u32[]{:S(2)}) copy-start(bf16[256,512]{1,0:T(8,128)(2,1)S(1)} %collective-permute-done.3) | copy-start | bytes 786436
  22.7 1.0 copy-start.7
  25.1 16.3 %copy-start.1 = (bf16[384,1024]{1,0:T(8,128)(2,1)}, bf16[384,1024]{1,0:T(8,128)(2,1)S(1)}, u32[]{:S(2)}) copy-start(bf16[384,1024]{1,0:T(8,128)(2,1)S(1)} %collective-permute-done.1.refs_2_.refs_4_) | copy-start | bytes 2359300
  26.5 14.9 %copy-start.3 = (bf16[384,1024]{1,0:T(8,128)(2,1)}, bf16[384,1024]{1,0:T(8,128)(2,1)S(1)}, u32[]{:S(2)}) copy-start(bf16[384,1024]{1,0:T(8,128)(2,1)S(1)} %collective-permute-done.refs_1_.refs_2_) | copy-start | bytes 2359300
  26.5 18.7 %collective-permute-start.4 = (bf16[384,1024]{1,0:T(8,128)(2,1)S(1)}, bf16[384,1024]{1,0:T(8,128)(2,1)S(1)}, u32[]{:S(2)}, u32[]{:S(2)}) collective-permute-start(bf16[384,1024]{1,0:T(8,128)(2,1)S(1)} %collective-permute-done.refs_1_.refs_2_), channel_id=1, source_target_pairs={{0,2},{2,4},{4,6},{6,7},{7,5},{5,3},{3,1},{1,0},{8,10},{10,12},{12... | collective-permute-start | bytes 2359304 | tf_op jit(solution)/shard_map/ppermute | solution.py:223
  26.9 22.2 %collective-permute-start.6 = (bf16[384,1024]{1,0:T(8,128)(2,1)S(1)}, bf16[384,1024]{1,0:T(8,128)(2,1)}, u32[]{:S(2)}, u32[]{:S(2)}) collective-permute-start(bf16[384,1024]{1,0:T(8,128)(2,1)S(1)} %collective-permute-done.1.refs_2_.refs_4_), channel_id=1, source_target_pairs={{2,0},{4,2},{6,4},{7,6},{5,7},{3,5},{1,3},{0,1},{10,8},{12,10},{14... | collective-permute-start | bytes 2359304 | tf_op jit(solution)/shard_map/ppermute | solution.py:226
  28.5 12.8 %collective-permute-start.8 = (bf16[64,4096]{1,0:T(8,128)(2,1)}, bf16[64,4096]{1,0:T(8,128)(2,1)}, u32[]{:S(2)}, u32[]{:S(2)}) collective-permute-start(bf16[64,4096]{1,0:T(8,128)(2,1)} %get-tuple-element.39), channel_id=1, source_target_pairs={{0,16},{8,24},{16,0},{24,8},{1,17},{9,25},{17,1},{25,9},{2,18},{10... | collective-permute-start | bytes 1572872 | tf_op jit(solution)/shard_map/ppermute | solution.py:229
  31.8 22.9 %collective-permute-start.10 = (bf16[64,1024]{1,0:T(8,128)(2,1)}, bf16[64,1024]{1,0:T(8,128)(2,1)S(1)}, u32[]{:S(2)}, u32[]{:S(2)}) collective-permute-start(bf16[64,1024]{1,0:T(8,128)(2,1)} %copy-done.16), channel_id=1, source_target_pairs={{0,7},{2,5},{4,3},{6,1},{7,0},{5,2},{3,4},{1,6},{8,15},{10,13},{12... | collective-permute-start | bytes 393224 | tf_op jit(solution)/shard_map/ppermute | solution.py:288
  39.4 9.8 %copy-start.8 = (f32[64,4096]{1,0:T(8,128)S(1)}, f32[64,4096]{1,0:T(8,128)}, u32[]{:S(2)}) copy-start(f32[64,4096]{1,0:T(8,128)} %copy-done.7) | copy-start | bytes 3145732
  41.5 20.5 %collective-permute-start.9 = (bf16[384,1024]{1,0:T(8,128)(2,1)S(1)}, bf16[384,1024]{1,0:T(8,128)(2,1)S(1)}, u32[]{:S(2)}, u32[]{:S(2)}) collective-permute-start(bf16[384,1024]{1,0:T(8,128)(2,1)S(1)} %pad_maximum_fusion.1), channel_id=1, source_target_pairs={{0,16},{8,24},{16,0},{24,8},{1,17},{9,25},{17,1},{25,9},{2,18},{10... | collective-permute-start | bytes 2359304 | tf_op jit(solution)/shard_map/ppermute | solution.py:229
  45.2 22.5 %collective-permute-start.5 = (bf16[384,1024]{1,0:T(8,128)(2,1)S(1)}, bf16[384,1024]{1,0:T(8,128)(2,1)S(1)}, u32[]{:S(2)}, u32[]{:S(2)}) collective-permute-start(bf16[384,1024]{1,0:T(8,128)(2,1)S(1)} %collective-permute-done.4.refs_0_), channel_id=1, source_target_pairs={{0,2},{2,4},{4,6},{6,7},{7,5},{5,3},{3,1},{1,0},{8,10},{10,12},{12... | collective-permute-start | bytes 2359304 | tf_op jit(solution)/shard_map/ppermute | solution.py:223
  49.1 18.6 %collective-permute-start.7 = (bf16[384,1024]{1,0:T(8,128)(2,1)}, bf16[384,1024]{1,0:T(8,128)(2,1)S(1)}, u32[]{:S(2)}, u32[]{:S(2)}) collective-permute-start(bf16[384,1024]{1,0:T(8,128)(2,1)} %collective-permute-done.6.refs_1_.refs_2_), channel_id=1, source_target_pairs={{2,0},{4,2},{6,4},{7,6},{5,7},{3,5},{1,3},{0,1},{10,8},{12,10},{14... | collective-permute-start | bytes 2359304 | tf_op jit(solution)/shard_map/ppermute | solution.py:226
  50.3 22.7 %collective-permute-start.15 = (bf16[64,2048]{1,0:T(8,128)(2,1)S(1)}, bf16[64,2048]{1,0:T(8,128)(2,1)S(1)}, u32[]{:S(2)}, u32[]{:S(2)}) collective-permute-start(bf16[64,2048]{1,0:T(8,128)(2,1)S(1)} %dynamic-slice_convert_fusion), channel_id=1, source_target_pairs={{0,1},{1,0},{2,3},{3,2},{4,5},{5,4},{6,7},{7,6},{8,9},{9,8},{10,11... | collective-permute-start | bytes 786440 | tf_op jit(solution)/shard_map/ppermute | solution.py:229
  54.7 7.3 %copy-start.2 = (bf16[384,1024]{1,0:T(8,128)(2,1)S(1)}, bf16[384,1024]{1,0:T(8,128)(2,1)}, u32[]{:S(2)}) copy-start(bf16[384,1024]{1,0:T(8,128)(2,1)} %copy-done.1) | copy-start | bytes 2359300
  54.7 7.3 %copy-start.4 = (bf16[384,1024]{1,0:T(8,128)(2,1)S(1)}, bf16[384,1024]{1,0:T(8,128)(2,1)}, u32[]{:S(2)}) copy-start(bf16[384,1024]{1,0:T(8,128)(2,1)} %copy-done.3) | copy-start | bytes 2359300
  54.7 7.3 %copy-start.6 = (bf16[192,1024]{1,0:T(8,128)(2,1)S(1)}, bf16[192,1024]{1,0:T(8,128)(2,1)}, u32[]{:S(2)}) copy-start(bf16[192,1024]{1,0:T(8,128)(2,1)} %get-tuple-element.77.refs_1_) | copy-start | bytes 1179652
  54.8 24.1 %collective-permute-start.16 = (bf16[384,1024]{1,0:T(8,128)(2,1)S(1)}, bf16[384,1024]{1,0:T(8,128)(2,1)S(1)}, u32[]{:S(2)}, u32[]{:S(2)}) collective-permute-start(bf16[384,1024]{1,0:T(8,128)(2,1)S(1)} %pad_maximum_fusion.2), channel_id=1, source_target_pairs={{0,16},{8,24},{16,0},{24,8},{1,17},{9,25},{17,1},{25,9},{2,18},{10... | collective-permute-start | bytes 2359304 | tf_op jit(solution)/shard_map/ppermute | solution.py:229
  68.6 26.3 %collective-permute-start.19 = (bf16[384,1024]{1,0:T(8,128)(2,1)}, bf16[384,1024]{1,0:T(8,128)(2,1)S(1)}, u32[]{:S(2)}, u32[]{:S(2)}) collective-permute-start(bf16[384,1024]{1,0:T(8,128)(2,1)} %get-tuple-element.51), channel_id=1, source_target_pairs={{0,16},{8,24},{16,0},{24,8},{1,17},{9,25},{17,1},{25,9},{2,18},{10... | collective-permute-start | bytes 2359304 | tf_op jit(solution)/shard_map/ppermute | solution.py:229
  72.9 3.4 %collective-permute-start.13 = (f32[512,64]{1,0:T(8,128)S(1)}, f32[512,64]{1,0:T(8,128)S(1)}, u32[]{:S(2)}, u32[]{:S(2)}) collective-permute-start(f32[512,64]{1,0:T(8,128)S(1)} %through_last.1), channel_id=1, source_target_pairs={{0,8},{8,0},{16,24},{24,16},{1,9},{9,1},{17,25},{25,17},{2,10},{10... | collective-permute-start | bytes 393224 | tf_op jit(solution)/shard_map/ppermute | solution.py:229
  73.0 14.7 %collective-permute-start.12 = (bf16[128,1024]{1,0:T(8,128)(2,1)S(1)}, bf16[128,1024]{1,0:T(8,128)(2,1)S(1)}, u32[]{:S(2)}, u32[]{:S(2)}) collective-permute-start(bf16[128,1024]{1,0:T(8,128)(2,1)S(1)} %get-tuple-element.49), channel_id=1, source_target_pairs={{2,0},{4,2},{6,4},{7,6},{5,7},{3,5},{1,3},{0,1},{10,8},{12,10},{14... | collective-permute-start | bytes 786440 | tf_op jit(solution)/shard_map/ppermute | solution.py:226
  75.1 13.3 %collective-permute-start.11 = (bf16[192,1024]{1,0:T(8,128)(2,1)S(1)}, bf16[192,1024]{1,0:T(8,128)(2,1)}, u32[]{:S(2)}, u32[]{:S(2)}) collective-permute-start(bf16[192,1024]{1,0:T(8,128)(2,1)S(1)} %get-tuple-element.48), channel_id=1, source_target_pairs={{0,2},{2,4},{4,6},{6,7},{7,5},{5,3},{3,1},{1,0},{8,10},{10,12},{12... | collective-permute-start | bytes 1179656 | tf_op jit(solution)/shard_map/ppermute | solution.py:223
  75.6 2.8 %copy-start.11 = (f32[64,2048]{1,0:T(8,128)}, f32[64,2048]{1,0:T(8,128)S(1)}, u32[]{:S(2)}) copy-start(f32[64,2048]{1,0:T(8,128)S(1)} %convert_add_fusion.1) | copy-start | bytes 1572868
  76.4 1.9 %copy-start.17 = (bf16[512,64]{1,0:T(8,128)(2,1)}, bf16[512,64]{1,0:T(8,128)(2,1)S(1)}, u32[]{:S(2)}) copy-start(bf16[512,64]{1,0:T(8,128)(2,1)S(1)} %fusion.2) | copy-start | bytes 196612
  76.6 11.1 %collective-permute-start.14 = (f32[64,256]{1,0:T(8,128)S(1)}, f32[64,256]{1,0:T(8,128)S(1)}, u32[]{:S(2)}, u32[]{:S(2)}) collective-permute-start(f32[64,256]{1,0:T(8,128)S(1)} %fusion.3), channel_id=1, source_target_pairs={{0,1},{1,0},{2,3},{3,2},{4,5},{5,4},{6,7},{7,6},{8,9},{9,8},{10,11... | collective-permute-start | bytes 196616 | tf_op jit(solution)/shard_map/ppermute | solution.py:229
  83.1 1.0 copy-start.5
  87.7 0.7 copy-start.9
  88.4 6.5 %collective-permute-start.18 = (bf16[64,1024]{1,0:T(8,128)(2,1)}, bf16[64,1024]{1,0:T(8,128)(2,1)S(1)}, u32[]{:S(2)}, u32[]{:S(2)}) collective-permute-start(bf16[64,1024]{1,0:T(8,128)(2,1)} %dynamic-slice_convert_fusion.1), channel_id=1, source_target_pairs={{0,2},{1,3},{2,0},{3,1},{4,6},{5,7},{6,4},{7,5},{8,10},{9,11},{10,... | collective-permute-start | bytes 393224 | tf_op jit(solution)/shard_map/ppermute | solution.py:229
  88.5 6.4 %collective-permute-start.17 = (f32[64,256]{1,0:T(8,128)S(1)}, f32[64,256]{1,0:T(8,128)S(1)}, u32[]{:S(2)}, u32[]{:S(2)}) collective-permute-start(f32[64,256]{1,0:T(8,128)S(1)} %add.89), channel_id=1, source_target_pairs={{0,2},{1,3},{2,0},{3,1},{4,6},{5,7},{6,4},{7,5},{8,10},{9,11},{10,... | collective-permute-start | bytes 196616 | tf_op jit(solution)/shard_map/ppermute | solution.py:229
  90.5 13.0 %collective-permute-start.22 = (bf16[192,1024]{1,0:T(8,128)(2,1)}, bf16[192,1024]{1,0:T(8,128)(2,1)S(1)}, u32[]{:S(2)}, u32[]{:S(2)}) collective-permute-start(bf16[192,1024]{1,0:T(8,128)(2,1)} %collective-permute-done.11.refs_0_), channel_id=1, source_target_pairs={{0,16},{8,24},{16,0},{24,8},{1,17},{9,25},{17,1},{25,9},{2,18},{10... | collective-permute-start | bytes 1179656 | tf_op jit(solution)/shard_map/ppermute | solution.py:229
  95.9 9.8 %copy-start.10 = (bf16[128,1024]{1,0:T(8,128)(2,1)S(1)}, bf16[128,1024]{1,0:T(8,128)(2,1)}, u32[]{:S(2)}) copy-start(bf16[128,1024]{1,0:T(8,128)(2,1)} %copy-done.9) | copy-start | bytes 786436
  95.9 7.5 %collective-permute-start.21 = (bf16[64,512]{1,0:T(8,128)(2,1)S(1)}, bf16[64,512]{1,0:T(8,128)(2,1)S(1)}, u32[]{:S(2)}, u32[]{:S(2)}) collective-permute-start(bf16[64,512]{1,0:T(8,128)(2,1)S(1)} %dynamic-slice_convert_fusion.2), channel_id=1, source_target_pairs={{0,4},{1,5},{2,6},{3,7},{4,0},{5,1},{6,2},{7,3},{8,12},{9,13},{10,... | collective-permute-start | bytes 196616 | tf_op jit(solution)/shard_map/ppermute | solution.py:229
  98.3 5.2 %collective-permute-start.20 = (f32[64,256]{1,0:T(8,128)S(1)}, f32[64,256]{1,0:T(8,128)S(1)}, u32[]{:S(2)}, u32[]{:S(2)}) collective-permute-start(f32[64,256]{1,0:T(8,128)S(1)} %add.95), channel_id=1, source_target_pairs={{0,4},{1,5},{2,6},{3,7},{4,0},{5,1},{6,2},{7,3},{8,12},{9,13},{10,... | collective-permute-start | bytes 196616 | tf_op jit(solution)/shard_map/ppermute | solution.py:229
  103.5 5.9 %collective-permute-start.23 = (f32[64,768]{1,0:T(8,128)S(1)}, f32[64,768]{1,0:T(8,128)S(1)}, u32[]{:S(2)}, u32[]{:S(2)}) collective-permute-start(f32[64,768]{1,0:T(8,128)S(1)} %pad_maximum_fusion.4), channel_id=1, source_target_pairs={{0,16},{8,24},{16,0},{24,8},{1,17},{9,25},{17,1},{25,9},{2,18},{10... | collective-permute-start | bytes 589832 | tf_op jit(solution)/shard_map/ppermute | solution.py:229
  109.5 3.9 %collective-permute-start.24 = (f32[256,512]{1,0:T(8,128)S(1)}, f32[256,512]{1,0:T(8,128)S(1)}, u32[]{:S(2)}, u32[]{:S(2)}) collective-permute-start(f32[256,512]{1,0:T(8,128)S(1)} %slice.69), channel_id=1, source_target_pairs={{0,8},{8,0},{16,24},{24,16},{1,9},{9,1},{17,25},{25,17},{2,10},{10... | collective-permute-start | bytes 1572872 | tf_op jit(solution)/shard_map/ppermute | solution.py:229
  109.6 2.3 %collective-permute-start.25 = (f32[64,1280]{1,0:T(8,128)S(1)}, f32[64,1280]{1,0:T(8,128)S(1)}, u32[]{:S(2)}, u32[]{:S(2)}) collective-permute-start(f32[64,1280]{1,0:T(8,128)S(1)} %pad_maximum_fusion.3.mine), channel_id=1, source_target_pairs={{0,8},{8,0},{16,24},{24,16},{1,9},{9,1},{17,25},{25,17},{2,10},{10... | collective-permute-start | bytes 983048 | tf_op jit(solution)/shard_map/ppermute | solution.py:229
  113.4 0.9 copy-start.18

commit v5 on v4

--- a/solution.py
+++ b/solution.py
@@ -368,7 +368,6 @@
         part_a, part_b = over(total_a, "fsdp", 2), over(sent, "fsdp", 2)
         part_a, part_b, done, gifts[hop] = together(part_a, part_b, done, gifts[hop])
         total_a, total_b = total_a + part_a, total_b + part_b.astype(F32)
-        done = product(2 * half - 2, rows_of(half - 1), done, "late")
         bit = 4
         while bit < n:
             total_a = total_a + over(total_a, "fsdp", bit)
@@ -381,6 +380,7 @@
             total_b = total_b + over(total_b, "dp", bit)
             bit *= 2
         total_a, total_b, gifts[half], done = together(total_a, total_b, gifts[half], done)
+        done = product(2 * half - 2, rows_of(half - 1), done, "late")
         totals = jnp.concatenate([total_b, total_a], axis=1)
         others = over(totals, "dp", 2)
         last = [

time: 116 us -> 121 us (1.043)
  waiting for transfers between devices: 26.9 us -> 29.6 us
  local copies, waits for them, and re-layouts: 7.8 us -> 9.05 us
    ppermute x17, waiting for transfers between devices: 22 us -> 24.6 us  [over(): lax.ppermute(a, axis, [(i, i ^ bit) for i in range(mesh.shape[axis])])]
    unnamed x40 -> x42, local copies, waits for them, and re-layouts: 3.27 us -> 3.89 us
  transfers between devices with their start and end apart: 26 -> 26, of which waited for: 12 -> 12; matrix products, arithmetic and copies ran while one was open for 9% -> 9% of each run, Pallas kernels for 33% -> 31%
where the time goes in v5:
time: 121 us; the launch traced here: 120 us
  Pallas kernels  37.5 us (31%)
  starting transfers between devices  35.1 us (29%)
  waiting for transfers between devices  29.6 us (24%)
  local copies, waits for them, and re-layouts  9.05 us (7%)
  other arithmetic  6.04 us (5%)
  matrix products  1.52 us (1%)
    pallas_call x7, Pallas kernels, products(): pl.pallas_call(body, grid_spec=pltpu.PrefetchScalarGridSpec(num_scalar_pr...  27 us
    ppermute x17, waiting for transfers between devices, over(): lax.ppermute(a, axis, [(i, i ^ bit) for i in range(mesh.shape[axis])])  24.6 us
    ppermute x17, starting transfers between devices, over(): lax.ppermute(a, axis, [(i, i ^ bit) for i in range(mesh.shape[axis])])  20.3 us
    pallas_call x1, Pallas kernels, terms_b(): pl.pallas_call(body, grid_spec=pltpu.PrefetchScalarGridSpec(num_scalar_pr...  8.17 us
    ppermute x4, starting transfers between devices, backward(): lax.ppermute(a, 'fsdp', [(order[(i + 1) % n], order[i]) for i in range(n)])  6.38 us
    ppermute x4, starting transfers between devices, forward(): lax.ppermute(a, 'fsdp', [(order[i], order[(i + 1) % n]) for i in range(n)])  4.83 us
    unnamed x42, local copies, waits for them, and re-layouts  3.89 us
    ppermute x1, starting transfers between devices, shards(): lax.ppermute(together(my_up, chunks[1])[0], 'fsdp', [(order[i], order[(i...  3.61 us
  transfers between devices with their start and end apart: 26, of which 12 were waited for; matrix products, arithmetic and copies ran while one was open for 9% of the time, Pallas kernels for 31%

profile of v5, /device:TPU:0, one launch (start us, length us, event | category | flops | bytes accessed | tf_op | source)
XLA Modules:
  0.0 120.0 jit_solution(1933849125683676854)
XLA Ops:
  0.7 0.5 collective-permute-start.2
  1.2 0.9 slice_select_fusion.4
  2.1 0.6 broadcast_in_dim.7
  2.7 0.6 fusion
  3.4 0.8 broadcast_select_fusion
  4.3 2.6 %collective-permute-start.1 = (bf16[384,1024]{1,0:T(8,128)(2,1)S(1)}, bf16[384,1024]{1,0:T(8,128)(2,1)S(1)}, u32[]{:S(2)}, u32[]{:S(2)}) collective-permute-start(bf16[384,1024]{1,0:T(8,128)(2,1)S(1)} %pad_maximum_fusion.refs_0_), channel_id=1, source_target_pairs={{2,0},{4,2},{6,4},{7,6},{5,7},{3,5},{1,3},{0,1},{10,8},{12,10},{14... | collective-permute-start | bytes 2359304 | tf_op jit(solution)/shard_map/ppermute | solution.py:226
  7.3 0.2 convolution_convert_fusion.1.low
  7.5 6.9 %collective-permute-done.3 = bf16[256,512]{1,0:T(8,128)(2,1)S(1)} collective-permute-done((bf16[256,512]{1,0:T(8,128)(2,1)S(1)}, bf16[256,512]{1,0:T(8,128)(2,1)S(1)}, u32[]{:S(2)}, u32[]{:S(2)}) %collective-permute-start.3) | collective-permute-done | bytes 262176 | tf_op jit(solution)/shard_map/ppermute | solution.py:229
  14.3 0.2 convolution_convert_fusion.low_partner
  14.5 8.2 %terms_b.1 = (f32[64,4096]{1,0:T(8,128)S(1)}, bf16[64,4096]{1,0:T(8,128)(2,1)}) custom-call(s32[18]{0:T(128)S(1)} %pad_add_fusion.info, bf16[256,16384]{1,0:T(8,128)(2,1)} %mine.15, bf16[256,16384]{1,0:T(8,128)(2,1)} %collective-permute-done.2.partner, bf16[64,256]{1,0:T(8,128)(2,1)S(1)} %convolution_convert_fusion.1.low, ...), custom_call_target="tpu_custom_call" | custom-call | flops 536870912 | bytes 8388608 | tf_op jit(solution)/shard_map/terms_b/pallas_call | solution.py:92
  22.7 1.0 copy-done.7
  23.7 1.4 %collective-permute-done.1.refs_2_.refs_4_ = bf16[384,1024]{1,0:T(8,128)(2,1)S(1)} collective-permute-done((bf16[384,1024]{1,0:T(8,128)(2,1)S(1)}, bf16[384,1024]{1,0:T(8,128)(2,1)S(1)}, u32[]{:S(2)}, u32[]{:S(2)}) %collective-permute-start.1) | collective-permute-done | bytes 786464 | tf_op jit(solution)/shard_map/ppermute | solution.py:226
  25.1 1.4 %collective-permute-done.refs_1_.refs_2_ = bf16[384,1024]{1,0:T(8,128)(2,1)S(1)} collective-permute-done((bf16[384,1024]{1,0:T(8,128)(2,1)S(1)}, bf16[384,1024]{1,0:T(8,128)(2,1)S(1)}, u32[]{:S(2)}, u32[]{:S(2)}) %collective-permute-start) | collective-permute-done | bytes 786464 | tf_op jit(solution)/shard_map/ppermute | solution.py:223
  26.5 0.4 collective-permute-start.4
  26.9 1.6 %collective-permute-start.6 = (bf16[384,1024]{1,0:T(8,128)(2,1)S(1)}, bf16[384,1024]{1,0:T(8,128)(2,1)}, u32[]{:S(2)}, u32[]{:S(2)}) collective-permute-start(bf16[384,1024]{1,0:T(8,128)(2,1)S(1)} %collective-permute-done.1.refs_2_.refs_4_), channel_id=1, source_target_pairs={{2,0},{4,2},{6,4},{7,6},{5,7},{3,5},{1,3},{0,1},{10,8},{12,10},{14... | collective-permute-start | bytes 2359304 | tf_op jit(solution)/shard_map/ppermute | solution.py:226
  28.5 1.5 %collective-permute-start.8 = (bf16[64,4096]{1,0:T(8,128)(2,1)}, bf16[64,4096]{1,0:T(8,128)(2,1)}, u32[]{:S(2)}, u32[]{:S(2)}) collective-permute-start(bf16[64,4096]{1,0:T(8,128)(2,1)} %get-tuple-element.39), channel_id=1, source_target_pairs={{0,16},{8,24},{16,0},{24,8},{1,17},{9,25},{17,1},{25,9},{2,18},{10... | collective-permute-start | bytes 1572872 | tf_op jit(solution)/shard_map/ppermute | solution.py:229
  30.0 0.9 constant_dynamic-slice_fusion.1
  30.9 0.9 constant_dynamic-slice_fusion
  31.8 3.6 %collective-permute-start.10 = (bf16[64,1024]{1,0:T(8,128)(2,1)}, bf16[64,1024]{1,0:T(8,128)(2,1)S(1)}, u32[]{:S(2)}, u32[]{:S(2)}) collective-permute-start(bf16[64,1024]{1,0:T(8,128)(2,1)} %copy-done.16), channel_id=1, source_target_pairs={{0,7},{2,5},{4,3},{6,1},{7,0},{5,2},{3,4},{1,6},{8,15},{10,13},{12... | collective-permute-start | bytes 393224 | tf_op jit(solution)/shard_map/ppermute | solution.py:288
  35.4 3.9 %through_first.1.refs_3_ = f32[512,64]{1,0:T(8,128)S(1)} custom-call(s32[18]{0:T(128)S(1)} %pad_add_fusion.info, bf16[256,16384]{1,0:T(8,128)(2,1)} %mine.15, bf16[256,16384]{1,0:T(8,128)(2,1)} %collective-permute-done.2.partner, bf16[384,1024]{1,0:T(8,128)(2,1)S(1)} %pad_maximum_fusion.refs_0_, bf16[384,1024]{1,0:T(8,128)(2,1)S(1)} %collective-permute-done.refs_1_.refs_2_, ...), custom_call_target="tpu_custom_call" | custom-call | flops 201326592 | bytes 3670016 | tf_op jit(solution)/shard_map/through_first/pallas_call | solution.py:151
  39.4 2.0 %collective-permute-done.8 = bf16[64,4096]{1,0:T(8,128)(2,1)} collective-permute-done((bf16[64,4096]{1,0:T(8,128)(2,1)}, bf16[64,4096]{1,0:T(8,128)(2,1)}, u32[]{:S(2)}, u32[]{:S(2)}) %collective-permute-start.8) | collective-permute-done | bytes 524320 | tf_op jit(solution)/shard_map/ppermute | solution.py:229
  41.5 1.6 %collective-permute-start.9 = (bf16[384,1024]{1,0:T(8,128)(2,1)S(1)}, bf16[384,1024]{1,0:T(8,128)(2,1)S(1)}, u32[]{:S(2)}, u32[]{:S(2)}) collective-permute-start(bf16[384,1024]{1,0:T(8,128)(2,1)S(1)} %pad_maximum_fusion.1), channel_id=1, source_target_pairs={{0,16},{8,24},{16,0},{24,8},{1,17},{9,25},{17,1},{25,9},{2,18},{10... | collective-permute-start | bytes 2359304 | tf_op jit(solution)/shard_map/ppermute | solution.py:229
  43.0 2.1 %collective-permute-done.4.refs_0_ = bf16[384,1024]{1,0:T(8,128)(2,1)S(1)} collective-permute-done((bf16[384,1024]{1,0:T(8,128)(2,1)S(1)}, bf16[384,1024]{1,0:T(8,128)(2,1)S(1)}, u32[]{:S(2)}, u32[]{:S(2)}) %collective-permute-start.4) | collective-permute-done | bytes 786464 | tf_op jit(solution)/shard_map/ppermute | solution.py:223
  45.2 4.0 %collective-permute-start.5 = (bf16[384,1024]{1,0:T(8,128)(2,1)S(1)}, bf16[384,1024]{1,0:T(8,128)(2,1)S(1)}, u32[]{:S(2)}, u32[]{:S(2)}) collective-permute-start(bf16[384,1024]{1,0:T(8,128)(2,1)S(1)} %collective-permute-done.4.refs_0_), channel_id=1, source_target_pairs={{0,2},{2,4},{4,6},{6,7},{7,5},{5,3},{3,1},{1,0},{8,10},{10,12},{12... | collective-permute-start | bytes 2359304 | tf_op jit(solution)/shard_map/ppermute | solution.py:223
  49.1 1.2 convert_add_fusion
  50.3 3.3 %collective-permute-start.15 = (bf16[64,2048]{1,0:T(8,128)(2,1)S(1)}, bf16[64,2048]{1,0:T(8,128)(2,1)S(1)}, u32[]{:S(2)}, u32[]{:S(2)}) collective-permute-start(bf16[64,2048]{1,0:T(8,128)(2,1)S(1)} %dynamic-slice_convert_fusion), channel_id=1, source_target_pairs={{0,1},{1,0},{2,3},{3,2},{4,5},{5,4},{6,7},{7,6},{8,9},{9,8},{10,11... | collective-permute-start | bytes 786440 | tf_op jit(solution)/shard_map/ppermute | solution.py:229
  53.6 1.0 slice.82
  54.8 1.6 %collective-permute-start.16 = (bf16[384,1024]{1,0:T(8,128)(2,1)S(1)}, bf16[384,1024]{1,0:T(8,128)(2,1)S(1)}, u32[]{:S(2)}, u32[]{:S(2)}) collective-permute-start(bf16[384,1024]{1,0:T(8,128)(2,1)S(1)} %pad_maximum_fusion.2), channel_id=1, source_target_pairs={{0,16},{8,24},{16,0},{24,8},{1,17},{9,25},{17,1},{25,9},{2,18},{10... | collective-permute-start | bytes 2359304 | tf_op jit(solution)/shard_map/ppermute | solution.py:229
  56.3 4.0 %through_second.1.refs_2_ = f32[512,64]{1,0:T(8,128)S(1)} custom-call(s32[18]{0:T(128)S(1)} %pad_add_fusion.info, bf16[256,16384]{1,0:T(8,128)(2,1)} %mine.15, bf16[256,16384]{1,0:T(8,128)(2,1)} %collective-permute-done.2.partner, bf16[384,1024]{1,0:T(8,128)(2,1)S(1)} %collective-permute-done.4.refs_0_, ...), custom_call_target="tpu_custom_call" | custom-call | flops 201326592 | bytes 3670016 | tf_op jit(solution)/shard_map/through_second/pallas_call | solution.py:151
  60.3 1.7 %collective-permute-done.9.refs_3_.refs_5_ = bf16[384,1024]{1,0:T(8,128)(2,1)S(1)} collective-permute-done((bf16[384,1024]{1,0:T(8,128)(2,1)S(1)}, bf16[384,1024]{1,0:T(8,128)(2,1)S(1)}, u32[]{:S(2)}, u32[]{:S(2)}) %collective-permute-start.9) | collective-permute-done | bytes 786464 | tf_op jit(solution)/shard_map/ppermute | solution.py:229
  62.0 5.7 %first.1.refs_4_ = f32[512,512]{1,0:T(8,128)} custom-call(s32[18]{0:T(128)S(1)} %pad_add_fusion.info, bf16[256,16384]{1,0:T(8,128)(2,1)} %mine.15, bf16[256,16384]{1,0:T(8,128)(2,1)} %collective-permute-done.2.partner, bf16[384,1024]{1,0:T(8,128)(2,1)S(1)} %pad_maximum_fusion.refs_0_, bf16[192,1024]{1,0:T(8,128)(2,1)S(1)} %copy-done.6, ...), custom_call_target="tpu_custom_call" | custom-call | flops 1610612736 | bytes 7340032 | tf_op jit(solution)/shard_map/first/pallas_call | solution.py:151
  67.7 0.9 assemble.1
  68.6 1.6 %collective-permute-start.19 = (bf16[384,1024]{1,0:T(8,128)(2,1)}, bf16[384,1024]{1,0:T(8,128)(2,1)S(1)}, u32[]{:S(2)}, u32[]{:S(2)}) collective-permute-start(bf16[384,1024]{1,0:T(8,128)(2,1)} %get-tuple-element.51), channel_id=1, source_target_pairs={{0,16},{8,24},{16,0},{24,8},{1,17},{9,25},{17,1},{25,9},{2,18},{10... | collective-permute-start | bytes 2359304 | tf_op jit(solution)/shard_map/ppermute | solution.py:229
  70.2 2.7 %through_last.1 = f32[512,64]{1,0:T(8,128)S(1)} custom-call(s32[18]{0:T(128)S(1)} %pad_add_fusion.info, bf16[256,16384]{1,0:T(8,128)(2,1)} %mine.15, bf16[256,16384]{1,0:T(8,128)(2,1)} %collective-permute-done.2.partner, bf16[384,1024]{1,0:T(8,128)(2,1)S(1)} %collective-permute-done.5.refs_0_.refs_2_, ...), custom_call_target="tpu_custom_call" | custom-call | flops 134217728 | bytes 2490368 | tf_op jit(solution)/shard_map/through_last/pallas_call | solution.py:151
  73.0 2.1 %collective-permute-start.12 = (bf16[128,1024]{1,0:T(8,128)(2,1)S(1)}, bf16[128,1024]{1,0:T(8,128)(2,1)S(1)}, u32[]{:S(2)}, u32[]{:S(2)}) collective-permute-start(bf16[128,1024]{1,0:T(8,128)(2,1)S(1)} %get-tuple-element.49), channel_id=1, source_target_pairs={{2,0},{4,2},{6,4},{7,6},{5,7},{3,5},{1,3},{0,1},{10,8},{12,10},{14... | collective-permute-start | bytes 786440 | tf_op jit(solution)/shard_map/ppermute | solution.py:226
  75.1 0.4 collective-permute-start.11
  75.6 0.7 dynamic-slice_convert_fusion.1
  76.4 0.2 fusion.3
  76.6 1.7 %collective-permute-start.14 = (f32[64,256]{1,0:T(8,128)S(1)}, f32[64,256]{1,0:T(8,128)S(1)}, u32[]{:S(2)}, u32[]{:S(2)}) collective-permute-start(f32[64,256]{1,0:T(8,128)S(1)} %fusion.3), channel_id=1, source_target_pairs={{0,1},{1,0},{2,3},{3,2},{4,5},{5,4},{6,7},{7,6},{8,9},{9,8},{10,11... | collective-permute-start | bytes 196616 | tf_op jit(solution)/shard_map/ppermute | solution.py:229
  78.3 0.6 collective-permute-done.16.refs_1_.refs_3_
  78.9 4.2 %middle.1.refs_4_ = f32[512,512]{1,0:T(8,128)S(1)} custom-call(s32[18]{0:T(128)S(1)} %pad_add_fusion.info, bf16[256,16384]{1,0:T(8,128)(2,1)} %mine.15, bf16[256,16384]{1,0:T(8,128)(2,1)} %collective-permute-done.2.partner, bf16[384,1024]{1,0:T(8,128)(2,1)S(1)} %collective-permute-done.4.refs_0_, ...), custom_call_target="tpu_custom_call" | custom-call | flops 1073741824 | bytes 5242880 | tf_op jit(solution)/shard_map/middle/pallas_call | solution.py:151
  83.1 1.0 copy-done.5
  84.0 3.7 %collective-permute-done.14 = f32[64,256]{1,0:T(8,128)S(1)} collective-permute-done((f32[64,256]{1,0:T(8,128)S(1)}, f32[64,256]{1,0:T(8,128)S(1)}, u32[]{:S(2)}, u32[]{:S(2)}) %collective-permute-start.14) | collective-permute-done | bytes 65568 | tf_op jit(solution)/shard_map/ppermute | solution.py:229
  87.8 0.7 copy-done.9
  88.5 2.0 %collective-permute-start.17 = (f32[64,256]{1,0:T(8,128)S(1)}, f32[64,256]{1,0:T(8,128)S(1)}, u32[]{:S(2)}, u32[]{:S(2)}) collective-permute-start(f32[64,256]{1,0:T(8,128)S(1)} %add.89), channel_id=1, source_target_pairs={{0,2},{1,3},{2,0},{3,1},{4,6},{5,7},{6,4},{7,5},{8,10},{9,11},{10,... | collective-permute-start | bytes 196616 | tf_op jit(solution)/shard_map/ppermute | solution.py:229
  90.5 0.7 collective-permute-start.22
  91.1 3.8 %collective-permute-done.17 = f32[64,256]{1,0:T(8,128)S(1)} collective-permute-done((f32[64,256]{1,0:T(8,128)S(1)}, f32[64,256]{1,0:T(8,128)S(1)}, u32[]{:S(2)}, u32[]{:S(2)}) %collective-permute-start.17) | collective-permute-done | bytes 65568 | tf_op jit(solution)/shard_map/ppermute | solution.py:229
  94.9 0.6 copy-done.19
  95.6 1.7 %collective-permute-start.20 = (f32[64,256]{1,0:T(8,128)S(1)}, f32[64,256]{1,0:T(8,128)S(1)}, u32[]{:S(2)}, u32[]{:S(2)}) collective-permute-start(f32[64,256]{1,0:T(8,128)S(1)} %add.95), channel_id=1, source_target_pairs={{0,4},{1,5},{2,6},{3,7},{4,0},{5,1},{6,2},{7,3},{8,12},{9,13},{10,... | collective-permute-start | bytes 196616 | tf_op jit(solution)/shard_map/ppermute | solution.py:229
  97.2 1.0 convert_add_fusion.2
  98.3 0.6 dynamic-slice_convert_fusion.2
  98.9 1.2 %collective-permute-start.21 = (bf16[64,512]{1,0:T(8,128)(2,1)}, bf16[64,512]{1,0:T(8,128)(2,1)}, u32[]{:S(2)}, u32[]{:S(2)}) collective-permute-start(bf16[64,512]{1,0:T(8,128)(2,1)} %dynamic-slice_convert_fusion.2), channel_id=1, source_target_pairs={{0,4},{1,5},{2,6},{3,7},{4,0},{5,1},{6,2},{7,3},{8,12},{9,13},{10,... | collective-permute-start | bytes 196616 | tf_op jit(solution)/shard_map/ppermute | solution.py:229
  100.2 2.6 %collective-permute-done.20 = f32[64,256]{1,0:T(8,128)S(1)} collective-permute-done((f32[64,256]{1,0:T(8,128)S(1)}, f32[64,256]{1,0:T(8,128)S(1)}, u32[]{:S(2)}, u32[]{:S(2)}) %collective-permute-start.20) | collective-permute-done | bytes 65568 | tf_op jit(solution)/shard_map/ppermute | solution.py:229
  102.8 1.6 %collective-permute-done.21 = bf16[64,512]{1,0:T(8,128)(2,1)} collective-permute-done((bf16[64,512]{1,0:T(8,128)(2,1)}, bf16[64,512]{1,0:T(8,128)(2,1)}, u32[]{:S(2)}, u32[]{:S(2)}) %collective-permute-start.21) | collective-permute-done | bytes 65568 | tf_op jit(solution)/shard_map/ppermute | solution.py:229
  104.4 0.9 convert_add_fusion.3
  105.3 2.3 %collective-permute-start.23 = (f32[64,768]{1,0:T(8,128)S(1)}, f32[64,768]{1,0:T(8,128)S(1)}, u32[]{:S(2)}, u32[]{:S(2)}) collective-permute-start(f32[64,768]{1,0:T(8,128)S(1)} %pad_maximum_fusion.4), channel_id=1, source_target_pairs={{0,16},{8,24},{16,0},{24,8},{1,17},{9,25},{17,1},{25,9},{2,18},{10... | collective-permute-start | bytes 589832 | tf_op jit(solution)/shard_map/ppermute | solution.py:229
  107.6 3.9 %late.1.refs_3_ = f32[512,512]{1,0:T(8,128)S(1)} custom-call(s32[18]{0:T(128)S(1)} %pad_add_fusion.info, bf16[256,16384]{1,0:T(8,128)(2,1)} %mine.15, bf16[256,16384]{1,0:T(8,128)(2,1)} %collective-permute-done.2.partner, bf16[384,1024]{1,0:T(8,128)(2,1)S(1)} %collective-permute-done.5.refs_0_.refs_2_, ...), custom_call_target="tpu_custom_call" | custom-call | flops 1073741824 | bytes 5242880 | tf_op jit(solution)/shard_map/late/pallas_call | solution.py:151
  111.5 2.6 %last.1 = f32[512,512]{1,0:T(8,128)S(1)} custom-call(s32[18]{0:T(128)S(1)} %pad_add_fusion.info, bf16[256,16384]{1,0:T(8,128)(2,1)} %mine.15, bf16[256,16384]{1,0:T(8,128)(2,1)} %collective-permute-done.2.partner, bf16[192,1024]{1,0:T(8,128)(2,1)} %collective-permute-done.11.refs_0_, bf16[128,1024]{1,0:T(8,128)(2,1)S(1)} %copy-done.10, ...), custom_call_target="tpu_custom_call" | custom-call | flops 536870912 | bytes 3145728 | tf_op jit(solution)/shard_map/last/pallas_call | solution.py:151
  114.4 0.6 collective-permute-start.25
  115.0 1.8 %collective-permute-done.25.other = f32[64,1280]{1,0:T(8,128)S(1)} collective-permute-done((f32[64,1280]{1,0:T(8,128)S(1)}, f32[64,1280]{1,0:T(8,128)S(1)}, u32[]{:S(2)}, u32[]{:S(2)}) %collective-permute-start.25) | collective-permute-done | bytes 327712 | tf_op jit(solution)/shard_map/ppermute | solution.py:229
  116.7 1.4 %finish.1 = (f32[64,2048]{1,0:T(8,128)}, f32[64,512]{1,0:T(8,128)}) custom-call(s32[18]{0:T(128)S(1)} %pad_add_fusion.info, f32[1]{0:T(128)} %constant.66.clone.1.factor, f32[64,1280]{1,0:T(8,128)S(1)} %pad_maximum_fusion.3.mine, f32[64,1280]{1,0:T(8,128)S(1)} %collective-permute-done.25.other), custom_call_target="tpu_custom_call" | custom-call | bytes 1310720 | tf_op jit(solution)/shard_map/finish/pallas_call | solution.py:194
  118.3 0.1 slice_select_fusion.1
  118.5 0.6 copy-done.18
  119.1 0.9 fusion.1
  (82 shorter events, 1.3 us)
Async XLA Ops:
  0.6 2.7 %copy-start = (bf16[64,2048]{1,0:T(8,128)(2,1)S(1)}, bf16[64,2048]{1,0:T(8,128)(2,1)}, u32[]{:S(2)}) copy-start(bf16[64,2048]{1,0:T(8,128)(2,1)} %param.12) | copy-start | bytes 786436
  0.6 2.1 %copy-start.15 = (bf16[512,2048]{1,0:T(8,128)(2,1)S(1)}, bf16[512,2048]{1,0:T(8,128)(2,1)}, u32[]{:S(2)}) copy-start(bf16[512,2048]{1,0:T(8,128)(2,1)} %param.9) | copy-start | bytes 6291460
  0.7 13.9 %collective-permute-start.2 = (bf16[256,16384]{1,0:T(8,128)(2,1)}, bf16[256,16384]{1,0:T(8,128)(2,1)}, u32[]{:S(2)}, u32[]{:S(2)}) collective-permute-start(bf16[256,16384]{1,0:T(8,128)(2,1)} %mine.15), channel_id=1, source_target_pairs={{0,8},{8,0},{16,24},{24,16},{1,9},{9,1},{17,25},{25,17},{2,10},{10... | collective-permute-start | bytes 25165832 | tf_op jit(solution)/shard_map/ppermute | solution.py:229
  3.4 0.9 copy-start.16
  3.4 3.7 %copy-start.12 = (bf16[256,512]{1,0:T(8,128)(2,1)S(1)}, bf16[256,512]{1,0:T(8,128)(2,1)}, u32[]{:S(2)}) copy-start(bf16[256,512]{1,0:T(8,128)(2,1)} %param.7) | copy-start | bytes 786436
  3.4 3.8 %copy-start.20 = (s32[8]{0:T(128)S(1)}, s32[8]{0:T(128)}, u32[]{:S(2)}) copy-start(s32[8]{0:T(128)} %constant.67.clone) | copy-start | bytes 100
  3.4 3.8 %copy-start.14 = (bf16[512,64]{0,1:T(8,128)(2,1)S(1)}, bf16[512,64]{0,1:T(8,128)(2,1)}, u32[]{:S(2)}) copy-start(bf16[512,64]{0,1:T(8,128)(2,1)} %param.11) | copy-start | bytes 196612
  4.3 20.8 %collective-permute-start.1 = (bf16[384,1024]{1,0:T(8,128)(2,1)S(1)}, bf16[384,1024]{1,0:T(8,128)(2,1)S(1)}, u32[]{:S(2)}, u32[]{:S(2)}) collective-permute-start(bf16[384,1024]{1,0:T(8,128)(2,1)S(1)} %pad_maximum_fusion.refs_0_), channel_id=1, source_target_pairs={{2,0},{4,2},{6,4},{7,6},{5,7},{3,5},{1,3},{0,1},{10,8},{12,10},{14... | collective-permute-start | bytes 2359304 | tf_op jit(solution)/shard_map/ppermute | solution.py:226
  6.9 19.5 %collective-permute-start = (bf16[384,1024]{1,0:T(8,128)(2,1)S(1)}, bf16[384,1024]{1,0:T(8,128)(2,1)S(1)}, u32[]{:S(2)}, u32[]{:S(2)}) collective-permute-start(bf16[384,1024]{1,0:T(8,128)(2,1)S(1)} %pad_maximum_fusion.refs_0_), channel_id=1, source_target_pairs={{0,2},{2,4},{4,6},{6,7},{7,5},{5,3},{3,1},{1,0},{8,10},{10,12},{12... | collective-permute-start | bytes 2359304 | tf_op jit(solution)/shard_map/ppermute | solution.py:223
  7.1 7.3 %collective-permute-start.3 = (bf16[256,512]{1,0:T(8,128)(2,1)S(1)}, bf16[256,512]{1,0:T(8,128)(2,1)S(1)}, u32[]{:S(2)}, u32[]{:S(2)}) collective-permute-start(bf16[256,512]{1,0:T(8,128)(2,1)S(1)} %copy-done.12), channel_id=1, source_target_pairs={{0,8},{8,0},{16,24},{24,16},{1,9},{9,1},{17,25},{25,17},{2,10},{10... | collective-permute-start | bytes 786440 | tf_op jit(solution)/shard_map/ppermute | solution.py:229
  14.3 8.4 %copy-start.13 = (bf16[256,512]{1,0:T(8,128)(2,1)}, bf16[256,512]{1,0:T(8,128)(2,1)S(1)}, u32[]{:S(2)}) copy-start(bf16[256,512]{1,0:T(8,128)(2,1)S(1)} %collective-permute-done.3) | copy-start | bytes 786436
  22.7 1.0 copy-start.7
  25.1 16.3 %copy-start.1 = (bf16[384,1024]{1,0:T(8,128)(2,1)}, bf16[384,1024]{1,0:T(8,128)(2,1)S(1)}, u32[]{:S(2)}) copy-start(bf16[384,1024]{1,0:T(8,128)(2,1)S(1)} %collective-permute-done.1.refs_2_.refs_4_) | copy-start | bytes 2359300
  26.5 14.9 %copy-start.3 = (bf16[384,1024]{1,0:T(8,128)(2,1)}, bf16[384,1024]{1,0:T(8,128)(2,1)S(1)}, u32[]{:S(2)}) copy-start(bf16[384,1024]{1,0:T(8,128)(2,1)S(1)} %collective-permute-done.refs_1_.refs_2_) | copy-start | bytes 2359300
  26.5 18.7 %collective-permute-start.4 = (bf16[384,1024]{1,0:T(8,128)(2,1)S(1)}, bf16[384,1024]{1,0:T(8,128)(2,1)S(1)}, u32[]{:S(2)}, u32[]{:S(2)}) collective-permute-start(bf16[384,1024]{1,0:T(8,128)(2,1)S(1)} %collective-permute-done.refs_1_.refs_2_), channel_id=1, source_target_pairs={{0,2},{2,4},{4,6},{6,7},{7,5},{5,3},{3,1},{1,0},{8,10},{10,12},{12... | collective-permute-start | bytes 2359304 | tf_op jit(solution)/shard_map/ppermute | solution.py:223
  26.9 22.2 %collective-permute-start.6 = (bf16[384,1024]{1,0:T(8,128)(2,1)S(1)}, bf16[384,1024]{1,0:T(8,128)(2,1)}, u32[]{:S(2)}, u32[]{:S(2)}) collective-permute-start(bf16[384,1024]{1,0:T(8,128)(2,1)S(1)} %collective-permute-done.1.refs_2_.refs_4_), channel_id=1, source_target_pairs={{2,0},{4,2},{6,4},{7,6},{5,7},{3,5},{1,3},{0,1},{10,8},{12,10},{14... | collective-permute-start | bytes 2359304 | tf_op jit(solution)/shard_map/ppermute | solution.py:226
  28.5 12.8 %collective-permute-start.8 = (bf16[64,4096]{1,0:T(8,128)(2,1)}, bf16[64,4096]{1,0:T(8,128)(2,1)}, u32[]{:S(2)}, u32[]{:S(2)}) collective-permute-start(bf16[64,4096]{1,0:T(8,128)(2,1)} %get-tuple-element.39), channel_id=1, source_target_pairs={{0,16},{8,24},{16,0},{24,8},{1,17},{9,25},{17,1},{25,9},{2,18},{10... | collective-permute-start | bytes 1572872 | tf_op jit(solution)/shard_map/ppermute | solution.py:229
  31.8 22.9 %collective-permute-start.10 = (bf16[64,1024]{1,0:T(8,128)(2,1)}, bf16[64,1024]{1,0:T(8,128)(2,1)S(1)}, u32[]{:S(2)}, u32[]{:S(2)}) collective-permute-start(bf16[64,1024]{1,0:T(8,128)(2,1)} %copy-done.16), channel_id=1, source_target_pairs={{0,7},{2,5},{4,3},{6,1},{7,0},{5,2},{3,4},{1,6},{8,15},{10,13},{12... | collective-permute-start | bytes 393224 | tf_op jit(solution)/shard_map/ppermute | solution.py:288
  39.4 9.8 %copy-start.8 = (f32[64,4096]{1,0:T(8,128)S(1)}, f32[64,4096]{1,0:T(8,128)}, u32[]{:S(2)}) copy-start(f32[64,4096]{1,0:T(8,128)} %copy-done.7) | copy-start | bytes 3145732
  41.5 20.5 %collective-permute-start.9 = (bf16[384,1024]{1,0:T(8,128)(2,1)S(1)}, bf16[384,1024]{1,0:T(8,128)(2,1)S(1)}, u32[]{:S(2)}, u32[]{:S(2)}) collective-permute-start(bf16[384,1024]{1,0:T(8,128)(2,1)S(1)} %pad_maximum_fusion.1), channel_id=1, source_target_pairs={{0,16},{8,24},{16,0},{24,8},{1,17},{9,25},{17,1},{25,9},{2,18},{10... | collective-permute-start | bytes 2359304 | tf_op jit(solution)/shard_map/ppermute | solution.py:229
  45.2 22.5 %collective-permute-start.5 = (bf16[384,1024]{1,0:T(8,128)(2,1)S(1)}, bf16[384,1024]{1,0:T(8,128)(2,1)S(1)}, u32[]{:S(2)}, u32[]{:S(2)}) collective-permute-start(bf16[384,1024]{1,0:T(8,128)(2,1)S(1)} %collective-permute-done.4.refs_0_), channel_id=1, source_target_pairs={{0,2},{2,4},{4,6},{6,7},{7,5},{5,3},{3,1},{1,0},{8,10},{10,12},{12... | collective-permute-start | bytes 2359304 | tf_op jit(solution)/shard_map/ppermute | solution.py:223
  49.1 18.6 %collective-permute-start.7 = (bf16[384,1024]{1,0:T(8,128)(2,1)}, bf16[384,1024]{1,0:T(8,128)(2,1)S(1)}, u32[]{:S(2)}, u32[]{:S(2)}) collective-permute-start(bf16[384,1024]{1,0:T(8,128)(2,1)} %collective-permute-done.6.refs_1_.refs_2_), channel_id=1, source_target_pairs={{2,0},{4,2},{6,4},{7,6},{5,7},{3,5},{1,3},{0,1},{10,8},{12,10},{14... | collective-permute-start | bytes 2359304 | tf_op jit(solution)/shard_map/ppermute | solution.py:226
  50.3 22.7 %collective-permute-start.15 = (bf16[64,2048]{1,0:T(8,128)(2,1)S(1)}, bf16[64,2048]{1,0:T(8,128)(2,1)S(1)}, u32[]{:S(2)}, u32[]{:S(2)}) collective-permute-start(bf16[64,2048]{1,0:T(8,128)(2,1)S(1)} %dynamic-slice_convert_fusion), channel_id=1, source_target_pairs={{0,1},{1,0},{2,3},{3,2},{4,5},{5,4},{6,7},{7,6},{8,9},{9,8},{10,11... | collective-permute-start | bytes 786440 | tf_op jit(solution)/shard_map/ppermute | solution.py:229
  54.7 7.3 %copy-start.2 = (bf16[384,1024]{1,0:T(8,128)(2,1)S(1)}, bf16[384,1024]{1,0:T(8,128)(2,1)}, u32[]{:S(2)}) copy-start(bf16[384,1024]{1,0:T(8,128)(2,1)} %copy-done.1) | copy-start | bytes 2359300
  54.7 7.3 %copy-start.4 = (bf16[384,1024]{1,0:T(8,128)(2,1)S(1)}, bf16[384,1024]{1,0:T(8,128)(2,1)}, u32[]{:S(2)}) copy-start(bf16[384,1024]{1,0:T(8,128)(2,1)} %copy-done.3) | copy-start | bytes 2359300
  54.7 7.3 %copy-start.6 = (bf16[192,1024]{1,0:T(8,128)(2,1)S(1)}, bf16[192,1024]{1,0:T(8,128)(2,1)}, u32[]{:S(2)}) copy-start(bf16[192,1024]{1,0:T(8,128)(2,1)} %get-tuple-element.77.refs_1_) | copy-start | bytes 1179652
  54.8 24.1 %collective-permute-start.16 = (bf16[384,1024]{1,0:T(8,128)(2,1)S(1)}, bf16[384,1024]{1,0:T(8,128)(2,1)S(1)}, u32[]{:S(2)}, u32[]{:S(2)}) collective-permute-start(bf16[384,1024]{1,0:T(8,128)(2,1)S(1)} %pad_maximum_fusion.2), channel_id=1, source_target_pairs={{0,16},{8,24},{16,0},{24,8},{1,17},{9,25},{17,1},{25,9},{2,18},{10... | collective-permute-start | bytes 2359304 | tf_op jit(solution)/shard_map/ppermute | solution.py:229
  68.6 26.3 %collective-permute-start.19 = (bf16[384,1024]{1,0:T(8,128)(2,1)}, bf16[384,1024]{1,0:T(8,128)(2,1)S(1)}, u32[]{:S(2)}, u32[]{:S(2)}) collective-permute-start(bf16[384,1024]{1,0:T(8,128)(2,1)} %get-tuple-element.51), channel_id=1, source_target_pairs={{0,16},{8,24},{16,0},{24,8},{1,17},{9,25},{17,1},{25,9},{2,18},{10... | collective-permute-start | bytes 2359304 | tf_op jit(solution)/shard_map/ppermute | solution.py:229
  72.9 3.4 %collective-permute-start.13 = (f32[512,64]{1,0:T(8,128)S(1)}, f32[512,64]{1,0:T(8,128)S(1)}, u32[]{:S(2)}, u32[]{:S(2)}) collective-permute-start(f32[512,64]{1,0:T(8,128)S(1)} %through_last.1), channel_id=1, source_target_pairs={{0,8},{8,0},{16,24},{24,16},{1,9},{9,1},{17,25},{25,17},{2,10},{10... | collective-permute-start | bytes 393224 | tf_op jit(solution)/shard_map/ppermute | solution.py:229
  73.0 14.7 %collective-permute-start.12 = (bf16[128,1024]{1,0:T(8,128)(2,1)S(1)}, bf16[128,1024]{1,0:T(8,128)(2,1)S(1)}, u32[]{:S(2)}, u32[]{:S(2)}) collective-permute-start(bf16[128,1024]{1,0:T(8,128)(2,1)S(1)} %get-tuple-element.49), channel_id=1, source_target_pairs={{2,0},{4,2},{6,4},{7,6},{5,7},{3,5},{1,3},{0,1},{10,8},{12,10},{14... | collective-permute-start | bytes 786440 | tf_op jit(solution)/shard_map/ppermute | solution.py:226
  75.1 13.3 %collective-permute-start.11 = (bf16[192,1024]{1,0:T(8,128)(2,1)S(1)}, bf16[192,1024]{1,0:T(8,128)(2,1)}, u32[]{:S(2)}, u32[]{:S(2)}) collective-permute-start(bf16[192,1024]{1,0:T(8,128)(2,1)S(1)} %get-tuple-element.48), channel_id=1, source_target_pairs={{0,2},{2,4},{4,6},{6,7},{7,5},{5,3},{3,1},{1,0},{8,10},{10,12},{12... | collective-permute-start | bytes 1179656 | tf_op jit(solution)/shard_map/ppermute | solution.py:223
  75.5 2.8 %copy-start.11 = (f32[64,2048]{1,0:T(8,128)}, f32[64,2048]{1,0:T(8,128)S(1)}, u32[]{:S(2)}) copy-start(f32[64,2048]{1,0:T(8,128)S(1)} %convert_add_fusion.1) | copy-start | bytes 1572868
  76.4 2.0 %copy-start.17 = (bf16[512,64]{1,0:T(8,128)(2,1)}, bf16[512,64]{1,0:T(8,128)(2,1)S(1)}, u32[]{:S(2)}) copy-start(bf16[512,64]{1,0:T(8,128)(2,1)S(1)} %fusion.2) | copy-start | bytes 196612
  76.6 11.1 %collective-permute-start.14 = (f32[64,256]{1,0:T(8,128)S(1)}, f32[64,256]{1,0:T(8,128)S(1)}, u32[]{:S(2)}, u32[]{:S(2)}) collective-permute-start(f32[64,256]{1,0:T(8,128)S(1)} %fusion.3), channel_id=1, source_target_pairs={{0,1},{1,0},{2,3},{3,2},{4,5},{5,4},{6,7},{7,6},{8,9},{9,8},{10,11... | collective-permute-start | bytes 196616 | tf_op jit(solution)/shard_map/ppermute | solution.py:229
  83.1 1.0 copy-start.5
  87.7 0.7 copy-start.9
  88.5 6.5 %collective-permute-start.18 = (bf16[64,1024]{1,0:T(8,128)(2,1)}, bf16[64,1024]{1,0:T(8,128)(2,1)S(1)}, u32[]{:S(2)}, u32[]{:S(2)}) collective-permute-start(bf16[64,1024]{1,0:T(8,128)(2,1)} %dynamic-slice_convert_fusion.1), channel_id=1, source_target_pairs={{0,2},{1,3},{2,0},{3,1},{4,6},{5,7},{6,4},{7,5},{8,10},{9,11},{10,... | collective-permute-start | bytes 393224 | tf_op jit(solution)/shard_map/ppermute | solution.py:229
  88.5 6.4 %collective-permute-start.17 = (f32[64,256]{1,0:T(8,128)S(1)}, f32[64,256]{1,0:T(8,128)S(1)}, u32[]{:S(2)}, u32[]{:S(2)}) collective-permute-start(f32[64,256]{1,0:T(8,128)S(1)} %add.89), channel_id=1, source_target_pairs={{0,2},{1,3},{2,0},{3,1},{4,6},{5,7},{6,4},{7,5},{8,10},{9,11},{10,... | collective-permute-start | bytes 196616 | tf_op jit(solution)/shard_map/ppermute | solution.py:229
  90.5 14.8 %collective-permute-start.22 = (bf16[192,1024]{1,0:T(8,128)(2,1)}, bf16[192,1024]{1,0:T(8,128)(2,1)S(1)}, u32[]{:S(2)}, u32[]{:S(2)}) collective-permute-start(bf16[192,1024]{1,0:T(8,128)(2,1)} %collective-permute-done.11.refs_0_), channel_id=1, source_target_pairs={{0,16},{8,24},{16,0},{24,8},{1,17},{9,25},{17,1},{25,9},{2,18},{10... | collective-permute-start | bytes 1179656 | tf_op jit(solution)/shard_map/ppermute | solution.py:229
  94.9 0.7 copy-start.19
  95.6 7.2 %collective-permute-start.20 = (f32[64,256]{1,0:T(8,128)S(1)}, f32[64,256]{1,0:T(8,128)S(1)}, u32[]{:S(2)}, u32[]{:S(2)}) collective-permute-start(f32[64,256]{1,0:T(8,128)S(1)} %add.95), channel_id=1, source_target_pairs={{0,4},{1,5},{2,6},{3,7},{4,0},{5,1},{6,2},{7,3},{8,12},{9,13},{10,... | collective-permute-start | bytes 196616 | tf_op jit(solution)/shard_map/ppermute | solution.py:229
  98.9 5.5 %collective-permute-start.21 = (bf16[64,512]{1,0:T(8,128)(2,1)}, bf16[64,512]{1,0:T(8,128)(2,1)}, u32[]{:S(2)}, u32[]{:S(2)}) collective-permute-start(bf16[64,512]{1,0:T(8,128)(2,1)} %dynamic-slice_convert_fusion.2), channel_id=1, source_target_pairs={{0,4},{1,5},{2,6},{3,7},{4,0},{5,1},{6,2},{7,3},{8,12},{9,13},{10,... | collective-permute-start | bytes 196616 | tf_op jit(solution)/shard_map/ppermute | solution.py:229
  105.3 6.2 %copy-start.10 = (bf16[128,1024]{1,0:T(8,128)(2,1)S(1)}, bf16[128,1024]{1,0:T(8,128)(2,1)}, u32[]{:S(2)}) copy-start(bf16[128,1024]{1,0:T(8,128)(2,1)} %copy-done.9) | copy-start | bytes 786436
  105.3 8.9 %collective-permute-start.23 = (f32[64,768]{1,0:T(8,128)S(1)}, f32[64,768]{1,0:T(8,128)S(1)}, u32[]{:S(2)}, u32[]{:S(2)}) collective-permute-start(f32[64,768]{1,0:T(8,128)S(1)} %pad_maximum_fusion.4), channel_id=1, source_target_pairs={{0,16},{8,24},{16,0},{24,8},{1,17},{9,25},{17,1},{25,9},{2,18},{10... | collective-permute-start | bytes 589832 | tf_op jit(solution)/shard_map/ppermute | solution.py:229
  114.3 3.9 %collective-permute-start.24 = (f32[256,512]{1,0:T(8,128)S(1)}, f32[256,512]{1,0:T(8,128)S(1)}, u32[]{:S(2)}, u32[]{:S(2)}) collective-permute-start(f32[256,512]{1,0:T(8,128)S(1)} %slice.69), channel_id=1, source_target_pairs={{0,8},{8,0},{16,24},{24,16},{1,9},{9,1},{17,25},{25,17},{2,10},{10... | collective-permute-start | bytes 1572872 | tf_op jit(solution)/shard_map/ppermute | solution.py:229
  114.4 2.3 %collective-permute-start.25 = (f32[64,1280]{1,0:T(8,128)S(1)}, f32[64,1280]{1,0:T(8,128)S(1)}, u32[]{:S(2)}, u32[]{:S(2)}) collective-permute-start(f32[64,1280]{1,0:T(8,128)S(1)} %pad_maximum_fusion.3.mine), channel_id=1, source_target_pairs={{0,8},{8,0},{16,24},{24,16},{1,9},{9,1},{17,25},{25,17},{2,10},{10... | collective-permute-start | bytes 983048 | tf_op jit(solution)/shard_map/ppermute | solution.py:229
  118.2 0.9 copy-start.18
